TPU v7x, 512 devices: a whole 4x8x8 slice. The times are simulated.
512 devices in a mesh: dp: 16 (over y, core), expert: 32 (over z, x).
Axes of the slice: x: 4, y: 8, z: 8, core: 2. Of those that a mesh axis runs over, the one named last changes fastest.
Arguments:
- stream_q: bfloat16 [4096, 4096], P('dp', 'expert'), may hold values from -6 to 6
- stream_k: bfloat16 [4096, 4096], P('dp', 'expert'), may hold values from -6 to 6
- stream_v: bfloat16 [4096, 4096], P('dp', 'expert'), may hold values from -6 to 6
- conv_taps: float32 [3, 3, 4096], P(None, None, 'expert'), may hold values from -14 to 14
- norm_gain: bfloat16 [4096], P('expert'), may hold values from 0.3984375 to 1.59375
- slot_token: int32 [16, 384], P('dp'), may hold values from 0 to 256, as said below
- expert_count: int32 [16, 2], P('dp'), may hold values from 0 to 256, as said below
- route_prob: float32 [4096], P('dp'), may hold values from 0.25 to 1
- w_proj: bfloat16 [4096, 2, 8192], P('dp', None, 'expert'), may hold values from -0.09375 to 0.09375
- grad_out: bfloat16 [4096, 8192], P('dp', 'expert'), may hold values from -0.75 to 0.75
Outputs:
- activation: bfloat16 [4096, 8192], P('dp', 'expert')
- weight_grad: float32 [4096, 2, 8192], P('dp', None, 'expert')
Inputs may be any that keep to these rules, and one draw needn't show every extreme that they name: `slot_token`: for each index of dp the slots hold its 256 local token numbers, each exactly once, grouped by expert in expert order; each group starts at a multiple of 128 and is padded with the value 256 up to a multiple of 128; all slots after the last group hold 256. `expert_count`: the size of each expert's group in slot_token, before padding; each row sums to 256.
All inputs are finite; a program needn't handle non-finite values.
Results may differ from a plain program's by a relative error of at most 0.023.
Values may be sent and summed in bfloat16 or wider, within the bound.
No kernel may reach another device: no remote copies, remote signals or barrier semaphores. Data moves between devices by JAX's collectives and lax.ppermute only.
A program may use at most 64 MiB of HBM per device.

v0:
```python
import jax
import jax.numpy as jnp
from jax import lax
from jax.sharding import PartitionSpec as P

D = 4096
BLOCK = 128


epsilon = 1e-06


def from_behind(value, axis, steps):
    count = lax.axis_size(axis)
    leading, last = (max(0, -steps), min(count, count - steps))
    return lax.ppermute(value, axis, [(source, source + steps) for source in range(leading, last)])


def block_owner(counts, num_blocks):
    padded = (counts + BLOCK - 1) // BLOCK * BLOCK
    ends = jnp.cumsum(padded)
    starts = jnp.arange(num_blocks, dtype=jnp.int32) * BLOCK
    owner = jnp.sum((starts[:, None] >= ends[None, :]).astype(jnp.int32), axis=1)
    return jnp.minimum(owner, counts.shape[0] - 1)


def on_device(
    stream_q,
    stream_k,
    stream_v,
    conv_taps,
    norm_gain,
    slot_token,
    expert_count,
    route_prob,
    w_proj,
    grad_out,
):
    stacked = jnp.stack([stream_q, stream_k, stream_v])
    before = from_behind(stacked[:, -2:, :], "dp", 1)
    extended = jnp.concatenate([before, stacked], axis=1).astype(jnp.float32)
    convolved = (
        conv_taps[:, 0, None, :] * extended[:, 2:]
        + conv_taps[:, 1, None, :] * extended[:, 1:-1]
        + conv_taps[:, 2, None, :] * extended[:, :-2]
    )
    mixed = (convolved[0] * convolved[1] * convolved[2]).astype(jnp.bfloat16)
    mixed_f = mixed.astype(jnp.float32)
    total = lax.psum(jnp.sum(mixed_f * mixed_f, axis=1), "expert")
    inv_rms = lax.rsqrt(total / D + epsilon)
    normed = (mixed_f * inv_rms[:, None] * norm_gain.astype(jnp.float32)).astype(jnp.bfloat16)
    gathered = lax.all_gather(normed, "expert", axis=1, tiled=True)
    tok_count = gathered.shape[0]
    slots = slot_token[0]
    num_blocks = slots.shape[0] // BLOCK
    owner = block_owner(expert_count[0], num_blocks)
    padded_rows = jnp.concatenate(
        [gathered, jnp.zeros((1, gathered.shape[1]), jnp.bfloat16)], axis=0
    )
    x_blocks = padded_rows[slots].reshape(num_blocks, BLOCK, gathered.shape[1])
    hid_local = w_proj.shape[2]
    experts_here = w_proj.shape[1]
    selector = (owner[:, None] == jnp.arange(experts_here, dtype=jnp.int32)[None, :]).astype(
        jnp.bfloat16
    )
    columns = x_blocks
    chosen_w = jnp.einsum(
        "neh,be->bnh",
        lax.all_gather(w_proj, "dp", axis=0, tiled=True),
        selector,
        preferred_element_type=jnp.float32,
    ).astype(jnp.bfloat16)
    pre_act = jnp.einsum("brn,bnh->brh", columns, chosen_w, preferred_element_type=jnp.float32)
    pre_act = pre_act.reshape(num_blocks * BLOCK, hid_local)
    slot_prob = jnp.concatenate([route_prob, jnp.zeros((1,), jnp.float32)])[slots][:, None]
    sigmoid_z = jax.nn.sigmoid(pre_act)
    hidden = (slot_prob * pre_act * sigmoid_z).astype(jnp.bfloat16)
    activation = (
        jnp.zeros((tok_count + 1, hid_local), jnp.bfloat16).at[slots].set(hidden)[:tok_count]
    )
    slot_grad = jnp.concatenate([grad_out, jnp.zeros((1, hid_local), jnp.bfloat16)], axis=0)[
        slots
    ].astype(jnp.float32)
    grad_pre = (slot_grad * slot_prob * sigmoid_z * (1.0 + pre_act * (1.0 - sigmoid_z))).astype(
        jnp.bfloat16
    )
    grad_blocks = grad_pre.reshape(num_blocks, BLOCK, hid_local)
    masked_grad = grad_blocks[None, :, :, :] * selector.T[:, :, None, None]
    columns = x_blocks
    weight_grad = lax.psum_scatter(
        jnp.einsum(
            "brd,ebrh->deh", columns, masked_grad, preferred_element_type=jnp.float32
        ).astype(jnp.bfloat16),
        "dp",
        scatter_dimension=0,
        tiled=True,
    ).astype(jnp.float32)
    return (activation, weight_grad)


def solution(mesh):
    placed = (
        P("dp", "expert"),
        P("dp", "expert"),
        P("dp", "expert"),
        P(None, None, "expert"),
        P("expert"),
        P("dp", None),
        P("dp", None),
        P("dp"),
        P("dp", None, "expert"),
        P("dp", "expert"),
    )
    return jax.shard_map(
        on_device,
        mesh=mesh,
        in_specs=placed,
        out_specs=(P("dp", "expert"), P("dp", None, "expert")),
        check_vma=False,
    )
```

profile of v0, /device:TPU:1, one launch (start us, length us, event | category | flops | bytes accessed | tf_op | source)
XLA Modules:
  0.0 302.4 jit_solution(1994741817525698117)
XLA Ops:
  7.2 0.0 copy-start.2
  7.2 0.0 copy-start.3
  7.2 0.0 all-gather.3.cloned.1.call-start
  7.2 0.7 pad_maximum_fusion.1
  8.0 4.6 %collective-permute-start = (bf16[3,2,128]{2,1,0:T(2,128)(2,1)S(1)}, bf16[3,2,128]{2,1,0:T(2,128)(2,1)S(1)}, u32[]{:S(2)}, u32[]{:S(2)}) collective-permute-start(bf16[3,2,128]{2,1,0:T(2,128)(2,1)S(1)} %pad_maximum_fusion.1), channel_id=1, source_target_pairs={{0,32},{32,64},{64,96},{96,128},{128,160},{160,192},{192,224},{224... | collective-permute-start | bytes 4616 | tf_op jit(solution)/shard_map/ppermute | solution.py:16
  12.6 0.8 fusion.29
  13.4 0.7 convert_element_type.59
  14.0 2.7 collective-permute-done
  16.7 0.9 maximum_convert_fusion
  17.7 0.1 fusion.2
  17.8 0.1 fusion.15
  17.9 64.4 %psum.7 = f32[256]{0:T(256)S(1)} all-reduce(f32[256]{0:T(256)S(1)} %get-tuple-element.10), channel_id=1, replica_groups=mesh['dp'=16,'expert'=32] {'expert'}, use_global_device_ids=true, to_apply=%region_1.0 | all-reduce | flops 256 | bytes 2048 | tf_op jit(solution)/shard_map/psum | solution.py:49
  82.4 0.7 fusion.17
  83.1 0.0 all-gather.3.cloned.1.call-update
  83.2 0.0 all-gather.5.cloned.1.call-start
  83.2 0.7 all-gather.5.cloned.1.call-update
  83.9 0.0 reduce-scatter.2.cloned.1.call-start
  84.0 0.7 pad_maximum_fusion
  84.6 0.7 fusion.24
  85.4 2.8 gather_fusion
  88.2 0.0 copy-done.2
  88.2 2.6 gather_fusion.2
  90.7 0.0 copy-done.3
  90.8 0.2 reduce-window.8
  90.9 0.1 fusion.25
  91.0 78.4 %all-gather.3.cloned.1.call-done = bf16[256,4096]{1,0:T(8,128)(2,1)} async-done(((bf16[256,128]{1,0:T(8,128)(2,1)}), bf16[256,4096]{1,0:T(8,128)(2,1)}) %all-gather.3.cloned.1.call-update) | async-done | bytes 2097168 | tf_op jit(solution)/shard_map/all_gather | solution.py:52
  169.4 1.8 concatenate.14
  171.2 4.1 %gather_fusion.1 = bf16[384,4096]{1,0:T(8,128)(2,1)} fusion(bf16[257,4096]{1,0:T(8,128)(2,1)S(1)} %concatenate.14, s32[1024]{0:T(1024)S(1)} %pad_clamp_fusion), kind=kCustom, calls=%fused_computation.1 | custom fusion | bytes 6292992 | tf_op jit(solution)/shard_map/gather | solution.py:60
  175.3 0.0 copy-start
  175.3 43.4 %all-gather.5.cloned.1.call-done = bf16[4096,2,256]{2,1,0:T(2,128)(2,1)} async-done(((bf16[256,2,256]{2,1,0:T(2,128)(2,1)}), bf16[4096,2,256]{2,1,0:T(2,128)(2,1)}) %all-gather.5.cloned.1.call-update) | async-done | bytes 4194320 | tf_op jit(solution)/shard_map/all_gather | solution.py:69
  218.6 0.0 copy-start.1
  218.6 7.5 %convolution_convert_fusion = bf16[3,4096,256]{2,0,1:T(4,128)(2,1)S(1)} fusion(bf16[4096,2,256]{2,1,0:T(2,128)(2,1)} %all-gather.5.cloned.1.call-done, s32[3]{0:T(128)S(1)} %broadcast_minimum_fusion), kind=kOutput, calls=%fused_computation.5 | convolution fusion | flops 15728646 | bytes 10485772 | tf_op jit(solution)/shard_map/neh,be->bnh/dot_general | solution.py:67
  226.1 0.0 copy-done
  226.1 0.0 copy-done.1
  226.1 1.3 fusion.6
  227.4 4.4 %bitcast_convert_fusion = bf16[4096,2,256]{2,0,1:T(8,128)(2,1)} fusion(bf16[3,128,4096,1]{2,1,0,3:T(8,128)(2,1)S(1)} %bitcast.50, bf16[2,3]{1,0:T(2,128)(2,1)S(1)} %compare_convert_fusion, bf16[3,128,256]{2,1,0:T(8,128)(2,1)S(1)} %get-tuple-element.15), kind=kOutput, calls=%fused_computation.4 | convolution fusion | flops 1613496320 | bytes 7536652 | tf_op jit(solution)/shard_map/brd,ebrh->deh/dot_general | solution.py:91
  231.8 0.0 reduce-scatter.2.cloned.1.call-update
  231.8 0.1 fusion.8
  232.0 1.9 scatter_custom_fusion
  233.9 0.7 slice.56
  234.5 59.3 %reduce-scatter.2.cloned.1.call-done = bf16[256,2,256]{2,0,1:T(8,128)(2,1)} async-done(((bf16[4096,2,256]{2,0,1:T(8,128)(2,1)}), bf16[256,2,256]{2,0,1:T(8,128)(2,1)}) %reduce-scatter.2.cloned.1.call-update) | async-done | bytes 262160 | tf_op jit(solution)/shard_map/reduce_scatter | solution.py:90
  293.8 2.0 copy.21
  (9 shorter events, 0.1 us)
Async XLA Ops:
  7.2 81.0 %copy-start.2 = (bf16[256,256]{1,0:T(8,128)(2,1)S(1)}, bf16[256,256]{1,0:T(8,128)(2,1)}, u32[]{:S(2)}) copy-start(bf16[256,256]{1,0:T(8,128)(2,1)} %param.19) | copy-start | bytes 393220
  7.2 83.6 %copy-start.3 = (s32[1,2]{1,0:T(1,128)S(1)}, s32[1,2]{1,0:T(1,128)}, u32[]{:S(2)}) copy-start(s32[1,2]{1,0:T(1,128)} %param.16) | copy-start | bytes 28
  7.2 162.2 %all-gather.3.cloned.1.call-start = ((), (), s32[]{:S(2)}) async-start(), calls=%async_computation.1 | async-start | bytes 2162688 | tf_op jit(solution)/shard_map/all_gather | solution.py:52
  8.0 8.8 %collective-permute-start = (bf16[3,2,128]{2,1,0:T(2,128)(2,1)S(1)}, bf16[3,2,128]{2,1,0:T(2,128)(2,1)S(1)}, u32[]{:S(2)}, u32[]{:S(2)}) collective-permute-start(bf16[3,2,128]{2,1,0:T(2,128)(2,1)S(1)} %pad_maximum_fusion.1), channel_id=1, source_target_pairs={{0,32},{32,64},{64,96},{96,128},{128,160},{160,192},{192,224},{224... | collective-permute-start | bytes 4616 | tf_op jit(solution)/shard_map/ppermute | solution.py:16
  83.2 135.5 %all-gather.5.cloned.1.call-start = ((), (), s32[]{:S(2)}) async-start(), calls=%async_computation.2 | async-start | bytes 4456448 | tf_op jit(solution)/shard_map/all_gather | solution.py:69
  83.9 209.9 %reduce-scatter.2.cloned.1.call-start = ((), (), s32[]{:S(2)}) async-start(), calls=%async_computation.3 | async-start | bytes 4456448 | tf_op jit(solution)/shard_map/reduce_scatter | solution.py:90
  175.3 50.9 %copy-start = (bf16[384,4096]{1,0:T(8,128)(2,1)S(1)}, bf16[384,4096]{1,0:T(8,128)(2,1)}, u32[]{:S(2)}) copy-start(bf16[384,4096]{1,0:T(8,128)(2,1)} %gather_fusion.1) | copy-start | bytes 9437188
  218.6 7.5 %copy-start.1 = (bf16[384,256]{1,0:T(8,128)(2,1)S(1)}, bf16[384,256]{1,0:T(8,128)(2,1)}, u32[]{:S(2)}) copy-start(bf16[384,256]{1,0:T(8,128)(2,1)} %gather_fusion.2) | copy-start | bytes 589828
Sparse Core Ops, SparseCore 0:
  83.3 86.0 all-gather.2
  171.5 47.0 all-gather.4
  232.0 61.8 reduce-scatter.1
where the time goes:
time: 304 us; the launch traced here: 302 us
  waiting for transfers between devices  184 us (61%)
  blocking collectives  64.4 us (21%)
  local copies, waits for them, and re-layouts  16.6 us (5%)
  between operations  13.9 us (5%)
  matrix products  13.1 us (4%)
  other arithmetic  5.15 us (2%)
  starting transfers between devices  4.7 us (2%)
    all_gather x1, waiting for transfers between devices, on_device(): gathered = lax.all_gather(normed, 'expert', axis=1, tiled=True)  78.4 us
    psum x1, blocking collectives, on_device(): total = lax.psum(jnp.sum(mixed_f * mixed_f, axis=1), 'expert')  64.4 us
    reduce_scatter x1, waiting for transfers between devices, on_device(): lax.psum_scatter(jnp.einsum('brd,ebrh->deh', columns, masked_grad, prefer...  59.3 us
    all_gather x1, waiting for transfers between devices, on_device(): lax.all_gather(w_proj, 'dp', axis=0, tiled=True)  43.4 us
    dot_general x1, matrix products, on_device(): jnp.einsum('neh,be->bnh', lax.all_gather(w_proj, 'dp', axis=0, tiled=True...  7.47 us
  transfers between devices with their start and end apart: 4, of which 4 were waited for; matrix products, arithmetic and copies ran while one was open for 6% of the time, Pallas kernels for 0%

commit v1 on v0

v1 whole, which is shorter than its diff:
```python
import functools

import jax
import jax.numpy as jnp
from jax import lax
from jax.experimental import pallas as pl
from jax.experimental.pallas import tpu as pltpu
from jax.sharding import PartitionSpec as P

D = 4096
BLOCK = 128
EPS = 1e-06
NZ, NX, NY = 8, 4, 8
TOK, CH, HID = 256, 128, 256
ROWS = TOK + 16
VMEM_LIMIT = 48 * 1024 * 1024
AXES = ("dp", "expert")
Z_GROUPS = [[z * NX + x for z in range(NZ)] for x in range(NX)]


def shift_x(value, steps):
    pairs = [
        (d * NZ * NX + z * NX + x, d * NZ * NX + z * NX + (x + steps) % NX)
        for d in range(2 * NY)
        for z in range(NZ)
        for x in range(NX)
    ]
    return lax.ppermute(value, AXES, pairs)


def to_row_block(value):
    pairs = [
        (i * NZ * NX + j, (j // 2) * NZ * NX + 2 * i + j % 2)
        for i in range(2 * NY)
        for j in range(NZ * NX)
    ]
    return lax.ppermute(value, AXES, pairs)


def gather_expert(copies):
    n, r, c = copies.shape
    b = lax.all_to_all(
        copies.reshape(n * r, c), "expert", 0, 0, axis_index_groups=Z_GROUPS, tiled=True
    ).reshape(n, r, c)
    low, high = b[: n // 2], b[n // 2 :]
    return (b, shift_x(b, 1), shift_x(b, -1), shift_x(low, 2), shift_x(high, -2))


def gathered_blocks(x_ref, parts):
    own, from_left, from_right, low, high = parts
    x = x_ref[0]
    for ref, off, z0 in (
        (own, 0, 0),
        (from_left, NX - 1, 0),
        (from_right, 1, 0),
        (low, 2, 0),
        (high, 2, NZ // 2),
    ):
        xx = lax.rem(x + off, NX)
        for k in range(ref.shape[0]):
            yield ref, k, (z0 + k) * NX + xx


def mix_kernel(q_ref, k_ref, v_ref, halo_ref, taps_ref, gain_ref, x1_ref, x2_ref):
    prod = None
    row = lax.broadcasted_iota(jnp.int32, (TOK, CH), 0)
    for s, ref in enumerate((q_ref, k_ref, v_ref)):
        cur = ref[...].astype(jnp.float32)
        h0 = halo_ref[s, 0:1, :].astype(jnp.float32)
        h1 = halo_ref[s, 1:2, :].astype(jnp.float32)
        lag1 = jnp.where(row == 0, h1, pltpu.roll(cur, 1, 0))
        lag2 = jnp.where(row == 0, h0, jnp.where(row == 1, h1, pltpu.roll(cur, 2, 0)))
        conv = (
            taps_ref[s, 0:1, :] * cur + taps_ref[s, 1:2, :] * lag1 + taps_ref[s, 2:3, :] * lag2
        )
        prod = conv if prod is None else prod * conv
    mixed = prod.astype(jnp.bfloat16)
    gain = gain_ref[...].astype(jnp.float32)
    tail = jnp.broadcast_to(gain, (16, CH)).astype(jnp.bfloat16)
    for n in range(NZ):
        x1_ref[n, 0:TOK, :] = mixed
        x1_ref[n, TOK:ROWS, :] = tail
    scaled = mixed.astype(jnp.float32) * gain
    x2_ref[...] = scaled.T.astype(jnp.bfloat16)


def forward_kernel(
    x_ref, count_ref, *refs
):
    parts = refs[:5]
    w_ref, g_ref, prob_ref, slot_ref, act_ref, gm_ref, xn_ref = refs[5:]
    square = jnp.zeros((TOK, CH), jnp.float32)
    for ref, k, j in gathered_blocks(x_ref, parts):
        m = ref[k, 0:TOK, :].astype(jnp.float32)
        gain = ref[k, TOK : TOK + 16, :].astype(jnp.float32)[0:1, :]
        square = square + m * m
        xn_ref[:, pl.ds(pl.multiple_of(j * CH, CH), CH)] = (m * gain).astype(jnp.bfloat16)
    inv = lax.rsqrt(jnp.sum(square, axis=1, keepdims=True) / D + EPS)
    both = jnp.dot(xn_ref[...], w_ref[...], preferred_element_type=jnp.float32)
    first = (count_ref[0, 0] + BLOCK - 1) // BLOCK * BLOCK
    slots = slot_ref.shape[1]
    tok = lax.broadcasted_iota(jnp.int32, (TOK, slots), 0)
    place = lax.broadcasted_iota(jnp.int32, (TOK, slots), 1)
    hit = jnp.where((slot_ref[...] == tok) & (place >= first), 1.0, 0.0)
    second = jnp.sum(hit, axis=1, keepdims=True) > 0.5
    r = lax.broadcasted_iota(jnp.int32, (TOK, TOK), 0)
    c = lax.broadcasted_iota(jnp.int32, (TOK, TOK), 1)
    prob = jnp.sum(jnp.where(r == c, prob_ref[...], 0.0), axis=1, keepdims=True)
    pre = jnp.where(second, both[:, HID:], both[:, :HID]) * inv
    sig = jax.nn.sigmoid(pre)
    act_ref[...] = (prob * pre * sig).astype(jnp.bfloat16)
    grad = g_ref[...].astype(jnp.float32) * prob * sig * (1.0 + pre * (1.0 - sig)) * inv
    gm_ref[:, :HID] = jnp.where(second, 0.0, grad).astype(jnp.bfloat16)
    gm_ref[:, HID:] = jnp.where(second, grad, 0.0).astype(jnp.bfloat16)


def weight_kernel(x_ref, *refs):
    parts = refs[:5]
    gm_ref, out_ref, xt_ref = refs[5:]
    for ref, k, j in gathered_blocks(x_ref, parts):
        half = lax.rem(j, 2)
        i = lax.div(j, 2)
        xt_ref[
            pl.ds(pl.multiple_of(half * CH, CH), CH), pl.ds(pl.multiple_of(i * TOK, TOK), TOK)
        ] = ref[k]
    out_ref[...] = jnp.dot(xt_ref[...], gm_ref[...], preferred_element_type=jnp.float32)


def vm(n):
    return [pl.BlockSpec(memory_space=pltpu.VMEM)] * n


def sm(n):
    return [pl.BlockSpec(memory_space=pltpu.SMEM)] * n


def on_device(
    stream_q,
    stream_k,
    stream_v,
    conv_taps,
    norm_gain,
    slot_token,
    expert_count,
    route_prob,
    w_proj,
    grad_out,
):
    params = pltpu.CompilerParams(vmem_limit_bytes=VMEM_LIMIT)
    bf, f32 = jnp.bfloat16, jnp.float32
    w_all = lax.all_gather(w_proj.reshape(TOK, 2 * HID), "dp", axis=0, tiled=True)
    last = jnp.stack([stream_q[-2:], stream_k[-2:], stream_v[-2:]])
    halo = lax.ppermute(last, "dp", [(s, s + 1) for s in range(2 * NY - 1)])
    x1, x2 = pl.pallas_call(
        mix_kernel,
        out_shape=(
            jax.ShapeDtypeStruct((NZ, ROWS, CH), bf),
            jax.ShapeDtypeStruct((CH, TOK), bf),
        ),
        in_specs=vm(6),
        out_specs=tuple(vm(2)),
        compiler_params=params,
    )(stream_q, stream_k, stream_v, halo, conv_taps, norm_gain.reshape(1, CH))
    x_pos = lax.rem(lax.axis_index("expert"), NX).astype(jnp.int32).reshape(1)
    x1_parts = gather_expert(x1)
    activation, gm = pl.pallas_call(
        forward_kernel,
        out_shape=(
            jax.ShapeDtypeStruct((TOK, HID), bf),
            jax.ShapeDtypeStruct((TOK, 2 * HID), bf),
        ),
        in_specs=sm(2) + vm(9),
        out_specs=tuple(vm(2)),
        scratch_shapes=[pltpu.VMEM((TOK, D), bf)],
        compiler_params=params,
    )(
        x_pos,
        expert_count,
        *x1_parts,
        w_all,
        grad_out,
        route_prob.reshape(1, TOK),
        slot_token,
    )
    gm_all = lax.all_gather(gm, "dp", axis=0, tiled=True)
    x2 = to_row_block(x2)
    x2, _ = lax.optimization_barrier((x2, gm))
    x2_parts = gather_expert(jnp.broadcast_to(x2[None], (NZ, CH, TOK)))
    grad_w = pl.pallas_call(
        weight_kernel,
        out_shape=jax.ShapeDtypeStruct((TOK, 2 * HID), f32),
        in_specs=sm(1) + vm(6),
        out_specs=pl.BlockSpec(memory_space=pltpu.VMEM),
        scratch_shapes=[pltpu.VMEM((2 * CH, D), bf)],
        compiler_params=params,
    )(x_pos, *x2_parts, gm_all)
    return activation, grad_w.reshape(TOK, 2, HID)


def solution(mesh):
    placed = (
        P("dp", "expert"),
        P("dp", "expert"),
        P("dp", "expert"),
        P(None, None, "expert"),
        P("expert"),
        P("dp", None),
        P("dp", None),
        P("dp"),
        P("dp", None, "expert"),
        P("dp", "expert"),
    )
    return jax.shard_map(
        on_device,
        mesh=mesh,
        in_specs=placed,
        out_specs=(P("dp", "expert"), P("dp", None, "expert")),
        check_vma=False,
    )
```

time: 304 us -> 163 us (0.54)
  waiting for transfers between devices: 184 us -> 40.6 us
  starting transfers between devices: 4.7 us -> 34.3 us
  matrix products: 13.1 us -> 0 us
  blocking collectives: 64.4 us -> 52.1 us
  Pallas kernels: 0 us -> 8.64 us
  local copies, waits for them, and re-layouts: 16.6 us -> 11.1 us
  other arithmetic: 5.15 us -> 0.01 us
    all_gather x2, waiting for transfers between devices: 122 us -> 0.03 us  [the longest x1 0.01 us: on_device(): gm_all = lax.all_gather(gm, 'dp', axis=0, tiled=True)]
    psum x1 -> x0, blocking collectives: 64.4 us -> none  [on_device(): total = lax.psum(jnp.sum(mixed_f * mixed_f, axis=1), 'expert')]
    reduce_scatter x1 -> x0, waiting for transfers between devices: 59.3 us -> none  [on_device(): lax.psum_scatter(jnp.einsum('brd,ebrh->deh', columns, masked_grad, prefer...]
    all_to_all x0 -> x2, blocking collectives: none -> 52.1 us  [gather_expert(): lax.all_to_all(copies.reshape(n * r, c), 'expert', 0, 0, axis_index_group...]
    ppermute x1 -> x10, waiting for transfers between devices: 2.71 us -> 40.6 us  [the longest x8 33.8 us: shift_x(): return lax.ppermute(value, AXES, pairs)]
    ppermute x1 -> x10, starting transfers between devices: 4.58 us -> 34.2 us  [the longest x8 25.1 us: shift_x(): return lax.ppermute(value, AXES, pairs)]
    dot_general x3 -> x0, matrix products: 13.1 us -> none  [the longest x1 7.47 us: on_device(): jnp.einsum('neh,be->bnh', lax.all_gather(w_proj, 'dp', axis=0, tiled=True...]
    gather x3 -> x0, local copies, waits for them, and re-layouts: 9.42 us -> none  [the longest x1 4.06 us: on_device(): x_blocks = padded_rows[slots].reshape(num_blocks, BLOCK, gathered.shape[1])]
  transfers between devices with their start and end apart: 4 -> 12, of which waited for: 4 -> 6; matrix products, arithmetic and copies ran while one was open for 6% -> 1% of each run, Pallas kernels for 0% -> 0%
where the time goes in v1:
time: 163 us; the launch traced here: 161 us
  blocking collectives  52.1 us (32%)
  waiting for transfers between devices  40.6 us (25%)
  starting transfers between devices  34.3 us (21%)
  between operations  14.2 us (9%)
  local copies, waits for them, and re-layouts  11.1 us (7%)
  Pallas kernels  8.64 us (5%)
    all_to_all x2, blocking collectives, gather_expert(): lax.all_to_all(copies.reshape(n * r, c), 'expert', 0, 0, axis_index_group...  52.1 us
    ppermute x8, waiting for transfers between devices, shift_x(): return lax.ppermute(value, AXES, pairs)  33.8 us
    ppermute x8, starting transfers between devices, shift_x(): return lax.ppermute(value, AXES, pairs)  25.1 us
    unnamed x19, local copies, waits for them, and re-layouts  8.46 us
    pallas_call x1, Pallas kernels, on_device(): pl.pallas_call(forward_kernel, out_shape=(jax.ShapeDtypeStruct((TOK, HID)...  4.78 us
    ppermute x1, starting transfers between devices, on_device(): halo = lax.ppermute(last, 'dp', [(s, s + 1) for s in range(2 * NY - 1)])  4.59 us
    ppermute x1, starting transfers between devices, to_row_block(): return lax.ppermute(value, AXES, pairs)  4.51 us
    ppermute x1, waiting for transfers between devices, on_device(): halo = lax.ppermute(last, 'dp', [(s, s + 1) for s in range(2 * NY - 1)])  4.2 us
  transfers between devices with their start and end apart: 12, of which 6 were waited for; matrix products, arithmetic and copies ran while one was open for 1% of the time, Pallas kernels for 0%

profile of v1, /device:TPU:1, one launch (start us, length us, event | category | flops | bytes accessed | tf_op | source)
XLA Modules:
  0.0 161.0 jit_solution(14696139512884374117)
XLA Ops:
  7.2 0.0 all-gather.3.cloned.1.call-start
  7.2 1.7 %copy.12 = bf16[32,8,2,256]{3,1,2,0:T(8,128)(2,1)} copy(bf16[32,8,2,256]{3,2,1,0:T(2,128)(2,1)} %bitcast.14) | data formatting | bytes 524288
  8.9 0.0 all-gather.3.cloned.1.call-update
  8.9 0.0 all-gather.5.cloned.1.call-start
  9.0 0.7 slice_bitcast_fusion.2
  9.7 0.7 slice_bitcast_fusion
  10.4 4.6 %collective-permute-start = (bf16[3,2,128]{2,1,0:T(2,128)(2,1)S(1)}, bf16[3,2,128]{2,1,0:T(2,128)(2,1)S(1)}, u32[]{:S(2)}, u32[]{:S(2)}) collective-permute-start(bf16[3,2,128]{2,1,0:T(2,128)(2,1)S(1)} %pad_maximum_fusion), channel_id=1, source_target_pairs={{0,32},{32,64},{64,96},{96,128},{128,160},{160,192},{192,224},{224... | collective-permute-start | bytes 4616 | tf_op jit(solution)/shard_map/ppermute | solution.py:153
  15.0 4.2 %collective-permute-done.halo_ref = bf16[3,2,128]{2,1,0:T(2,128)(2,1)S(1)} collective-permute-done((bf16[3,2,128]{2,1,0:T(2,128)(2,1)S(1)}, bf16[3,2,128]{2,1,0:T(2,128)(2,1)S(1)}, u32[]{:S(2)}, u32[]{:S(2)}) %collective-permute-start) | collective-permute-done | bytes 1568 | tf_op jit(solution)/shard_map/ppermute | solution.py:153
  19.2 0.0 copy-start.1
  19.2 0.8 copy-done.1
  20.0 0.0 copy-start.2
  20.0 0.8 copy-done.2
  20.8 0.0 copy-start.3
  20.9 0.8 copy-done.3
  21.7 0.7 copy-done.4
  22.4 0.7 copy-done.7
  23.0 0.2 shard_map.113
  23.3 24.3 %all_to_all.12.refs_0_ = bf16[8,272,128]{2,1,0:T(8,128)(2,1)S(1)} all-to-all(bf16[8,272,128]{2,1,0:T(8,128)(2,1)S(1)} %get-tuple-element.7), channel_id=1, replica_groups={{0,4,8,12,16,20,24,28},{1,5,9,13,17,21,25,29},{2,6,10,14,18,22,26,30},{..., dimensions={0} | all-to-all | bytes 1114112 | tf_op jit(solution)/shard_map/all_to_all | solution.py:42
  47.6 4.4 %collective-permute-start.2 = (bf16[8,272,128]{2,1,0:T(8,128)(2,1)S(1)}, bf16[8,272,128]{2,1,0:T(8,128)(2,1)S(1)}, u32[]{:S(2)}, u32[]{:S(2)}) collective-permute-start(bf16[8,272,128]{2,1,0:T(8,128)(2,1)S(1)} %all_to_all.12.refs_0_), channel_id=1, source_target_pairs={{0,3},{1,0},{2,1},{3,2},{4,7},{5,4},{6,5},{7,6},{8,11},{9,8},{10,9... | collective-permute-start | bytes 1671176 | tf_op jit(solution)/shard_map/ppermute | solution.py:28
  51.9 1.9 %collective-permute-start.1 = (bf16[8,272,128]{2,1,0:T(8,128)(2,1)S(1)}, bf16[8,272,128]{2,1,0:T(8,128)(2,1)S(1)}, u32[]{:S(2)}, u32[]{:S(2)}) collective-permute-start(bf16[8,272,128]{2,1,0:T(8,128)(2,1)S(1)} %all_to_all.12.refs_0_), channel_id=1, source_target_pairs={{0,1},{1,2},{2,3},{3,0},{4,5},{5,6},{6,7},{7,4},{8,9},{9,10},{10,1... | collective-permute-start | bytes 1671176 | tf_op jit(solution)/shard_map/ppermute | solution.py:28
  53.9 3.6 %collective-permute-start.4 = (bf16[4,272,128]{2,1,0:T(8,128)(2,1)S(1)}, bf16[4,272,128]{2,1,0:T(8,128)(2,1)S(1)}, u32[]{:S(2)}, u32[]{:S(2)}) collective-permute-start(bf16[4,272,128]{2,1,0:T(8,128)(2,1)S(1)} %get-tuple-element.12), channel_id=1, source_target_pairs={{0,2},{1,3},{2,0},{3,1},{4,6},{5,7},{6,4},{7,5},{8,10},{9,11},{10,... | collective-permute-start | bytes 835592 | tf_op jit(solution)/shard_map/ppermute | solution.py:28
  57.6 3.2 %collective-permute-start.3 = (bf16[4,272,128]{2,1,0:T(8,128)(2,1)S(1)}, bf16[4,272,128]{2,1,0:T(8,128)(2,1)S(1)}, u32[]{:S(2)}, u32[]{:S(2)}) collective-permute-start(bf16[4,272,128]{2,1,0:T(8,128)(2,1)S(1)} %get-tuple-element.13), channel_id=1, source_target_pairs={{0,2},{1,3},{2,0},{3,1},{4,6},{5,7},{6,4},{7,5},{8,10},{9,11},{10,... | collective-permute-start | bytes 835592 | tf_op jit(solution)/shard_map/ppermute | solution.py:28
  60.7 12.9 %collective-permute-done.4.refs_4_ = bf16[4,272,128]{2,1,0:T(8,128)(2,1)S(1)} collective-permute-done((bf16[4,272,128]{2,1,0:T(8,128)(2,1)S(1)}, bf16[4,272,128]{2,1,0:T(8,128)(2,1)S(1)}, u32[]{:S(2)}, u32[]{:S(2)}) %collective-permute-start.4) | collective-permute-done | bytes 278560 | tf_op jit(solution)/shard_map/ppermute | solution.py:28
  73.7 6.0 %collective-permute-done.3.refs_3_ = bf16[4,272,128]{2,1,0:T(8,128)(2,1)S(1)} collective-permute-done((bf16[4,272,128]{2,1,0:T(8,128)(2,1)S(1)}, bf16[4,272,128]{2,1,0:T(8,128)(2,1)S(1)}, u32[]{:S(2)}, u32[]{:S(2)}) %collective-permute-start.3) | collective-permute-done | bytes 278560 | tf_op jit(solution)/shard_map/ppermute | solution.py:28
  79.6 0.0 collective-permute-done.2.refs_2_
  79.6 0.0 collective-permute-done.1.refs_1_
  79.6 0.0 all-gather.3.cloned.1.call-done.refs_5_
  79.6 0.0 copy-start
  79.7 0.9 copy-done
  80.6 0.7 copy-done.5
  81.2 0.7 copy-done.6
  81.9 0.7 copy-done.8
  82.6 4.8 %shard_map.114 = (bf16[256,256]{1,0:T(8,128)(2,1)}, bf16[256,512]{1,0:T(8,128)(2,1)}) custom-call(s32[1]{0:T(128)} %bitcast.x_ref, s32[1,2]{1,0:T(1,128)S(1)} %copy-done.8, bf16[8,272,128]{2,1,0:T(8,128)(2,1)S(1)} %all_to_all.12.refs_0_, bf16[8,272,128]{2,1,0:T(8,128)(2,1)S(1)} %collective-permute-done.1.refs_1_, ...), custom_call_target="tpu_custom_call" | custom-call | tf_op jit(solution)/shard_map/pallas_call | solution.py:166
  87.3 0.0 all-gather.5.cloned.1.call-update
  87.4 4.5 %collective-permute-start.5 = (bf16[128,256]{1,0:T(8,128)(2,1)S(1)}, bf16[128,256]{1,0:T(8,128)(2,1)S(1)}, u32[]{:S(2)}, u32[]{:S(2)}) collective-permute-start(bf16[128,256]{1,0:T(8,128)(2,1)S(1)} %get-tuple-element.9), channel_id=1, source_target_pairs={{0,0},{1,1},{2,32},{3,33},{4,64},{5,65},{6,96},{7,97},{8,128},{9,1... | collective-permute-start | bytes 196616 | tf_op jit(solution)/shard_map/ppermute | solution.py:37
  91.9 2.6 %collective-permute-done.5 = bf16[128,256]{1,0:T(8,128)(2,1)S(1)} collective-permute-done((bf16[128,256]{1,0:T(8,128)(2,1)S(1)}, bf16[128,256]{1,0:T(8,128)(2,1)S(1)}, u32[]{:S(2)}, u32[]{:S(2)}) %collective-permute-start.5) | collective-permute-done | bytes 65568 | tf_op jit(solution)/shard_map/ppermute | solution.py:37
  94.5 27.8 %all_to_all.13.refs_0_ = bf16[8,128,256]{2,1,0:T(8,128)(2,1)S(1)} all-to-all(bf16[8,128,256]{2,1,0:T(8,128)(2,1)S(1)} %broadcast_in_dim.2), channel_id=1, replica_groups={{0,4,8,12,16,20,24,28},{1,5,9,13,17,21,25,29},{2,6,10,14,18,22,26,30},{..., dimensions={0} | all-to-all | bytes 1048576 | tf_op jit(solution)/shard_map/all_to_all | solution.py:42
  122.3 1.9 %collective-permute-start.7 = (bf16[8,128,256]{2,1,0:T(8,128)(2,1)S(1)}, bf16[8,128,256]{2,1,0:T(8,128)(2,1)S(1)}, u32[]{:S(2)}, u32[]{:S(2)}) collective-permute-start(bf16[8,128,256]{2,1,0:T(8,128)(2,1)S(1)} %all_to_all.13.refs_0_), channel_id=1, source_target_pairs={{0,3},{1,0},{2,1},{3,2},{4,7},{5,4},{6,5},{7,6},{8,11},{9,8},{10,9... | collective-permute-start | bytes 1572872 | tf_op jit(solution)/shard_map/ppermute | solution.py:28
  124.2 3.4 %collective-permute-start.6 = (bf16[8,128,256]{2,1,0:T(8,128)(2,1)S(1)}, bf16[8,128,256]{2,1,0:T(8,128)(2,1)S(1)}, u32[]{:S(2)}, u32[]{:S(2)}) collective-permute-start(bf16[8,128,256]{2,1,0:T(8,128)(2,1)S(1)} %all_to_all.13.refs_0_), channel_id=1, source_target_pairs={{0,1},{1,2},{2,3},{3,0},{4,5},{5,6},{6,7},{7,4},{8,9},{9,10},{10,1... | collective-permute-start | bytes 1572872 | tf_op jit(solution)/shard_map/ppermute | solution.py:28
  127.6 2.1 %collective-permute-start.9 = (bf16[4,128,256]{2,1,0:T(8,128)(2,1)S(1)}, bf16[4,128,256]{2,1,0:T(8,128)(2,1)S(1)}, u32[]{:S(2)}, u32[]{:S(2)}) collective-permute-start(bf16[4,128,256]{2,1,0:T(8,128)(2,1)S(1)} %get-tuple-element.14), channel_id=1, source_target_pairs={{0,2},{1,3},{2,0},{3,1},{4,6},{5,7},{6,4},{7,5},{8,10},{9,11},{10,... | collective-permute-start | bytes 786440 | tf_op jit(solution)/shard_map/ppermute | solution.py:28
  129.8 4.7 %collective-permute-start.8 = (bf16[4,128,256]{2,1,0:T(8,128)(2,1)S(1)}, bf16[4,128,256]{2,1,0:T(8,128)(2,1)S(1)}, u32[]{:S(2)}, u32[]{:S(2)}) collective-permute-start(bf16[4,128,256]{2,1,0:T(8,128)(2,1)S(1)} %get-tuple-element.15), channel_id=1, source_target_pairs={{0,2},{1,3},{2,0},{3,1},{4,6},{5,7},{6,4},{7,5},{8,10},{9,11},{10,... | collective-permute-start | bytes 786440 | tf_op jit(solution)/shard_map/ppermute | solution.py:28
  134.4 9.3 %collective-permute-done.9.refs_4_ = bf16[4,128,256]{2,1,0:T(8,128)(2,1)S(1)} collective-permute-done((bf16[4,128,256]{2,1,0:T(8,128)(2,1)S(1)}, bf16[4,128,256]{2,1,0:T(8,128)(2,1)S(1)}, u32[]{:S(2)}, u32[]{:S(2)}) %collective-permute-start.9) | collective-permute-done | bytes 262176 | tf_op jit(solution)/shard_map/ppermute | solution.py:28
  143.7 5.6 %collective-permute-done.8.refs_3_ = bf16[4,128,256]{2,1,0:T(8,128)(2,1)S(1)} collective-permute-done((bf16[4,128,256]{2,1,0:T(8,128)(2,1)S(1)}, bf16[4,128,256]{2,1,0:T(8,128)(2,1)S(1)}, u32[]{:S(2)}, u32[]{:S(2)}) %collective-permute-start.8) | collective-permute-done | bytes 262176 | tf_op jit(solution)/shard_map/ppermute | solution.py:28
  149.4 0.0 collective-permute-done.7.refs_2_
  149.4 0.0 collective-permute-done.6.refs_1_
  149.4 0.0 all-gather.5.cloned.1.call-done.refs_5_
  149.4 3.6 %shard_map.115 = f32[256,512]{1,0:T(8,128)S(1)} custom-call(s32[1]{0:T(128)} %bitcast.x_ref, bf16[8,128,256]{2,1,0:T(8,128)(2,1)S(1)} %all_to_all.13.refs_0_, bf16[8,128,256]{2,1,0:T(8,128)(2,1)S(1)} %collective-permute-done.6.refs_1_, bf16[8,128,256]{2,1,0:T(8,128)(2,1)S(1)} %collective-permute-done.7.refs_2_, ...), custom_call_target="tpu_custom_call" | custom-call | tf_op jit(solution)/shard_map/pallas_call | solution.py:189
  153.0 1.1 reshape.48
  (9 shorter events, 0.1 us)
Async XLA Ops:
  7.2 72.5 %all-gather.3.cloned.1.call-start = ((), (), s32[]{:S(2)}) async-start(), calls=%async_computation.2 | async-start | bytes 4456448 | tf_op jit(solution)/shard_map/all_gather | solution.py:151
  8.9 140.5 %all-gather.5.cloned.1.call-start = ((), (), s32[]{:S(2)}) async-start(), calls=%async_computation.3 | async-start | bytes 4456448 | tf_op jit(solution)/shard_map/all_gather | solution.py:185
  10.4 8.8 %collective-permute-start = (bf16[3,2,128]{2,1,0:T(2,128)(2,1)S(1)}, bf16[3,2,128]{2,1,0:T(2,128)(2,1)S(1)}, u32[]{:S(2)}, u32[]{:S(2)}) collective-permute-start(bf16[3,2,128]{2,1,0:T(2,128)(2,1)S(1)} %pad_maximum_fusion), channel_id=1, source_target_pairs={{0,32},{32,64},{64,96},{96,128},{128,160},{160,192},{192,224},{224... | collective-permute-start | bytes 4616 | tf_op jit(solution)/shard_map/ppermute | solution.py:153
  19.2 0.8 copy-start.1
  20.0 0.8 copy-start.2
  20.8 0.8 copy-start.3
  21.7 0.7 copy-start.4
  22.4 0.7 copy-start.7
  47.6 32.1 %collective-permute-start.2 = (bf16[8,272,128]{2,1,0:T(8,128)(2,1)S(1)}, bf16[8,272,128]{2,1,0:T(8,128)(2,1)S(1)}, u32[]{:S(2)}, u32[]{:S(2)}) collective-permute-start(bf16[8,272,128]{2,1,0:T(8,128)(2,1)S(1)} %all_to_all.12.refs_0_), channel_id=1, source_target_pairs={{0,3},{1,0},{2,1},{3,2},{4,7},{5,4},{6,5},{7,6},{8,11},{9,8},{10,9... | collective-permute-start | bytes 1671176 | tf_op jit(solution)/shard_map/ppermute | solution.py:28
  51.9 27.7 %collective-permute-start.1 = (bf16[8,272,128]{2,1,0:T(8,128)(2,1)S(1)}, bf16[8,272,128]{2,1,0:T(8,128)(2,1)S(1)}, u32[]{:S(2)}, u32[]{:S(2)}) collective-permute-start(bf16[8,272,128]{2,1,0:T(8,128)(2,1)S(1)} %all_to_all.12.refs_0_), channel_id=1, source_target_pairs={{0,1},{1,2},{2,3},{3,0},{4,5},{5,6},{6,7},{7,4},{8,9},{9,10},{10,1... | collective-permute-start | bytes 1671176 | tf_op jit(solution)/shard_map/ppermute | solution.py:28
  53.9 19.7 %collective-permute-start.4 = (bf16[4,272,128]{2,1,0:T(8,128)(2,1)S(1)}, bf16[4,272,128]{2,1,0:T(8,128)(2,1)S(1)}, u32[]{:S(2)}, u32[]{:S(2)}) collective-permute-start(bf16[4,272,128]{2,1,0:T(8,128)(2,1)S(1)} %get-tuple-element.12), channel_id=1, source_target_pairs={{0,2},{1,3},{2,0},{3,1},{4,6},{5,7},{6,4},{7,5},{8,10},{9,11},{10,... | collective-permute-start | bytes 835592 | tf_op jit(solution)/shard_map/ppermute | solution.py:28
  57.6 22.1 %collective-permute-start.3 = (bf16[4,272,128]{2,1,0:T(8,128)(2,1)S(1)}, bf16[4,272,128]{2,1,0:T(8,128)(2,1)S(1)}, u32[]{:S(2)}, u32[]{:S(2)}) collective-permute-start(bf16[4,272,128]{2,1,0:T(8,128)(2,1)S(1)} %get-tuple-element.13), channel_id=1, source_target_pairs={{0,2},{1,3},{2,0},{3,1},{4,6},{5,7},{6,4},{7,5},{8,10},{9,11},{10,... | collective-permute-start | bytes 835592 | tf_op jit(solution)/shard_map/ppermute | solution.py:28
  79.6 0.9 copy-start
  80.6 0.7 copy-start.5
  81.2 0.7 copy-start.6
  81.9 0.7 copy-start.8
  87.4 7.1 %collective-permute-start.5 = (bf16[128,256]{1,0:T(8,128)(2,1)S(1)}, bf16[128,256]{1,0:T(8,128)(2,1)S(1)}, u32[]{:S(2)}, u32[]{:S(2)}) collective-permute-start(bf16[128,256]{1,0:T(8,128)(2,1)S(1)} %get-tuple-element.9), channel_id=1, source_target_pairs={{0,0},{1,1},{2,32},{3,33},{4,64},{5,65},{6,96},{7,97},{8,128},{9,1... | collective-permute-start | bytes 196616 | tf_op jit(solution)/shard_map/ppermute | solution.py:37
  122.3 27.1 %collective-permute-start.7 = (bf16[8,128,256]{2,1,0:T(8,128)(2,1)S(1)}, bf16[8,128,256]{2,1,0:T(8,128)(2,1)S(1)}, u32[]{:S(2)}, u32[]{:S(2)}) collective-permute-start(bf16[8,128,256]{2,1,0:T(8,128)(2,1)S(1)} %all_to_all.13.refs_0_), channel_id=1, source_target_pairs={{0,3},{1,0},{2,1},{3,2},{4,7},{5,4},{6,5},{7,6},{8,11},{9,8},{10,9... | collective-permute-start | bytes 1572872 | tf_op jit(solution)/shard_map/ppermute | solution.py:28
  124.2 25.1 %collective-permute-start.6 = (bf16[8,128,256]{2,1,0:T(8,128)(2,1)S(1)}, bf16[8,128,256]{2,1,0:T(8,128)(2,1)S(1)}, u32[]{:S(2)}, u32[]{:S(2)}) collective-permute-start(bf16[8,128,256]{2,1,0:T(8,128)(2,1)S(1)} %all_to_all.13.refs_0_), channel_id=1, source_target_pairs={{0,1},{1,2},{2,3},{3,0},{4,5},{5,6},{6,7},{7,4},{8,9},{9,10},{10,1... | collective-permute-start | bytes 1572872 | tf_op jit(solution)/shard_map/ppermute | solution.py:28
  127.6 16.1 %collective-permute-start.9 = (bf16[4,128,256]{2,1,0:T(8,128)(2,1)S(1)}, bf16[4,128,256]{2,1,0:T(8,128)(2,1)S(1)}, u32[]{:S(2)}, u32[]{:S(2)}) collective-permute-start(bf16[4,128,256]{2,1,0:T(8,128)(2,1)S(1)} %get-tuple-element.14), channel_id=1, source_target_pairs={{0,2},{1,3},{2,0},{3,1},{4,6},{5,7},{6,4},{7,5},{8,10},{9,11},{10,... | collective-permute-start | bytes 786440 | tf_op jit(solution)/shard_map/ppermute | solution.py:28
  129.8 19.6 %collective-permute-start.8 = (bf16[4,128,256]{2,1,0:T(8,128)(2,1)S(1)}, bf16[4,128,256]{2,1,0:T(8,128)(2,1)S(1)}, u32[]{:S(2)}, u32[]{:S(2)}) collective-permute-start(bf16[4,128,256]{2,1,0:T(8,128)(2,1)S(1)} %get-tuple-element.15), channel_id=1, source_target_pairs={{0,2},{1,3},{2,0},{3,1},{4,6},{5,7},{6,4},{7,5},{8,10},{9,11},{10,... | collective-permute-start | bytes 786440 | tf_op jit(solution)/shard_map/ppermute | solution.py:28
Sparse Core Ops, SparseCore 0:
  10.7 50.4 all-gather.2
  87.5 40.8 all-gather.4

commit v2 on v1

--- a/solution.py
+++ b/solution.py
@@ -37,13 +37,16 @@
     return lax.ppermute(value, AXES, pairs)
 
 
-def gather_expert(copies):
+def spread_z(copies):
     n, r, c = copies.shape
-    b = lax.all_to_all(
+    return lax.all_to_all(
         copies.reshape(n * r, c), "expert", 0, 0, axis_index_groups=Z_GROUPS, tiled=True
     ).reshape(n, r, c)
-    low, high = b[: n // 2], b[n // 2 :]
-    return (b, shift_x(b, 1), shift_x(b, -1), shift_x(low, 2), shift_x(high, -2))
+
+
+def spread_x(b):
+    half = b.shape[0] // 2
+    return (b, shift_x(b, 1), shift_x(b, -1), shift_x(b[:half], 2), shift_x(b[half:], -2))
 
 
 def gathered_blocks(x_ref, parts):
@@ -61,13 +64,42 @@
             yield ref, k, (z0 + k) * NX + xx
 
 
-def mix_kernel(q_ref, k_ref, v_ref, halo_ref, taps_ref, gain_ref, x1_ref, x2_ref):
+def load_all(pairs, sems):
+    copies = [pltpu.make_async_copy(src, dst, sems.at[n]) for n, (src, dst) in enumerate(pairs)]
+    for copy in copies:
+        copy.start()
+    return copies
+
+
+def pack_kernel(q_ref, k_ref, v_ref, out_ref, sems):
+    last = pl.ds(TOK - 16, 16)
+    for copy in load_all(
+        [(r.at[last], out_ref.at[s]) for s, r in enumerate((q_ref, k_ref, v_ref))], sems
+    ):
+        copy.wait()
+
+
+def mix_kernel(
+    q_hbm, k_hbm, v_hbm, taps_hbm, gain_hbm, halo_ref, x1_ref, x2_ref,
+    q_ref, k_ref, v_ref, taps_ref, gain_ref, sems,
+):
+    for copy in load_all(
+        [
+            (q_hbm, q_ref),
+            (k_hbm, k_ref),
+            (v_hbm, v_ref),
+            (taps_hbm, taps_ref),
+            (gain_hbm, gain_ref),
+        ],
+        sems,
+    ):
+        copy.wait()
     prod = None
     row = lax.broadcasted_iota(jnp.int32, (TOK, CH), 0)
     for s, ref in enumerate((q_ref, k_ref, v_ref)):
         cur = ref[...].astype(jnp.float32)
-        h0 = halo_ref[s, 0:1, :].astype(jnp.float32)
-        h1 = halo_ref[s, 1:2, :].astype(jnp.float32)
+        before = halo_ref[s].astype(jnp.float32)
+        h0, h1 = before[14:15, :], before[15:16, :]
         lag1 = jnp.where(row == 0, h1, pltpu.roll(cur, 1, 0))
         lag2 = jnp.where(row == 0, h0, jnp.where(row == 1, h1, pltpu.roll(cur, 2, 0)))
         conv = (
@@ -84,11 +116,12 @@
     x2_ref[...] = scaled.T.astype(jnp.bfloat16)
 
 
-def forward_kernel(
-    x_ref, count_ref, *refs
-):
+def forward_kernel(x_ref, *refs):
     parts = refs[:5]
-    w_ref, g_ref, prob_ref, slot_ref, act_ref, gm_ref, xn_ref = refs[5:]
+    sources, (act_ref, gm_ref, xn_ref) = refs[5:10], refs[10:13]
+    held, sems = refs[13:18], refs[18]
+    g_ref, prob_ref, slot_ref, count_ref, w_ref = held
+    copies = load_all(list(zip(sources, held)), sems)
     square = jnp.zeros((TOK, CH), jnp.float32)
     for ref, k, j in gathered_blocks(x_ref, parts):
         m = ref[k, 0:TOK, :].astype(jnp.float32)
@@ -96,8 +129,10 @@
         square = square + m * m
         xn_ref[:, pl.ds(pl.multiple_of(j * CH, CH), CH)] = (m * gain).astype(jnp.bfloat16)
     inv = lax.rsqrt(jnp.sum(square, axis=1, keepdims=True) / D + EPS)
+    for copy in copies:
+        copy.wait()
     both = jnp.dot(xn_ref[...], w_ref[...], preferred_element_type=jnp.float32)
-    first = (count_ref[0, 0] + BLOCK - 1) // BLOCK * BLOCK
+    first = (count_ref[0:1, 0:1] + BLOCK - 1) // BLOCK * BLOCK
     slots = slot_ref.shape[1]
     tok = lax.broadcasted_iota(jnp.int32, (TOK, slots), 0)
     place = lax.broadcasted_iota(jnp.int32, (TOK, slots), 1)
@@ -116,18 +151,25 @@
 
 def weight_kernel(x_ref, *refs):
     parts = refs[:5]
-    gm_ref, out_ref, xt_ref = refs[5:]
+    gm_hbm, out_ref, xt_ref, gm_ref, sems = refs[5:]
+    copies = load_all([(gm_hbm, gm_ref)], sems)
     for ref, k, j in gathered_blocks(x_ref, parts):
         half = lax.rem(j, 2)
         i = lax.div(j, 2)
         xt_ref[
             pl.ds(pl.multiple_of(half * CH, CH), CH), pl.ds(pl.multiple_of(i * TOK, TOK), TOK)
         ] = ref[k]
+    for copy in copies:
+        copy.wait()
     out_ref[...] = jnp.dot(xt_ref[...], gm_ref[...], preferred_element_type=jnp.float32)
 
 
 def vm(n):
     return [pl.BlockSpec(memory_space=pltpu.VMEM)] * n
+
+
+def hbm(n):
+    return [pl.BlockSpec(memory_space=pltpu.HBM)] * n
 
 
 def sm(n):
@@ -147,51 +189,84 @@
     grad_out,
 ):
     params = pltpu.CompilerParams(vmem_limit_bytes=VMEM_LIMIT)
+    full = pltpu.CompilerParams(vmem_limit_bytes=56 * 1024 * 1024)
     bf, f32 = jnp.bfloat16, jnp.float32
+    halo = pl.pallas_call(
+        pack_kernel,
+        out_shape=jax.ShapeDtypeStruct((3, 16, CH), bf),
+        in_specs=hbm(3),
+        out_specs=vm(1)[0],
+        scratch_shapes=[pltpu.SemaphoreType.DMA((3,))],
+        compiler_params=full,
+    )(stream_q, stream_k, stream_v)
+    halo, w_proj = lax.optimization_barrier((halo, w_proj))
     w_all = lax.all_gather(w_proj.reshape(TOK, 2 * HID), "dp", axis=0, tiled=True)
-    last = jnp.stack([stream_q[-2:], stream_k[-2:], stream_v[-2:]])
-    halo = lax.ppermute(last, "dp", [(s, s + 1) for s in range(2 * NY - 1)])
+    halo = lax.ppermute(halo, "dp", [(s, s + 1) for s in range(2 * NY - 1)])
     x1, x2 = pl.pallas_call(
         mix_kernel,
         out_shape=(
             jax.ShapeDtypeStruct((NZ, ROWS, CH), bf),
             jax.ShapeDtypeStruct((CH, TOK), bf),
         ),
-        in_specs=vm(6),
+        in_specs=hbm(5) + vm(1),
         out_specs=tuple(vm(2)),
-        compiler_params=params,
-    )(stream_q, stream_k, stream_v, halo, conv_taps, norm_gain.reshape(1, CH))
+        scratch_shapes=[
+            pltpu.VMEM((TOK, CH), bf),
+            pltpu.VMEM((TOK, CH), bf),
+            pltpu.VMEM((TOK, CH), bf),
+            pltpu.VMEM((3, 3, CH), f32),
+            pltpu.VMEM((1, CH), bf),
+            pltpu.SemaphoreType.DMA((5,)),
+        ],
+        compiler_params=full,
+    )(stream_q, stream_k, stream_v, conv_taps, norm_gain.reshape(1, CH), halo)
     x_pos = lax.rem(lax.axis_index("expert"), NX).astype(jnp.int32).reshape(1)
-    x1_parts = gather_expert(x1)
+    x2 = to_row_block(x2)
+    x1 = spread_z(x1)
+    x1, x2 = lax.optimization_barrier((x1, x2))
+    x1_parts = spread_x(x1)
+    x2 = spread_z(jnp.broadcast_to(x2[None], (NZ, CH, TOK)))
+    x1_parts, x2 = lax.optimization_barrier((x1_parts, x2))
     activation, gm = pl.pallas_call(
         forward_kernel,
         out_shape=(
             jax.ShapeDtypeStruct((TOK, HID), bf),
             jax.ShapeDtypeStruct((TOK, 2 * HID), bf),
         ),
-        in_specs=sm(2) + vm(9),
+        in_specs=sm(1) + vm(5) + hbm(5),
         out_specs=tuple(vm(2)),
-        scratch_shapes=[pltpu.VMEM((TOK, D), bf)],
+        scratch_shapes=[
+            pltpu.VMEM((TOK, D), bf),
+            pltpu.VMEM((TOK, HID), bf),
+            pltpu.VMEM((1, TOK), f32),
+            pltpu.VMEM((1, 384), jnp.int32),
+            pltpu.VMEM((1, 2), jnp.int32),
+            pltpu.VMEM((D, 2 * HID), bf),
+            pltpu.SemaphoreType.DMA((5,)),
+        ],
         compiler_params=params,
     )(
         x_pos,
-        expert_count,
         *x1_parts,
-        w_all,
         grad_out,
         route_prob.reshape(1, TOK),
         slot_token,
+        expert_count,
+        w_all,
     )
     gm_all = lax.all_gather(gm, "dp", axis=0, tiled=True)
-    x2 = to_row_block(x2)
     x2, _ = lax.optimization_barrier((x2, gm))
-    x2_parts = gather_expert(jnp.broadcast_to(x2[None], (NZ, CH, TOK)))
+    x2_parts = spread_x(x2)
     grad_w = pl.pallas_call(
         weight_kernel,
         out_shape=jax.ShapeDtypeStruct((TOK, 2 * HID), f32),
-        in_specs=sm(1) + vm(6),
-        out_specs=pl.BlockSpec(memory_space=pltpu.VMEM),
-        scratch_shapes=[pltpu.VMEM((2 * CH, D), bf)],
+        in_specs=sm(1) + vm(5) + hbm(1),
+        out_specs=vm(1)[0],
+        scratch_shapes=[
+            pltpu.VMEM((2 * CH, D), bf),
+            pltpu.VMEM((D, 2 * HID), bf),
+            pltpu.SemaphoreType.DMA((1,)),
+        ],
         compiler_params=params,
     )(x_pos, *x2_parts, gm_all)
     return activation, grad_w.reshape(TOK, 2, HID)

time: 163 us -> 150 us (0.920)
  blocking collectives: 52.1 us -> 0 us
  waiting for transfers between devices: 40.6 us -> 71.7 us
  starting transfers between devices: 34.3 us -> 46.3 us
  local copies, waits for them, and re-layouts: 11.1 us -> 4.33 us
  Pallas kernels: 8.64 us -> 12.7 us
    all_to_all x2 -> x0, blocking collectives: 52.1 us -> none  [gather_expert(): lax.all_to_all(copies.reshape(n * r, c), 'expert', 0, 0, axis_index_group...]
    all_gather x1, waiting for transfers between devices: 0.01 us -> 16.6 us  [on_device(): gm_all = lax.all_gather(gm, 'dp', axis=0, tiled=True)]
    all_to_all x0 -> x2, starting transfers between devices: none -> 13.4 us  [spread_z(): lax.all_to_all(copies.reshape(n * r, c), 'expert', 0, 0, axis_index_group...]
    all_to_all x0 -> x2, waiting for transfers between devices: none -> 10.5 us  [spread_z(): lax.all_to_all(copies.reshape(n * r, c), 'expert', 0, 0, axis_index_group...]
    unnamed x19 -> x11, local copies, waits for them, and re-layouts: 8.46 us -> 2.31 us
    pallas_call x1, Pallas kernels: 0.23 us -> 2.65 us  [on_device(): pl.pallas_call(mix_kernel, out_shape=(jax.ShapeDtypeStruct((NZ, ROWS, CH)...]
    ppermute x8, waiting for transfers between devices: 33.8 us -> 36 us  [shift_x(): return lax.ppermute(value, AXES, pairs)]
  transfers between devices with their start and end apart: 12 -> 14, of which waited for: 6 -> 9; matrix products, arithmetic and copies ran while one was open for 1% -> 1% of each run, Pallas kernels for 0% -> 2%
where the time goes in v2:
time: 150 us; the launch traced here: 149 us
  waiting for transfers between devices  71.7 us (48%)
  starting transfers between devices  46.3 us (31%)
  between operations  14.2 us (9%)
  Pallas kernels  12.7 us (8%)
  local copies, waits for them, and re-layouts  4.33 us (3%)
    ppermute x8, waiting for transfers between devices, shift_x(): return lax.ppermute(value, AXES, pairs)  36 us
    ppermute x8, starting transfers between devices, shift_x(): return lax.ppermute(value, AXES, pairs)  24.8 us
    all_gather x1, waiting for transfers between devices, on_device(): gm_all = lax.all_gather(gm, 'dp', axis=0, tiled=True)  16.6 us
    all_to_all x2, starting transfers between devices, spread_z(): lax.all_to_all(copies.reshape(n * r, c), 'expert', 0, 0, axis_index_group...  13.4 us
    all_to_all x2, waiting for transfers between devices, spread_z(): lax.all_to_all(copies.reshape(n * r, c), 'expert', 0, 0, axis_index_group...  10.5 us
    pallas_call x1, Pallas kernels, on_device(): pl.pallas_call(forward_kernel, out_shape=(jax.ShapeDtypeStruct((TOK, HID)...  5.18 us
    ppermute x1, starting transfers between devices, on_device(): halo = lax.ppermute(halo, 'dp', [(s, s + 1) for s in range(2 * NY - 1)])  4.59 us
    ppermute x1, waiting for transfers between devices, on_device(): halo = lax.ppermute(halo, 'dp', [(s, s + 1) for s in range(2 * NY - 1)])  4.43 us
  transfers between devices with their start and end apart: 14, of which 9 were waited for; matrix products, arithmetic and copies ran while one was open for 1% of the time, Pallas kernels for 2%

profile of v2, /device:TPU:1, one launch (start us, length us, event | category | flops | bytes accessed | tf_op | source)
XLA Modules:
  0.0 149.3 jit_solution(7465199455659134301)
XLA Ops:
  7.2 0.0 copy-start
  7.2 0.0 copy-start.2
  7.2 0.0 copy-start.3
  7.2 0.0 copy-start.1
  7.2 0.0 all-gather.3.cloned.1.call-start
  7.2 1.4 shard_map.113
  8.6 1.7 %copy.12 = bf16[32,8,2,256]{3,1,2,0:T(8,128)(2,1)} copy(bf16[32,8,2,256]{3,2,1,0:T(2,128)(2,1)} %bitcast.7) | data formatting | bytes 524288
  10.3 0.0 all-gather.3.cloned.1.call-update
  10.3 4.6 %collective-permute-start = (bf16[3,16,128]{2,1,0:T(8,128)(2,1)}, bf16[3,16,128]{2,1,0:T(8,128)(2,1)S(1)}, u32[]{:S(2)}, u32[]{:S(2)}) collective-permute-start(bf16[3,16,128]{2,1,0:T(8,128)(2,1)} %shard_map.113), channel_id=1, source_target_pairs={{0,32},{32,64},{64,96},{96,128},{128,160},{160,192},{192,224},{224... | collective-permute-start | bytes 36872 | tf_op jit(solution)/shard_map/ppermute | solution.py:204
  14.9 4.4 %collective-permute-done.halo_ref = bf16[3,16,128]{2,1,0:T(8,128)(2,1)S(1)} collective-permute-done((bf16[3,16,128]{2,1,0:T(8,128)(2,1)}, bf16[3,16,128]{2,1,0:T(8,128)(2,1)S(1)}, u32[]{:S(2)}, u32[]{:S(2)}) %collective-permute-start) | collective-permute-done | bytes 12320 | tf_op jit(solution)/shard_map/ppermute | solution.py:204
  19.4 0.0 copy-start.4
  19.4 0.6 copy-done.4
  20.0 2.7 %shard_map.114 = (bf16[8,272,128]{2,1,0:T(8,128)(2,1)}, bf16[128,256]{1,0:T(8,128)(2,1)}) custom-call(bf16[256,128]{1,0:T(8,128)(2,1)} %q_hbm.1, bf16[256,128]{1,0:T(8,128)(2,1)} %k_hbm.1, bf16[256,128]{1,0:T(8,128)(2,1)} %v_hbm.1, f32[3,3,128]{2,1,0:T(4,128)} %taps_hbm.1, bf16[1,128]{1,0:T(2,128)(2,1)} %bitcast.8, bf16[3,16,128]{2,1,0:T(8,128)(2,1)} %copy-done.4), custom_call_target="tpu_custom_call" | custom-call | tf_op jit(solution)/shard_map/pallas_call | solution.py:205
  22.6 6.6 %all-to-all-start = ((bf16[8,272,128]{2,1,0:T(8,128)(2,1)}), bf16[8,272,128]{2,1,0:T(8,128)(2,1)S(1)}, u32[]{:S(2)}, u32[]{:S(2)}) async-start(bf16[8,272,128]{2,1,0:T(8,128)(2,1)} %get-tuple-element.18), calls=%async_computation | async-start | bytes 1114112 | tf_op jit(solution)/shard_map/all_to_all | solution.py:42
  29.3 3.5 %collective-permute-start.1 = (bf16[128,256]{1,0:T(8,128)(2,1)}, bf16[128,256]{1,0:T(8,128)(2,1)S(1)}, u32[]{:S(2)}, u32[]{:S(2)}) collective-permute-start(bf16[128,256]{1,0:T(8,128)(2,1)} %get-tuple-element.19), channel_id=1, source_target_pairs={{0,0},{1,1},{2,32},{3,33},{4,64},{5,65},{6,96},{7,97},{8,128},{9,1... | collective-permute-start | bytes 196616 | tf_op jit(solution)/shard_map/ppermute | solution.py:37
  32.7 4.1 %collective-permute-done.1 = bf16[128,256]{1,0:T(8,128)(2,1)S(1)} collective-permute-done((bf16[128,256]{1,0:T(8,128)(2,1)}, bf16[128,256]{1,0:T(8,128)(2,1)S(1)}, u32[]{:S(2)}, u32[]{:S(2)}) %collective-permute-start.1) | collective-permute-done | bytes 65568 | tf_op jit(solution)/shard_map/ppermute | solution.py:37
  36.9 10.5 %all-to-all-done.refs_0_ = bf16[8,272,128]{2,1,0:T(8,128)(2,1)S(1)} async-done(((bf16[8,272,128]{2,1,0:T(8,128)(2,1)}), bf16[8,272,128]{2,1,0:T(8,128)(2,1)S(1)}, u32[]{:S(2)}, u32[]{:S(2)}) %all-to-all-start) | async-done | bytes 557088 | tf_op jit(solution)/shard_map/all_to_all | solution.py:42
  47.4 0.8 broadcast_in_dim.2
  48.2 6.7 %all-to-all-start.1 = ((bf16[8,128,256]{2,1,0:T(8,128)(2,1)}), bf16[8,128,256]{2,1,0:T(8,128)(2,1)S(1)}, u32[]{:S(2)}, u32[]{:S(2)}) async-start(bf16[8,128,256]{2,1,0:T(8,128)(2,1)} %broadcast_in_dim.2), calls=%async_computation.1 | async-start | bytes 1048576 | tf_op jit(solution)/shard_map/all_to_all | solution.py:42
  54.9 0.0 all-gather.5.cloned.1.call-start
  55.0 4.1 %collective-permute-start.3 = (bf16[8,272,128]{2,1,0:T(8,128)(2,1)S(1)}, bf16[8,272,128]{2,1,0:T(8,128)(2,1)S(1)}, u32[]{:S(2)}, u32[]{:S(2)}) collective-permute-start(bf16[8,272,128]{2,1,0:T(8,128)(2,1)S(1)} %all-to-all-done.refs_0_), channel_id=1, source_target_pairs={{0,3},{1,0},{2,1},{3,2},{4,7},{5,4},{6,5},{7,6},{8,11},{9,8},{10,9... | collective-permute-start | bytes 1671176 | tf_op jit(solution)/shard_map/ppermute | solution.py:28
  59.0 1.9 %collective-permute-start.2 = (bf16[8,272,128]{2,1,0:T(8,128)(2,1)S(1)}, bf16[8,272,128]{2,1,0:T(8,128)(2,1)S(1)}, u32[]{:S(2)}, u32[]{:S(2)}) collective-permute-start(bf16[8,272,128]{2,1,0:T(8,128)(2,1)S(1)} %all-to-all-done.refs_0_), channel_id=1, source_target_pairs={{0,1},{1,2},{2,3},{3,0},{4,5},{5,6},{6,7},{7,4},{8,9},{9,10},{10,1... | collective-permute-start | bytes 1671176 | tf_op jit(solution)/shard_map/ppermute | solution.py:28
  61.0 3.6 %collective-permute-start.5 = (bf16[4,272,128]{2,1,0:T(8,128)(2,1)S(1)}, bf16[4,272,128]{2,1,0:T(8,128)(2,1)S(1)}, u32[]{:S(2)}, u32[]{:S(2)}) collective-permute-start(bf16[4,272,128]{2,1,0:T(8,128)(2,1)S(1)} %get-tuple-element.32), channel_id=1, source_target_pairs={{0,2},{1,3},{2,0},{3,1},{4,6},{5,7},{6,4},{7,5},{8,10},{9,11},{10,... | collective-permute-start | bytes 835592 | tf_op jit(solution)/shard_map/ppermute | solution.py:28
  64.7 3.2 %collective-permute-start.4 = (bf16[4,272,128]{2,1,0:T(8,128)(2,1)S(1)}, bf16[4,272,128]{2,1,0:T(8,128)(2,1)S(1)}, u32[]{:S(2)}, u32[]{:S(2)}) collective-permute-start(bf16[4,272,128]{2,1,0:T(8,128)(2,1)S(1)} %get-tuple-element.33), channel_id=1, source_target_pairs={{0,2},{1,3},{2,0},{3,1},{4,6},{5,7},{6,4},{7,5},{8,10},{9,11},{10,... | collective-permute-start | bytes 835592 | tf_op jit(solution)/shard_map/ppermute | solution.py:28
  67.8 13.2 %collective-permute-done.5.refs_4_ = bf16[4,272,128]{2,1,0:T(8,128)(2,1)S(1)} collective-permute-done((bf16[4,272,128]{2,1,0:T(8,128)(2,1)S(1)}, bf16[4,272,128]{2,1,0:T(8,128)(2,1)S(1)}, u32[]{:S(2)}, u32[]{:S(2)}) %collective-permute-start.5) | collective-permute-done | bytes 278560 | tf_op jit(solution)/shard_map/ppermute | solution.py:28
  81.1 6.0 %collective-permute-done.4.refs_3_ = bf16[4,272,128]{2,1,0:T(8,128)(2,1)S(1)} collective-permute-done((bf16[4,272,128]{2,1,0:T(8,128)(2,1)S(1)}, bf16[4,272,128]{2,1,0:T(8,128)(2,1)S(1)}, u32[]{:S(2)}, u32[]{:S(2)}) %collective-permute-start.4) | collective-permute-done | bytes 278560 | tf_op jit(solution)/shard_map/ppermute | solution.py:28
  87.0 0.0 collective-permute-done.3.refs_2_
  87.0 0.9 collective-permute-done.2.refs_1_
  87.9 0.0 all-to-all-done.1.refs_0_
  87.9 0.0 all-gather.3.cloned.1.call-done.refs_9_
  87.9 0.0 copy-done
  87.9 0.0 copy-done.2
  88.0 0.0 copy-done.3
  88.0 0.0 copy-done.1
  88.0 5.2 %shard_map.115 = (bf16[256,256]{1,0:T(8,128)(2,1)}, bf16[256,512]{1,0:T(8,128)(2,1)}) custom-call(s32[1]{0:T(128)} %bitcast.x_ref, bf16[8,272,128]{2,1,0:T(8,128)(2,1)S(1)} %all-to-all-done.refs_0_, bf16[8,272,128]{2,1,0:T(8,128)(2,1)S(1)} %collective-permute-done.2.refs_1_, bf16[8,272,128]{2,1,0:T(8,128)(2,1)S(1)} %collective-permute-done.3.refs_2_, ...), custom_call_target="tpu_custom_call" | custom-call | tf_op jit(solution)/shard_map/pallas_call | solution.py:230
  93.2 0.0 all-gather.5.cloned.1.call-update
  93.2 1.9 %collective-permute-start.7 = (bf16[8,128,256]{2,1,0:T(8,128)(2,1)S(1)}, bf16[8,128,256]{2,1,0:T(8,128)(2,1)S(1)}, u32[]{:S(2)}, u32[]{:S(2)}) collective-permute-start(bf16[8,128,256]{2,1,0:T(8,128)(2,1)S(1)} %all-to-all-done.1.refs_0_), channel_id=1, source_target_pairs={{0,3},{1,0},{2,1},{3,2},{4,7},{5,4},{6,5},{7,6},{8,11},{9,8},{10,9... | collective-permute-start | bytes 1572872 | tf_op jit(solution)/shard_map/ppermute | solution.py:28
  95.1 3.4 %collective-permute-start.6 = (bf16[8,128,256]{2,1,0:T(8,128)(2,1)S(1)}, bf16[8,128,256]{2,1,0:T(8,128)(2,1)S(1)}, u32[]{:S(2)}, u32[]{:S(2)}) collective-permute-start(bf16[8,128,256]{2,1,0:T(8,128)(2,1)S(1)} %all-to-all-done.1.refs_0_), channel_id=1, source_target_pairs={{0,1},{1,2},{2,3},{3,0},{4,5},{5,6},{6,7},{7,4},{8,9},{9,10},{10,1... | collective-permute-start | bytes 1572872 | tf_op jit(solution)/shard_map/ppermute | solution.py:28
  98.5 2.6 %collective-permute-start.9 = (bf16[4,128,256]{2,1,0:T(8,128)(2,1)S(1)}, bf16[4,128,256]{2,1,0:T(8,128)(2,1)S(1)}, u32[]{:S(2)}, u32[]{:S(2)}) collective-permute-start(bf16[4,128,256]{2,1,0:T(8,128)(2,1)S(1)} %get-tuple-element.34), channel_id=1, source_target_pairs={{0,2},{1,3},{2,0},{3,1},{4,6},{5,7},{6,4},{7,5},{8,10},{9,11},{10,... | collective-permute-start | bytes 786440 | tf_op jit(solution)/shard_map/ppermute | solution.py:28
  101.1 4.2 %collective-permute-start.8 = (bf16[4,128,256]{2,1,0:T(8,128)(2,1)S(1)}, bf16[4,128,256]{2,1,0:T(8,128)(2,1)S(1)}, u32[]{:S(2)}, u32[]{:S(2)}) collective-permute-start(bf16[4,128,256]{2,1,0:T(8,128)(2,1)S(1)} %get-tuple-element.35), channel_id=1, source_target_pairs={{0,2},{1,3},{2,0},{3,1},{4,6},{5,7},{6,4},{7,5},{8,10},{9,11},{10,... | collective-permute-start | bytes 786440 | tf_op jit(solution)/shard_map/ppermute | solution.py:28
  105.3 10.3 %collective-permute-done.9.refs_4_ = bf16[4,128,256]{2,1,0:T(8,128)(2,1)S(1)} collective-permute-done((bf16[4,128,256]{2,1,0:T(8,128)(2,1)S(1)}, bf16[4,128,256]{2,1,0:T(8,128)(2,1)S(1)}, u32[]{:S(2)}, u32[]{:S(2)}) %collective-permute-start.9) | collective-permute-done | bytes 262176 | tf_op jit(solution)/shard_map/ppermute | solution.py:28
  115.6 5.6 %collective-permute-done.8.refs_3_ = bf16[4,128,256]{2,1,0:T(8,128)(2,1)S(1)} collective-permute-done((bf16[4,128,256]{2,1,0:T(8,128)(2,1)S(1)}, bf16[4,128,256]{2,1,0:T(8,128)(2,1)S(1)}, u32[]{:S(2)}, u32[]{:S(2)}) %collective-permute-start.8) | collective-permute-done | bytes 262176 | tf_op jit(solution)/shard_map/ppermute | solution.py:28
  121.2 0.0 collective-permute-done.7.refs_2_
  121.2 0.0 collective-permute-done.6.refs_1_
  121.2 16.6 %all-gather.5.cloned.1.call-done.refs_5_ = bf16[4096,512]{1,0:T(8,128)(2,1)} async-done(((bf16[256,512]{1,0:T(8,128)(2,1)}), bf16[4096,512]{1,0:T(8,128)(2,1)}) %all-gather.5.cloned.1.call-update) | async-done | bytes 4194320 | tf_op jit(solution)/shard_map/all_gather | solution.py:257
  137.8 3.5 %shard_map.116 = f32[256,512]{1,0:T(8,128)S(1)} custom-call(s32[1]{0:T(128)} %bitcast.x_ref, bf16[8,128,256]{2,1,0:T(8,128)(2,1)S(1)} %all-to-all-done.1.refs_0_, bf16[8,128,256]{2,1,0:T(8,128)(2,1)S(1)} %collective-permute-done.6.refs_1_, bf16[8,128,256]{2,1,0:T(8,128)(2,1)S(1)} %collective-permute-done.7.refs_2_, ...), custom_call_target="tpu_custom_call" | custom-call | tf_op jit(solution)/shard_map/pallas_call | solution.py:260
  141.4 1.1 reshape.36
  (2 shorter events, 0.1 us)
Async XLA Ops:
  7.2 80.8 %copy-start = (bf16[256,256]{1,0:T(8,128)(2,1)S(1)}, bf16[256,256]{1,0:T(8,128)(2,1)}, u32[]{:S(2)}) copy-start(bf16[256,256]{1,0:T(8,128)(2,1)} %refs_5_.1) | copy-start | bytes 393220
  7.2 80.8 %copy-start.2 = (f32[256]{0:T(256)S(1)}, f32[256]{0:T(256)}, u32[]{:S(2)}) copy-start(f32[256]{0:T(256)} %param.17) | copy-start | bytes 3076
  7.2 80.8 %copy-start.3 = (s32[1,2]{1,0:T(1,128)S(1)}, s32[1,2]{1,0:T(1,128)}, u32[]{:S(2)}) copy-start(s32[1,2]{1,0:T(1,128)} %refs_8_.1) | copy-start | bytes 28
  7.2 80.8 %copy-start.1 = (s32[1,384]{1,0:T(1,128)S(1)}, s32[1,384]{1,0:T(1,128)}, u32[]{:S(2)}) copy-start(s32[1,384]{1,0:T(1,128)} %refs_7_.1) | copy-start | bytes 4612
  7.2 80.7 %all-gather.3.cloned.1.call-start = ((), (), s32[]{:S(2)}) async-start(), calls=%async_computation.2 | async-start | bytes 4456448 | tf_op jit(solution)/shard_map/all_gather | solution.py:203
  10.3 9.0 %collective-permute-start = (bf16[3,16,128]{2,1,0:T(8,128)(2,1)}, bf16[3,16,128]{2,1,0:T(8,128)(2,1)S(1)}, u32[]{:S(2)}, u32[]{:S(2)}) collective-permute-start(bf16[3,16,128]{2,1,0:T(8,128)(2,1)} %shard_map.113), channel_id=1, source_target_pairs={{0,32},{32,64},{64,96},{96,128},{128,160},{160,192},{192,224},{224... | collective-permute-start | bytes 36872 | tf_op jit(solution)/shard_map/ppermute | solution.py:204
  19.4 0.6 copy-start.4
  22.6 24.7 %all-to-all-start = ((bf16[8,272,128]{2,1,0:T(8,128)(2,1)}), bf16[8,272,128]{2,1,0:T(8,128)(2,1)S(1)}, u32[]{:S(2)}, u32[]{:S(2)}) async-start(bf16[8,272,128]{2,1,0:T(8,128)(2,1)} %get-tuple-element.18), calls=%async_computation | async-start | bytes 1114112 | tf_op jit(solution)/shard_map/all_to_all | solution.py:42
  29.3 7.6 %collective-permute-start.1 = (bf16[128,256]{1,0:T(8,128)(2,1)}, bf16[128,256]{1,0:T(8,128)(2,1)S(1)}, u32[]{:S(2)}, u32[]{:S(2)}) collective-permute-start(bf16[128,256]{1,0:T(8,128)(2,1)} %get-tuple-element.19), channel_id=1, source_target_pairs={{0,0},{1,1},{2,32},{3,33},{4,64},{5,65},{6,96},{7,97},{8,128},{9,1... | collective-permute-start | bytes 196616 | tf_op jit(solution)/shard_map/ppermute | solution.py:37
  48.2 39.7 %all-to-all-start.1 = ((bf16[8,128,256]{2,1,0:T(8,128)(2,1)}), bf16[8,128,256]{2,1,0:T(8,128)(2,1)S(1)}, u32[]{:S(2)}, u32[]{:S(2)}) async-start(bf16[8,128,256]{2,1,0:T(8,128)(2,1)} %broadcast_in_dim.2), calls=%async_computation.1 | async-start | bytes 1048576 | tf_op jit(solution)/shard_map/all_to_all | solution.py:42
  54.9 82.9 %all-gather.5.cloned.1.call-start = ((), (), s32[]{:S(2)}) async-start(), calls=%async_computation.3 | async-start | bytes 4456448 | tf_op jit(solution)/shard_map/all_gather | solution.py:257
  55.0 32.1 %collective-permute-start.3 = (bf16[8,272,128]{2,1,0:T(8,128)(2,1)S(1)}, bf16[8,272,128]{2,1,0:T(8,128)(2,1)S(1)}, u32[]{:S(2)}, u32[]{:S(2)}) collective-permute-start(bf16[8,272,128]{2,1,0:T(8,128)(2,1)S(1)} %all-to-all-done.refs_0_), channel_id=1, source_target_pairs={{0,3},{1,0},{2,1},{3,2},{4,7},{5,4},{6,5},{7,6},{8,11},{9,8},{10,9... | collective-permute-start | bytes 1671176 | tf_op jit(solution)/shard_map/ppermute | solution.py:28
  59.0 28.9 %collective-permute-start.2 = (bf16[8,272,128]{2,1,0:T(8,128)(2,1)S(1)}, bf16[8,272,128]{2,1,0:T(8,128)(2,1)S(1)}, u32[]{:S(2)}, u32[]{:S(2)}) collective-permute-start(bf16[8,272,128]{2,1,0:T(8,128)(2,1)S(1)} %all-to-all-done.refs_0_), channel_id=1, source_target_pairs={{0,1},{1,2},{2,3},{3,0},{4,5},{5,6},{6,7},{7,4},{8,9},{9,10},{10,1... | collective-permute-start | bytes 1671176 | tf_op jit(solution)/shard_map/ppermute | solution.py:28
  61.0 20.0 %collective-permute-start.5 = (bf16[4,272,128]{2,1,0:T(8,128)(2,1)S(1)}, bf16[4,272,128]{2,1,0:T(8,128)(2,1)S(1)}, u32[]{:S(2)}, u32[]{:S(2)}) collective-permute-start(bf16[4,272,128]{2,1,0:T(8,128)(2,1)S(1)} %get-tuple-element.32), channel_id=1, source_target_pairs={{0,2},{1,3},{2,0},{3,1},{4,6},{5,7},{6,4},{7,5},{8,10},{9,11},{10,... | collective-permute-start | bytes 835592 | tf_op jit(solution)/shard_map/ppermute | solution.py:28
  64.7 22.4 %collective-permute-start.4 = (bf16[4,272,128]{2,1,0:T(8,128)(2,1)S(1)}, bf16[4,272,128]{2,1,0:T(8,128)(2,1)S(1)}, u32[]{:S(2)}, u32[]{:S(2)}) collective-permute-start(bf16[4,272,128]{2,1,0:T(8,128)(2,1)S(1)} %get-tuple-element.33), channel_id=1, source_target_pairs={{0,2},{1,3},{2,0},{3,1},{4,6},{5,7},{6,4},{7,5},{8,10},{9,11},{10,... | collective-permute-start | bytes 835592 | tf_op jit(solution)/shard_map/ppermute | solution.py:28
  93.2 28.0 %collective-permute-start.7 = (bf16[8,128,256]{2,1,0:T(8,128)(2,1)S(1)}, bf16[8,128,256]{2,1,0:T(8,128)(2,1)S(1)}, u32[]{:S(2)}, u32[]{:S(2)}) collective-permute-start(bf16[8,128,256]{2,1,0:T(8,128)(2,1)S(1)} %all-to-all-done.1.refs_0_), channel_id=1, source_target_pairs={{0,3},{1,0},{2,1},{3,2},{4,7},{5,4},{6,5},{7,6},{8,11},{9,8},{10,9... | collective-permute-start | bytes 1572872 | tf_op jit(solution)/shard_map/ppermute | solution.py:28
  95.1 26.1 %collective-permute-start.6 = (bf16[8,128,256]{2,1,0:T(8,128)(2,1)S(1)}, bf16[8,128,256]{2,1,0:T(8,128)(2,1)S(1)}, u32[]{:S(2)}, u32[]{:S(2)}) collective-permute-start(bf16[8,128,256]{2,1,0:T(8,128)(2,1)S(1)} %all-to-all-done.1.refs_0_), channel_id=1, source_target_pairs={{0,1},{1,2},{2,3},{3,0},{4,5},{5,6},{6,7},{7,4},{8,9},{9,10},{10,1... | collective-permute-start | bytes 1572872 | tf_op jit(solution)/shard_map/ppermute | solution.py:28
  98.5 17.1 %collective-permute-start.9 = (bf16[4,128,256]{2,1,0:T(8,128)(2,1)S(1)}, bf16[4,128,256]{2,1,0:T(8,128)(2,1)S(1)}, u32[]{:S(2)}, u32[]{:S(2)}) collective-permute-start(bf16[4,128,256]{2,1,0:T(8,128)(2,1)S(1)} %get-tuple-element.34), channel_id=1, source_target_pairs={{0,2},{1,3},{2,0},{3,1},{4,6},{5,7},{6,4},{7,5},{8,10},{9,11},{10,... | collective-permute-start | bytes 786440 | tf_op jit(solution)/shard_map/ppermute | solution.py:28
  101.1 20.1 %collective-permute-start.8 = (bf16[4,128,256]{2,1,0:T(8,128)(2,1)S(1)}, bf16[4,128,256]{2,1,0:T(8,128)(2,1)S(1)}, u32[]{:S(2)}, u32[]{:S(2)}) collective-permute-start(bf16[4,128,256]{2,1,0:T(8,128)(2,1)S(1)} %get-tuple-element.35), channel_id=1, source_target_pairs={{0,2},{1,3},{2,0},{3,1},{4,6},{5,7},{6,4},{7,5},{8,10},{9,11},{10,... | collective-permute-start | bytes 786440 | tf_op jit(solution)/shard_map/ppermute | solution.py:28
Sparse Core Ops, SparseCore 0:
  10.5 55.0 all-gather.2
  93.3 44.4 all-gather.4

commit v3 on v2

--- a/solution.py
+++ b/solution.py
@@ -13,8 +13,10 @@
 NZ, NX, NY = 8, 4, 8
 TOK, CH, HID = 256, 128, 256
 ROWS = TOK + 16
+CROWS = CH + 16
 VMEM_LIMIT = 48 * 1024 * 1024
 AXES = ("dp", "expert")
+Y_GROUPS = [[y * 2 + c for y in range(NY)] for c in range(2)]
 Z_GROUPS = [[z * NX + x for z in range(NZ)] for x in range(NX)]
 
 
@@ -28,6 +30,11 @@
     return lax.ppermute(value, AXES, pairs)
 
 
+def other_core(value):
+    pairs = [(n, (n // (NZ * NX) ^ 1) * NZ * NX + n % (NZ * NX)) for n in range(2 * NY * NZ * NX)]
+    return lax.ppermute(value, AXES, pairs)
+
+
 def to_row_block(value):
     pairs = [
         (i * NZ * NX + j, (j // 2) * NZ * NX + 2 * i + j % 2)
@@ -37,11 +44,15 @@
     return lax.ppermute(value, AXES, pairs)
 
 
-def spread_z(copies):
+def spread(copies, axis, groups):
     n, r, c = copies.shape
     return lax.all_to_all(
-        copies.reshape(n * r, c), "expert", 0, 0, axis_index_groups=Z_GROUPS, tiled=True
+        copies.reshape(n * r, c), axis, 0, 0, axis_index_groups=groups, tiled=True
     ).reshape(n, r, c)
+
+
+def spread_z(copies):
+    return spread(copies, "expert", Z_GROUPS)
 
 
 def spread_x(b):
@@ -79,9 +90,24 @@
         copy.wait()
 
 
+def in_second(slot_ref, count_ref):
+    first = (count_ref[0:1, 0:1] + BLOCK - 1) // BLOCK * BLOCK
+    slots = slot_ref.shape[1]
+    tok = lax.broadcasted_iota(jnp.int32, (TOK, slots), 0)
+    place = lax.broadcasted_iota(jnp.int32, (TOK, slots), 1)
+    hit = jnp.where((slot_ref[...] == tok) & (place >= first), 1.0, 0.0)
+    return jnp.sum(hit, axis=1, keepdims=True)
+
+
+def diagonal():
+    r = lax.broadcasted_iota(jnp.int32, (TOK, TOK), 0)
+    c = lax.broadcasted_iota(jnp.int32, (TOK, TOK), 1)
+    return r == c
+
+
 def mix_kernel(
-    q_hbm, k_hbm, v_hbm, taps_hbm, gain_hbm, halo_ref, x1_ref, x2_ref,
-    q_ref, k_ref, v_ref, taps_ref, gain_ref, sems,
+    q_hbm, k_hbm, v_hbm, taps_hbm, gain_hbm, slot_hbm, count_hbm, halo_ref, x1_ref, x2_ref,
+    q_ref, k_ref, v_ref, taps_ref, gain_ref, slot_ref, count_ref, sems,
 ):
     for copy in load_all(
         [
@@ -90,6 +116,8 @@
             (v_hbm, v_ref),
             (taps_hbm, taps_ref),
             (gain_hbm, gain_ref),
+            (slot_hbm, slot_ref),
+            (count_hbm, count_ref),
         ],
         sems,
     ):
@@ -113,13 +141,16 @@
         x1_ref[n, 0:TOK, :] = mixed
         x1_ref[n, TOK:ROWS, :] = tail
     scaled = mixed.astype(jnp.float32) * gain
-    x2_ref[...] = scaled.T.astype(jnp.bfloat16)
+    x2_ref[0:CH, :] = scaled.T.astype(jnp.bfloat16)
+    second = jnp.sum(
+        jnp.where(diagonal(), in_second(slot_ref, count_ref), 0.0), axis=0, keepdims=True
+    )
+    x2_ref[CH:CROWS, :] = jnp.broadcast_to(second, (16, TOK)).astype(jnp.bfloat16)
 
 
 def forward_kernel(x_ref, *refs):
     parts = refs[:5]
-    sources, (act_ref, gm_ref, xn_ref) = refs[5:10], refs[10:13]
-    held, sems = refs[13:18], refs[18]
+    sources, (act_ref, gm_ref, xn_ref), held, sems = refs[5:10], refs[10:13], refs[13:18], refs[18]
     g_ref, prob_ref, slot_ref, count_ref, w_ref = held
     copies = load_all(list(zip(sources, held)), sems)
     square = jnp.zeros((TOK, CH), jnp.float32)
@@ -132,36 +163,37 @@
     for copy in copies:
         copy.wait()
     both = jnp.dot(xn_ref[...], w_ref[...], preferred_element_type=jnp.float32)
-    first = (count_ref[0:1, 0:1] + BLOCK - 1) // BLOCK * BLOCK
-    slots = slot_ref.shape[1]
-    tok = lax.broadcasted_iota(jnp.int32, (TOK, slots), 0)
-    place = lax.broadcasted_iota(jnp.int32, (TOK, slots), 1)
-    hit = jnp.where((slot_ref[...] == tok) & (place >= first), 1.0, 0.0)
-    second = jnp.sum(hit, axis=1, keepdims=True) > 0.5
-    r = lax.broadcasted_iota(jnp.int32, (TOK, TOK), 0)
-    c = lax.broadcasted_iota(jnp.int32, (TOK, TOK), 1)
-    prob = jnp.sum(jnp.where(r == c, prob_ref[...], 0.0), axis=1, keepdims=True)
+    second = in_second(slot_ref, count_ref) > 0.5
+    prob = jnp.sum(jnp.where(diagonal(), prob_ref[...], 0.0), axis=1, keepdims=True)
     pre = jnp.where(second, both[:, HID:], both[:, :HID]) * inv
     sig = jax.nn.sigmoid(pre)
     act_ref[...] = (prob * pre * sig).astype(jnp.bfloat16)
     grad = g_ref[...].astype(jnp.float32) * prob * sig * (1.0 + pre * (1.0 - sig)) * inv
-    gm_ref[:, :HID] = jnp.where(second, 0.0, grad).astype(jnp.bfloat16)
-    gm_ref[:, HID:] = jnp.where(second, grad, 0.0).astype(jnp.bfloat16)
+    grad = grad.astype(jnp.bfloat16)
+    for n in range(NY):
+        gm_ref[n] = grad
 
 
 def weight_kernel(x_ref, *refs):
     parts = refs[:5]
-    gm_hbm, out_ref, xt_ref, gm_ref, sems = refs[5:]
-    copies = load_all([(gm_hbm, gm_ref)], sems)
+    mine_hbm, other_hbm, out_ref, xt_ref, gm_ref, sems = refs[5:]
+    copies = load_all([(mine_hbm, gm_ref.at[0]), (other_hbm, gm_ref.at[1])], sems)
     for ref, k, j in gathered_blocks(x_ref, parts):
-        half = lax.rem(j, 2)
         i = lax.div(j, 2)
-        xt_ref[
-            pl.ds(pl.multiple_of(half * CH, CH), CH), pl.ds(pl.multiple_of(i * TOK, TOK), TOK)
-        ] = ref[k]
+        place = jnp.where(lax.rem(i, 2) == x_ref[1], lax.div(i, 2), NY + lax.div(i, 2))
+        rows = pl.ds(pl.multiple_of(lax.rem(j, 2) * CH, CH), CH)
+        cols = pl.ds(pl.multiple_of(place * TOK, TOK), TOK)
+        second = ref[k, CH:CROWS, :].astype(jnp.float32)[0:1, :]
+        block = ref[k, 0:CH, :].astype(jnp.float32)
+        xt_ref[0, rows, cols] = (block * (1.0 - second)).astype(jnp.bfloat16)
+        xt_ref[1, rows, cols] = (block * second).astype(jnp.bfloat16)
     for copy in copies:
         copy.wait()
-    out_ref[...] = jnp.dot(xt_ref[...], gm_ref[...], preferred_element_type=jnp.float32)
+    grads = gm_ref[...].reshape(D, HID)
+    for e in range(2):
+        out_ref[:, e * HID : (e + 1) * HID] = jnp.dot(
+            xt_ref[e], grads, preferred_element_type=jnp.float32
+        )
 
 
 def vm(n):
@@ -206,9 +238,9 @@
         mix_kernel,
         out_shape=(
             jax.ShapeDtypeStruct((NZ, ROWS, CH), bf),
-            jax.ShapeDtypeStruct((CH, TOK), bf),
+            jax.ShapeDtypeStruct((CROWS, TOK), bf),
         ),
-        in_specs=hbm(5) + vm(1),
+        in_specs=hbm(7) + vm(1),
         out_specs=tuple(vm(2)),
         scratch_shapes=[
             pltpu.VMEM((TOK, CH), bf),
@@ -216,22 +248,25 @@
             pltpu.VMEM((TOK, CH), bf),
             pltpu.VMEM((3, 3, CH), f32),
             pltpu.VMEM((1, CH), bf),
-            pltpu.SemaphoreType.DMA((5,)),
+            pltpu.VMEM((1, 384), jnp.int32),
+            pltpu.VMEM((1, 2), jnp.int32),
+            pltpu.SemaphoreType.DMA((7,)),
         ],
         compiler_params=full,
-    )(stream_q, stream_k, stream_v, conv_taps, norm_gain.reshape(1, CH), halo)
-    x_pos = lax.rem(lax.axis_index("expert"), NX).astype(jnp.int32).reshape(1)
+    )(stream_q, stream_k, stream_v, conv_taps, norm_gain.reshape(1, CH), slot_token, expert_count, halo)
+    x_pos = jnp.stack([lax.rem(lax.axis_index("expert"), NX), lax.rem(lax.axis_index("dp"), 2)])
+    x_pos = x_pos.astype(jnp.int32)
     x2 = to_row_block(x2)
     x1 = spread_z(x1)
     x1, x2 = lax.optimization_barrier((x1, x2))
     x1_parts = spread_x(x1)
-    x2 = spread_z(jnp.broadcast_to(x2[None], (NZ, CH, TOK)))
+    x2 = spread_z(jnp.broadcast_to(x2[None], (NZ, CROWS, TOK)))
     x1_parts, x2 = lax.optimization_barrier((x1_parts, x2))
     activation, gm = pl.pallas_call(
         forward_kernel,
         out_shape=(
             jax.ShapeDtypeStruct((TOK, HID), bf),
-            jax.ShapeDtypeStruct((TOK, 2 * HID), bf),
+            jax.ShapeDtypeStruct((NY, TOK, HID), bf),
         ),
         in_specs=sm(1) + vm(5) + hbm(5),
         out_specs=tuple(vm(2)),
@@ -254,21 +289,23 @@
         expert_count,
         w_all,
     )
-    gm_all = lax.all_gather(gm, "dp", axis=0, tiled=True)
-    x2, _ = lax.optimization_barrier((x2, gm))
+    x2, gm = lax.optimization_barrier((x2, gm))
+    mine = spread(gm, "dp", Y_GROUPS)
     x2_parts = spread_x(x2)
+    mine, x2_parts = lax.optimization_barrier((mine, x2_parts))
+    gm_parts = (mine, other_core(mine))
     grad_w = pl.pallas_call(
         weight_kernel,
         out_shape=jax.ShapeDtypeStruct((TOK, 2 * HID), f32),
-        in_specs=sm(1) + vm(5) + hbm(1),
+        in_specs=sm(1) + vm(5) + hbm(2),
         out_specs=vm(1)[0],
         scratch_shapes=[
-            pltpu.VMEM((2 * CH, D), bf),
-            pltpu.VMEM((D, 2 * HID), bf),
-            pltpu.SemaphoreType.DMA((1,)),
+            pltpu.VMEM((2, 2 * CH, D), bf),
+            pltpu.VMEM((2, NY, TOK, HID), bf),
+            pltpu.SemaphoreType.DMA((2,)),
         ],
         compiler_params=params,
-    )(x_pos, *x2_parts, gm_all)
+    )(x_pos, *x2_parts, *gm_parts)
     return activation, grad_w.reshape(TOK, 2, HID)
 
 

time: 150 us -> 151 us (level)
  waiting for transfers between devices: 71.7 us -> 58.1 us
  starting transfers between devices: 46.3 us -> 57.5 us
  local copies, waits for them, and re-layouts: 4.33 us -> 7.71 us
    all_gather x1 -> x0, waiting for transfers between devices: 16.6 us -> none  [on_device(): gm_all = lax.all_gather(gm, 'dp', axis=0, tiled=True)]
    ppermute x0 -> x1, starting transfers between devices: none -> 6.06 us  [other_core(): return lax.ppermute(value, AXES, pairs)]
    all_to_all x2 -> x3, starting transfers between devices: 13.4 us -> 18.2 us  [spread(): lax.all_to_all(copies.reshape(n * r, c), axis, 0, 0, axis_index_groups=gr...]
    unnamed x11 -> x19, local copies, waits for them, and re-layouts: 2.31 us -> 5.64 us
    ppermute x0 -> x1, waiting for transfers between devices: none -> 2.26 us  [other_core(): return lax.ppermute(value, AXES, pairs)]
    all_to_all x2 -> x3, waiting for transfers between devices: 10.5 us -> 10.5 us  [spread(): lax.all_to_all(copies.reshape(n * r, c), axis, 0, 0, axis_index_groups=gr...]
  transfers between devices with their start and end apart: 14 -> 15, of which waited for: 9 -> 9; matrix products, arithmetic and copies ran while one was open for 1% -> 1% of each run, Pallas kernels for 2% -> 2%
where the time goes in v3:
time: 151 us; the launch traced here: 150 us
  waiting for transfers between devices  58.1 us (38%)
  starting transfers between devices  57.5 us (38%)
  between operations  14.2 us (9%)
  Pallas kernels  12.8 us (8%)
  local copies, waits for them, and re-layouts  7.71 us (5%)
    ppermute x8, waiting for transfers between devices, shift_x(): return lax.ppermute(value, AXES, pairs)  36.7 us
    ppermute x8, starting transfers between devices, shift_x(): return lax.ppermute(value, AXES, pairs)  25.2 us
    all_to_all x3, starting transfers between devices, spread(): lax.all_to_all(copies.reshape(n * r, c), axis, 0, 0, axis_index_groups=gr...  18.2 us
    all_to_all x3, waiting for transfers between devices, spread(): lax.all_to_all(copies.reshape(n * r, c), axis, 0, 0, axis_index_groups=gr...  10.5 us
    ppermute x1, starting transfers between devices, other_core(): return lax.ppermute(value, AXES, pairs)  6.06 us
    pallas_call x1, Pallas kernels, on_device(): pl.pallas_call(forward_kernel, out_shape=(jax.ShapeDtypeStruct((TOK, HID)...  6.03 us
    unnamed x19, local copies, waits for them, and re-layouts  5.64 us
    ppermute x1, starting transfers between devices, on_device(): halo = lax.ppermute(halo, 'dp', [(s, s + 1) for s in range(2 * NY - 1)])  4.59 us
  transfers between devices with their start and end apart: 15, of which 9 were waited for; matrix products, arithmetic and copies ran while one was open for 1% of the time, Pallas kernels for 2%

profile of v3, /device:TPU:1, one launch (start us, length us, event | category | flops | bytes accessed | tf_op | source)
XLA Modules:
  0.0 150.5 jit_solution(946153350952364694)
XLA Ops:
  7.2 0.0 copy-start.6
  7.2 0.0 copy-start.5
  7.2 0.0 copy-start.4
  7.2 0.0 copy-start.7
  7.2 0.0 all-gather.2.cloned.1.call-start
  7.3 1.4 shard_map.113
  8.6 1.7 %copy.12 = bf16[32,8,2,256]{3,1,2,0:T(8,128)(2,1)} copy(bf16[32,8,2,256]{3,2,1,0:T(2,128)(2,1)} %bitcast.8) | data formatting | bytes 524288
  10.3 0.0 all-gather.2.cloned.1.call-update
  10.3 4.6 %collective-permute-start = (bf16[3,16,128]{2,1,0:T(8,128)(2,1)}, bf16[3,16,128]{2,1,0:T(8,128)(2,1)S(1)}, u32[]{:S(2)}, u32[]{:S(2)}) collective-permute-start(bf16[3,16,128]{2,1,0:T(8,128)(2,1)} %shard_map.113), channel_id=1, source_target_pairs={{0,32},{32,64},{64,96},{96,128},{128,160},{160,192},{192,224},{224... | collective-permute-start | bytes 36872 | tf_op jit(solution)/shard_map/ppermute | solution.py:236
  14.9 4.4 %collective-permute-done.halo_ref = bf16[3,16,128]{2,1,0:T(8,128)(2,1)S(1)} collective-permute-done((bf16[3,16,128]{2,1,0:T(8,128)(2,1)}, bf16[3,16,128]{2,1,0:T(8,128)(2,1)S(1)}, u32[]{:S(2)}, u32[]{:S(2)}) %collective-permute-start) | collective-permute-done | bytes 12320 | tf_op jit(solution)/shard_map/ppermute | solution.py:236
  19.4 0.6 copy-done.8
  20.0 2.7 %shard_map.114 = (bf16[8,272,128]{2,1,0:T(8,128)(2,1)}, bf16[144,256]{1,0:T(8,128)(2,1)}) custom-call(bf16[256,128]{1,0:T(8,128)(2,1)} %q_hbm.1, bf16[256,128]{1,0:T(8,128)(2,1)} %k_hbm.1, bf16[256,128]{1,0:T(8,128)(2,1)} %v_hbm.1, f32[3,3,128]{2,1,0:T(4,128)} %taps_hbm.1, bf16[1,128]{1,0:T(2,128)(2,1)} %bitcast.9, s32[1,384]{1,0:T(1,128)} %refs_7_.1, ...), custom_call_target="tpu_custom_call" | custom-call | tf_op jit(solution)/shard_map/pallas_call | solution.py:237
  22.7 6.6 %all-to-all-start = ((bf16[8,272,128]{2,1,0:T(8,128)(2,1)}), bf16[8,272,128]{2,1,0:T(8,128)(2,1)S(1)}, u32[]{:S(2)}, u32[]{:S(2)}) async-start(bf16[8,272,128]{2,1,0:T(8,128)(2,1)} %get-tuple-element.25), calls=%async_computation | async-start | bytes 1114112 | tf_op jit(solution)/shard_map/all_to_all | solution.py:49
  29.3 3.5 %collective-permute-start.1 = (bf16[144,256]{1,0:T(8,128)(2,1)}, bf16[144,256]{1,0:T(8,128)(2,1)S(1)}, u32[]{:S(2)}, u32[]{:S(2)}) collective-permute-start(bf16[144,256]{1,0:T(8,128)(2,1)} %get-tuple-element.26), channel_id=1, source_target_pairs={{0,0},{1,1},{2,32},{3,33},{4,64},{5,65},{6,96},{7,97},{8,128},{9,1... | collective-permute-start | bytes 221192 | tf_op jit(solution)/shard_map/ppermute | solution.py:44
  32.8 4.2 %collective-permute-done.1 = bf16[144,256]{1,0:T(8,128)(2,1)S(1)} collective-permute-done((bf16[144,256]{1,0:T(8,128)(2,1)}, bf16[144,256]{1,0:T(8,128)(2,1)S(1)}, u32[]{:S(2)}, u32[]{:S(2)}) %collective-permute-start.1) | collective-permute-done | bytes 73760 | tf_op jit(solution)/shard_map/ppermute | solution.py:44
  37.0 10.5 %all-to-all-done.refs_0_ = bf16[8,272,128]{2,1,0:T(8,128)(2,1)S(1)} async-done(((bf16[8,272,128]{2,1,0:T(8,128)(2,1)}), bf16[8,272,128]{2,1,0:T(8,128)(2,1)S(1)}, u32[]{:S(2)}, u32[]{:S(2)}) %all-to-all-start) | async-done | bytes 557088 | tf_op jit(solution)/shard_map/all_to_all | solution.py:49
  47.6 0.9 broadcast_in_dim.2
  48.4 7.0 %all-to-all-start.1 = ((bf16[8,144,256]{2,1,0:T(8,128)(2,1)}), bf16[8,144,256]{2,1,0:T(8,128)(2,1)S(1)}, u32[]{:S(2)}, u32[]{:S(2)}) async-start(bf16[8,144,256]{2,1,0:T(8,128)(2,1)} %broadcast_in_dim.2), calls=%async_computation.1 | async-start | bytes 1179648 | tf_op jit(solution)/shard_map/all_to_all | solution.py:49
  55.4 4.4 %collective-permute-start.3 = (bf16[8,272,128]{2,1,0:T(8,128)(2,1)S(1)}, bf16[8,272,128]{2,1,0:T(8,128)(2,1)S(1)}, u32[]{:S(2)}, u32[]{:S(2)}) collective-permute-start(bf16[8,272,128]{2,1,0:T(8,128)(2,1)S(1)} %all-to-all-done.refs_0_), channel_id=1, source_target_pairs={{0,3},{1,0},{2,1},{3,2},{4,7},{5,4},{6,5},{7,6},{8,11},{9,8},{10,9... | collective-permute-start | bytes 1671176 | tf_op jit(solution)/shard_map/ppermute | solution.py:30
  59.8 1.9 %collective-permute-start.2 = (bf16[8,272,128]{2,1,0:T(8,128)(2,1)S(1)}, bf16[8,272,128]{2,1,0:T(8,128)(2,1)S(1)}, u32[]{:S(2)}, u32[]{:S(2)}) collective-permute-start(bf16[8,272,128]{2,1,0:T(8,128)(2,1)S(1)} %all-to-all-done.refs_0_), channel_id=1, source_target_pairs={{0,1},{1,2},{2,3},{3,0},{4,5},{5,6},{6,7},{7,4},{8,9},{9,10},{10,1... | collective-permute-start | bytes 1671176 | tf_op jit(solution)/shard_map/ppermute | solution.py:30
  61.8 3.6 %collective-permute-start.5 = (bf16[4,272,128]{2,1,0:T(8,128)(2,1)S(1)}, bf16[4,272,128]{2,1,0:T(8,128)(2,1)S(1)}, u32[]{:S(2)}, u32[]{:S(2)}) collective-permute-start(bf16[4,272,128]{2,1,0:T(8,128)(2,1)S(1)} %get-tuple-element.48), channel_id=1, source_target_pairs={{0,2},{1,3},{2,0},{3,1},{4,6},{5,7},{6,4},{7,5},{8,10},{9,11},{10,... | collective-permute-start | bytes 835592 | tf_op jit(solution)/shard_map/ppermute | solution.py:30
  65.4 3.2 %collective-permute-start.4 = (bf16[4,272,128]{2,1,0:T(8,128)(2,1)S(1)}, bf16[4,272,128]{2,1,0:T(8,128)(2,1)S(1)}, u32[]{:S(2)}, u32[]{:S(2)}) collective-permute-start(bf16[4,272,128]{2,1,0:T(8,128)(2,1)S(1)} %get-tuple-element.49), channel_id=1, source_target_pairs={{0,2},{1,3},{2,0},{3,1},{4,6},{5,7},{6,4},{7,5},{8,10},{9,11},{10,... | collective-permute-start | bytes 835592 | tf_op jit(solution)/shard_map/ppermute | solution.py:30
  68.6 0.1 pad_add_fusion.x_ref
  68.7 13.2 %collective-permute-done.5.refs_4_ = bf16[4,272,128]{2,1,0:T(8,128)(2,1)S(1)} collective-permute-done((bf16[4,272,128]{2,1,0:T(8,128)(2,1)S(1)}, bf16[4,272,128]{2,1,0:T(8,128)(2,1)S(1)}, u32[]{:S(2)}, u32[]{:S(2)}) %collective-permute-start.5) | collective-permute-done | bytes 278560 | tf_op jit(solution)/shard_map/ppermute | solution.py:30
  81.8 6.0 %collective-permute-done.4.refs_3_ = bf16[4,272,128]{2,1,0:T(8,128)(2,1)S(1)} collective-permute-done((bf16[4,272,128]{2,1,0:T(8,128)(2,1)S(1)}, bf16[4,272,128]{2,1,0:T(8,128)(2,1)S(1)}, u32[]{:S(2)}, u32[]{:S(2)}) %collective-permute-start.4) | collective-permute-done | bytes 278560 | tf_op jit(solution)/shard_map/ppermute | solution.py:30
  87.8 0.0 collective-permute-done.3.refs_2_
  87.8 0.9 collective-permute-done.2.refs_1_
  88.7 0.0 all-to-all-done.1.refs_0_
  88.7 0.0 copy-done.6
  88.7 6.0 %shard_map.115 = (bf16[256,256]{1,0:T(8,128)(2,1)}, bf16[8,256,256]{2,1,0:T(8,128)(2,1)}) custom-call(s32[2]{0:T(128)S(1)} %pad_add_fusion.x_ref, bf16[8,272,128]{2,1,0:T(8,128)(2,1)S(1)} %all-to-all-done.refs_0_, bf16[8,272,128]{2,1,0:T(8,128)(2,1)S(1)} %collective-permute-done.2.refs_1_, bf16[8,272,128]{2,1,0:T(8,128)(2,1)S(1)} %collective-permute-done.3.refs_2_, ...), custom_call_target="tpu_custom_call" | custom-call | tf_op jit(solution)/shard_map/pallas_call | solution.py:265
  94.8 4.5 %all-to-all-start.2 = ((bf16[8,256,256]{2,1,0:T(8,128)(2,1)}), bf16[8,256,256]{2,1,0:T(8,128)(2,1)S(1)}, u32[]{:S(2)}, u32[]{:S(2)}) async-start(bf16[8,256,256]{2,1,0:T(8,128)(2,1)} %get-tuple-element.38), calls=%async_computation.2 | async-start | bytes 2097152 | tf_op jit(solution)/shard_map/all_to_all | solution.py:49
  99.3 1.9 %collective-permute-start.7 = (bf16[8,144,256]{2,1,0:T(8,128)(2,1)S(1)}, bf16[8,144,256]{2,1,0:T(8,128)(2,1)S(1)}, u32[]{:S(2)}, u32[]{:S(2)}) collective-permute-start(bf16[8,144,256]{2,1,0:T(8,128)(2,1)S(1)} %all-to-all-done.1.refs_0_), channel_id=1, source_target_pairs={{0,3},{1,0},{2,1},{3,2},{4,7},{5,4},{6,5},{7,6},{8,11},{9,8},{10,9... | collective-permute-start | bytes 1769480 | tf_op jit(solution)/shard_map/ppermute | solution.py:30
  101.2 3.4 %collective-permute-start.6 = (bf16[8,144,256]{2,1,0:T(8,128)(2,1)S(1)}, bf16[8,144,256]{2,1,0:T(8,128)(2,1)S(1)}, u32[]{:S(2)}, u32[]{:S(2)}) collective-permute-start(bf16[8,144,256]{2,1,0:T(8,128)(2,1)S(1)} %all-to-all-done.1.refs_0_), channel_id=1, source_target_pairs={{0,1},{1,2},{2,3},{3,0},{4,5},{5,6},{6,7},{7,4},{8,9},{9,10},{10,1... | collective-permute-start | bytes 1769480 | tf_op jit(solution)/shard_map/ppermute | solution.py:30
  104.7 3.4 %collective-permute-start.9 = (bf16[4,144,256]{2,1,0:T(8,128)(2,1)S(1)}, bf16[4,144,256]{2,1,0:T(8,128)(2,1)S(1)}, u32[]{:S(2)}, u32[]{:S(2)}) collective-permute-start(bf16[4,144,256]{2,1,0:T(8,128)(2,1)S(1)} %get-tuple-element.46), channel_id=1, source_target_pairs={{0,2},{1,3},{2,0},{3,1},{4,6},{5,7},{6,4},{7,5},{8,10},{9,11},{10,... | collective-permute-start | bytes 884744 | tf_op jit(solution)/shard_map/ppermute | solution.py:30
  108.1 3.4 %collective-permute-start.8 = (bf16[4,144,256]{2,1,0:T(8,128)(2,1)S(1)}, bf16[4,144,256]{2,1,0:T(8,128)(2,1)S(1)}, u32[]{:S(2)}, u32[]{:S(2)}) collective-permute-start(bf16[4,144,256]{2,1,0:T(8,128)(2,1)S(1)} %get-tuple-element.47), channel_id=1, source_target_pairs={{0,2},{1,3},{2,0},{3,1},{4,6},{5,7},{6,4},{7,5},{8,10},{9,11},{10,... | collective-permute-start | bytes 884744 | tf_op jit(solution)/shard_map/ppermute | solution.py:30
  111.5 10.7 %collective-permute-done.9.refs_4_ = bf16[4,144,256]{2,1,0:T(8,128)(2,1)S(1)} collective-permute-done((bf16[4,144,256]{2,1,0:T(8,128)(2,1)S(1)}, bf16[4,144,256]{2,1,0:T(8,128)(2,1)S(1)}, u32[]{:S(2)}, u32[]{:S(2)}) %collective-permute-start.9) | collective-permute-done | bytes 294944 | tf_op jit(solution)/shard_map/ppermute | solution.py:30
  122.2 0.7 copy-done
  122.9 5.9 %collective-permute-done.8.refs_3_ = bf16[4,144,256]{2,1,0:T(8,128)(2,1)S(1)} collective-permute-done((bf16[4,144,256]{2,1,0:T(8,128)(2,1)S(1)}, bf16[4,144,256]{2,1,0:T(8,128)(2,1)S(1)}, u32[]{:S(2)}, u32[]{:S(2)}) %collective-permute-start.8) | collective-permute-done | bytes 294944 | tf_op jit(solution)/shard_map/ppermute | solution.py:30
  128.8 0.7 copy-done.2
  129.6 0.0 collective-permute-done.7.refs_2_
  129.6 0.0 collective-permute-done.6.refs_1_
  129.6 0.0 all-to-all-done.2.refs_5_
  129.6 6.1 %collective-permute-start.10 = (bf16[8,256,256]{2,1,0:T(8,128)(2,1)S(1)}, bf16[8,256,256]{2,1,0:T(8,128)(2,1)S(1)}, u32[]{:S(2)}, u32[]{:S(2)}) collective-permute-start(bf16[8,256,256]{2,1,0:T(8,128)(2,1)S(1)} %all-to-all-done.2.refs_5_), channel_id=1, source_target_pairs={{0,32},{1,33},{2,34},{3,35},{4,36},{5,37},{6,38},{7,39},{8,40},{9,... | collective-permute-start | bytes 3145736 | tf_op jit(solution)/shard_map/ppermute | solution.py:35
  135.6 2.3 %collective-permute-done.10.refs_6_ = bf16[8,256,256]{2,1,0:T(8,128)(2,1)S(1)} collective-permute-done((bf16[8,256,256]{2,1,0:T(8,128)(2,1)S(1)}, bf16[8,256,256]{2,1,0:T(8,128)(2,1)S(1)}, u32[]{:S(2)}, u32[]{:S(2)}) %collective-permute-start.10) | collective-permute-done | bytes 1048608 | tf_op jit(solution)/shard_map/ppermute | solution.py:35
  137.9 1.0 copy-done.1
  138.9 1.0 copy-done.3
  139.8 2.7 %shard_map.116 = f32[256,512]{1,0:T(8,128)S(1)} custom-call(s32[2]{0:T(128)S(1)} %pad_add_fusion.x_ref, bf16[8,144,256]{2,1,0:T(8,128)(2,1)S(1)} %all-to-all-done.1.refs_0_, bf16[8,144,256]{2,1,0:T(8,128)(2,1)S(1)} %collective-permute-done.6.refs_1_, bf16[8,144,256]{2,1,0:T(8,128)(2,1)S(1)} %collective-permute-done.7.refs_2_, ...), custom_call_target="tpu_custom_call" | custom-call | tf_op jit(solution)/shard_map/pallas_call | solution.py:297
  142.5 1.1 reshape.38
  (11 shorter events, 0.1 us)
Async XLA Ops:
  7.2 81.5 %copy-start.6 = (s32[1,2]{1,0:T(1,128)S(1)}, s32[1,2]{1,0:T(1,128)}, u32[]{:S(2)}) copy-start(s32[1,2]{1,0:T(1,128)} %refs_8_.1) | copy-start | bytes 28
  7.2 81.5 %copy-start.5 = (s32[1,384]{1,0:T(1,128)S(1)}, s32[1,384]{1,0:T(1,128)}, u32[]{:S(2)}) copy-start(s32[1,384]{1,0:T(1,128)} %refs_7_.1) | copy-start | bytes 4612
  7.2 81.5 %copy-start.4 = (bf16[256,256]{1,0:T(8,128)(2,1)S(1)}, bf16[256,256]{1,0:T(8,128)(2,1)}, u32[]{:S(2)}) copy-start(bf16[256,256]{1,0:T(8,128)(2,1)} %refs_5_.1) | copy-start | bytes 393220
  7.2 81.5 %copy-start.7 = (f32[256]{0:T(256)S(1)}, f32[256]{0:T(256)}, u32[]{:S(2)}) copy-start(f32[256]{0:T(256)} %param.17) | copy-start | bytes 3076
  7.2 81.5 %all-gather.2.cloned.1.call-start = ((), (), s32[]{:S(2)}) async-start(), calls=%async_computation.3 | async-start | bytes 4456448 | tf_op jit(solution)/shard_map/all_gather | solution.py:235
  10.3 9.0 %collective-permute-start = (bf16[3,16,128]{2,1,0:T(8,128)(2,1)}, bf16[3,16,128]{2,1,0:T(8,128)(2,1)S(1)}, u32[]{:S(2)}, u32[]{:S(2)}) collective-permute-start(bf16[3,16,128]{2,1,0:T(8,128)(2,1)} %shard_map.113), channel_id=1, source_target_pairs={{0,32},{32,64},{64,96},{96,128},{128,160},{160,192},{192,224},{224... | collective-permute-start | bytes 36872 | tf_op jit(solution)/shard_map/ppermute | solution.py:236
  19.4 0.6 copy-start.8
  22.7 24.8 %all-to-all-start = ((bf16[8,272,128]{2,1,0:T(8,128)(2,1)}), bf16[8,272,128]{2,1,0:T(8,128)(2,1)S(1)}, u32[]{:S(2)}, u32[]{:S(2)}) async-start(bf16[8,272,128]{2,1,0:T(8,128)(2,1)} %get-tuple-element.25), calls=%async_computation | async-start | bytes 1114112 | tf_op jit(solution)/shard_map/all_to_all | solution.py:49
  29.3 7.7 %collective-permute-start.1 = (bf16[144,256]{1,0:T(8,128)(2,1)}, bf16[144,256]{1,0:T(8,128)(2,1)S(1)}, u32[]{:S(2)}, u32[]{:S(2)}) collective-permute-start(bf16[144,256]{1,0:T(8,128)(2,1)} %get-tuple-element.26), channel_id=1, source_target_pairs={{0,0},{1,1},{2,32},{3,33},{4,64},{5,65},{6,96},{7,97},{8,128},{9,1... | collective-permute-start | bytes 221192 | tf_op jit(solution)/shard_map/ppermute | solution.py:44
  48.4 40.3 %all-to-all-start.1 = ((bf16[8,144,256]{2,1,0:T(8,128)(2,1)}), bf16[8,144,256]{2,1,0:T(8,128)(2,1)S(1)}, u32[]{:S(2)}, u32[]{:S(2)}) async-start(bf16[8,144,256]{2,1,0:T(8,128)(2,1)} %broadcast_in_dim.2), calls=%async_computation.1 | async-start | bytes 1179648 | tf_op jit(solution)/shard_map/all_to_all | solution.py:49
  55.4 32.4 %collective-permute-start.3 = (bf16[8,272,128]{2,1,0:T(8,128)(2,1)S(1)}, bf16[8,272,128]{2,1,0:T(8,128)(2,1)S(1)}, u32[]{:S(2)}, u32[]{:S(2)}) collective-permute-start(bf16[8,272,128]{2,1,0:T(8,128)(2,1)S(1)} %all-to-all-done.refs_0_), channel_id=1, source_target_pairs={{0,3},{1,0},{2,1},{3,2},{4,7},{5,4},{6,5},{7,6},{8,11},{9,8},{10,9... | collective-permute-start | bytes 1671176 | tf_op jit(solution)/shard_map/ppermute | solution.py:30
  59.8 28.9 %collective-permute-start.2 = (bf16[8,272,128]{2,1,0:T(8,128)(2,1)S(1)}, bf16[8,272,128]{2,1,0:T(8,128)(2,1)S(1)}, u32[]{:S(2)}, u32[]{:S(2)}) collective-permute-start(bf16[8,272,128]{2,1,0:T(8,128)(2,1)S(1)} %all-to-all-done.refs_0_), channel_id=1, source_target_pairs={{0,1},{1,2},{2,3},{3,0},{4,5},{5,6},{6,7},{7,4},{8,9},{9,10},{10,1... | collective-permute-start | bytes 1671176 | tf_op jit(solution)/shard_map/ppermute | solution.py:30
  61.8 20.0 %collective-permute-start.5 = (bf16[4,272,128]{2,1,0:T(8,128)(2,1)S(1)}, bf16[4,272,128]{2,1,0:T(8,128)(2,1)S(1)}, u32[]{:S(2)}, u32[]{:S(2)}) collective-permute-start(bf16[4,272,128]{2,1,0:T(8,128)(2,1)S(1)} %get-tuple-element.48), channel_id=1, source_target_pairs={{0,2},{1,3},{2,0},{3,1},{4,6},{5,7},{6,4},{7,5},{8,10},{9,11},{10,... | collective-permute-start | bytes 835592 | tf_op jit(solution)/shard_map/ppermute | solution.py:30
  65.4 22.4 %collective-permute-start.4 = (bf16[4,272,128]{2,1,0:T(8,128)(2,1)S(1)}, bf16[4,272,128]{2,1,0:T(8,128)(2,1)S(1)}, u32[]{:S(2)}, u32[]{:S(2)}) collective-permute-start(bf16[4,272,128]{2,1,0:T(8,128)(2,1)S(1)} %get-tuple-element.49), channel_id=1, source_target_pairs={{0,2},{1,3},{2,0},{3,1},{4,6},{5,7},{6,4},{7,5},{8,10},{9,11},{10,... | collective-permute-start | bytes 835592 | tf_op jit(solution)/shard_map/ppermute | solution.py:30
  94.8 34.8 %all-to-all-start.2 = ((bf16[8,256,256]{2,1,0:T(8,128)(2,1)}), bf16[8,256,256]{2,1,0:T(8,128)(2,1)S(1)}, u32[]{:S(2)}, u32[]{:S(2)}) async-start(bf16[8,256,256]{2,1,0:T(8,128)(2,1)} %get-tuple-element.38), calls=%async_computation.2 | async-start | bytes 2097152 | tf_op jit(solution)/shard_map/all_to_all | solution.py:49
  99.3 30.2 %collective-permute-start.7 = (bf16[8,144,256]{2,1,0:T(8,128)(2,1)S(1)}, bf16[8,144,256]{2,1,0:T(8,128)(2,1)S(1)}, u32[]{:S(2)}, u32[]{:S(2)}) collective-permute-start(bf16[8,144,256]{2,1,0:T(8,128)(2,1)S(1)} %all-to-all-done.1.refs_0_), channel_id=1, source_target_pairs={{0,3},{1,0},{2,1},{3,2},{4,7},{5,4},{6,5},{7,6},{8,11},{9,8},{10,9... | collective-permute-start | bytes 1769480 | tf_op jit(solution)/shard_map/ppermute | solution.py:30
  101.2 28.3 %collective-permute-start.6 = (bf16[8,144,256]{2,1,0:T(8,128)(2,1)S(1)}, bf16[8,144,256]{2,1,0:T(8,128)(2,1)S(1)}, u32[]{:S(2)}, u32[]{:S(2)}) collective-permute-start(bf16[8,144,256]{2,1,0:T(8,128)(2,1)S(1)} %all-to-all-done.1.refs_0_), channel_id=1, source_target_pairs={{0,1},{1,2},{2,3},{3,0},{4,5},{5,6},{6,7},{7,4},{8,9},{9,10},{10,1... | collective-permute-start | bytes 1769480 | tf_op jit(solution)/shard_map/ppermute | solution.py:30
  104.7 17.6 %collective-permute-start.9 = (bf16[4,144,256]{2,1,0:T(8,128)(2,1)S(1)}, bf16[4,144,256]{2,1,0:T(8,128)(2,1)S(1)}, u32[]{:S(2)}, u32[]{:S(2)}) collective-permute-start(bf16[4,144,256]{2,1,0:T(8,128)(2,1)S(1)} %get-tuple-element.46), channel_id=1, source_target_pairs={{0,2},{1,3},{2,0},{3,1},{4,6},{5,7},{6,4},{7,5},{8,10},{9,11},{10,... | collective-permute-start | bytes 884744 | tf_op jit(solution)/shard_map/ppermute | solution.py:30
  108.1 20.8 %collective-permute-start.8 = (bf16[4,144,256]{2,1,0:T(8,128)(2,1)S(1)}, bf16[4,144,256]{2,1,0:T(8,128)(2,1)S(1)}, u32[]{:S(2)}, u32[]{:S(2)}) collective-permute-start(bf16[4,144,256]{2,1,0:T(8,128)(2,1)S(1)} %get-tuple-element.47), channel_id=1, source_target_pairs={{0,2},{1,3},{2,0},{3,1},{4,6},{5,7},{6,4},{7,5},{8,10},{9,11},{10,... | collective-permute-start | bytes 884744 | tf_op jit(solution)/shard_map/ppermute | solution.py:30
  122.2 0.7 copy-start
  128.8 0.7 copy-start.2
  129.6 8.3 %collective-permute-start.10 = (bf16[8,256,256]{2,1,0:T(8,128)(2,1)S(1)}, bf16[8,256,256]{2,1,0:T(8,128)(2,1)S(1)}, u32[]{:S(2)}, u32[]{:S(2)}) collective-permute-start(bf16[8,256,256]{2,1,0:T(8,128)(2,1)S(1)} %all-to-all-done.2.refs_5_), channel_id=1, source_target_pairs={{0,32},{1,33},{2,34},{3,35},{4,36},{5,37},{6,38},{7,39},{8,40},{9,... | collective-permute-start | bytes 3145736 | tf_op jit(solution)/shard_map/ppermute | solution.py:35
  137.9 1.0 copy-start.1
  138.9 1.0 copy-start.3
Sparse Core Ops, SparseCore 0:
  10.7 55.5 all-gather.1

commit v4 on v3

--- a/solution.py
+++ b/solution.py
@@ -1,4 +1,4 @@
-import functools
+import itertools
 
 import jax
 import jax.numpy as jnp
@@ -14,7 +14,8 @@
 TOK, CH, HID = 256, 128, 256
 ROWS = TOK + 16
 CROWS = CH + 16
-VMEM_LIMIT = 48 * 1024 * 1024
+HALVES = TOK // CH
+VMEM_LIMIT = 40 * 1024 * 1024
 AXES = ("dp", "expert")
 Y_GROUPS = [[y * 2 + c for y in range(NY)] for c in range(2)]
 Z_GROUPS = [[z * NX + x for z in range(NZ)] for x in range(NX)]
@@ -48,31 +49,7 @@
     n, r, c = copies.shape
     return lax.all_to_all(
         copies.reshape(n * r, c), axis, 0, 0, axis_index_groups=groups, tiled=True
-    ).reshape(n, r, c)
-
-
-def spread_z(copies):
-    return spread(copies, "expert", Z_GROUPS)
-
-
-def spread_x(b):
-    half = b.shape[0] // 2
-    return (b, shift_x(b, 1), shift_x(b, -1), shift_x(b[:half], 2), shift_x(b[half:], -2))
-
-
-def gathered_blocks(x_ref, parts):
-    own, from_left, from_right, low, high = parts
-    x = x_ref[0]
-    for ref, off, z0 in (
-        (own, 0, 0),
-        (from_left, NX - 1, 0),
-        (from_right, 1, 0),
-        (low, 2, 0),
-        (high, 2, NZ // 2),
-    ):
-        xx = lax.rem(x + off, NX)
-        for k in range(ref.shape[0]):
-            yield ref, k, (z0 + k) * NX + xx
+    )
 
 
 def load_all(pairs, sems):
@@ -141,28 +118,69 @@
         x1_ref[n, 0:TOK, :] = mixed
         x1_ref[n, TOK:ROWS, :] = tail
     scaled = mixed.astype(jnp.float32) * gain
-    x2_ref[0:CH, :] = scaled.T.astype(jnp.bfloat16)
+    turned = scaled.T.astype(jnp.bfloat16)
     second = jnp.sum(
         jnp.where(diagonal(), in_second(slot_ref, count_ref), 0.0), axis=0, keepdims=True
     )
-    x2_ref[CH:CROWS, :] = jnp.broadcast_to(second, (16, TOK)).astype(jnp.bfloat16)
-
-
-def forward_kernel(x_ref, *refs):
-    parts = refs[:5]
-    sources, (act_ref, gm_ref, xn_ref), held, sems = refs[5:10], refs[10:13], refs[13:18], refs[18]
-    g_ref, prob_ref, slot_ref, count_ref, w_ref = held
-    copies = load_all(list(zip(sources, held)), sems)
+    second = jnp.broadcast_to(second, (16, TOK)).astype(jnp.bfloat16)
+    for h in range(HALVES):
+        tokens = slice(h * CH, (h + 1) * CH)
+        x2_ref[h * CROWS : h * CROWS + CH, :] = turned[:, tokens]
+        x2_ref[h * CROWS + CH : (h + 1) * CROWS, :] = second[:, tokens]
+
+
+def scaled_rows(ref, blocks, first, xn_ref, square):
+    for k in range(blocks):
+        row = k * ROWS
+        m = ref[row : row + TOK, :].astype(jnp.float32)
+        gain = ref[row + TOK : row + ROWS, :].astype(jnp.float32)[0:1, :]
+        square = square + m * m
+        xn_ref[:, (first + k) * CH : (first + k + 1) * CH] = (m * gain).astype(jnp.bfloat16)
+    return square
+
+
+def near_kernel(x_ref, own_ref, left_ref, right_ref, w_hbm, acc_ref, square_ref, xn_ref, w_ref, sems):
+    x = x_ref[0]
+    copies = load_all(
+        [
+            (w_hbm.at[:, lax.rem(x + off, NX)], w_ref.at[n])
+            for n, off in enumerate((0, NX - 1, 1))
+        ],
+        sems,
+    )
     square = jnp.zeros((TOK, CH), jnp.float32)
-    for ref, k, j in gathered_blocks(x_ref, parts):
-        m = ref[k, 0:TOK, :].astype(jnp.float32)
-        gain = ref[k, TOK : TOK + 16, :].astype(jnp.float32)[0:1, :]
-        square = square + m * m
-        xn_ref[:, pl.ds(pl.multiple_of(j * CH, CH), CH)] = (m * gain).astype(jnp.bfloat16)
+    for n, ref in enumerate((own_ref, left_ref, right_ref)):
+        square = scaled_rows(ref, NZ, n * NZ, xn_ref, square)
+    square_ref[...] = square
+    for copy in copies:
+        copy.wait()
+    acc_ref[...] = jnp.dot(
+        xn_ref[...], w_ref[...].reshape(3 * NZ * CH, 2 * HID), preferred_element_type=jnp.float32
+    )
+
+
+def forward_kernel(
+    x_ref, low_ref, high_ref, acc_ref, square_ref, g_hbm, prob_hbm, slot_hbm, count_hbm, w_hbm,
+    act_ref, gm_ref, xn_ref, g_ref, prob_ref, slot_ref, count_ref, w_ref, sems,
+):
+    copies = load_all(
+        [
+            (w_hbm.at[:, lax.rem(x_ref[0] + 2, NX)], w_ref),
+            (g_hbm, g_ref),
+            (prob_hbm, prob_ref),
+            (slot_hbm, slot_ref),
+            (count_hbm, count_ref),
+        ],
+        sems,
+    )
+    square = scaled_rows(low_ref, NZ // 2, 0, xn_ref, square_ref[...])
+    square = scaled_rows(high_ref, NZ // 2, NZ // 2, xn_ref, square)
     inv = lax.rsqrt(jnp.sum(square, axis=1, keepdims=True) / D + EPS)
     for copy in copies:
         copy.wait()
-    both = jnp.dot(xn_ref[...], w_ref[...], preferred_element_type=jnp.float32)
+    both = acc_ref[...] + jnp.dot(
+        xn_ref[...], w_ref[...].reshape(NZ * CH, 2 * HID), preferred_element_type=jnp.float32
+    )
     second = in_second(slot_ref, count_ref) > 0.5
     prob = jnp.sum(jnp.where(diagonal(), prob_ref[...], 0.0), axis=1, keepdims=True)
     pre = jnp.where(second, both[:, HID:], both[:, :HID]) * inv
@@ -174,25 +192,33 @@
         gm_ref[n] = grad
 
 
-def weight_kernel(x_ref, *refs):
-    parts = refs[:5]
-    mine_hbm, other_hbm, out_ref, xt_ref, gm_ref, sems = refs[5:]
-    copies = load_all([(mine_hbm, gm_ref.at[0]), (other_hbm, gm_ref.at[1])], sems)
-    for ref, k, j in gathered_blocks(x_ref, parts):
-        i = lax.div(j, 2)
-        place = jnp.where(lax.rem(i, 2) == x_ref[1], lax.div(i, 2), NY + lax.div(i, 2))
-        rows = pl.ds(pl.multiple_of(lax.rem(j, 2) * CH, CH), CH)
-        cols = pl.ds(pl.multiple_of(place * TOK, TOK), TOK)
-        second = ref[k, CH:CROWS, :].astype(jnp.float32)[0:1, :]
-        block = ref[k, 0:CH, :].astype(jnp.float32)
-        xt_ref[0, rows, cols] = (block * (1.0 - second)).astype(jnp.bfloat16)
-        xt_ref[1, rows, cols] = (block * second).astype(jnp.bfloat16)
-    for copy in copies:
-        copy.wait()
-    grads = gm_ref[...].reshape(D, HID)
+def weight_mine_kernel(x_ref, x_hbm, mine_hbm, acc_ref, rest_ref, xt_ref, rows_ref, gm_ref, sems):
+    copies = load_all([(x_hbm, rows_ref), (mine_hbm, gm_ref)], sems)
+    copies[0].wait()
+    half_x = [lax.rem(x_ref[0] + off, NX) for off in (0, NX - 1, 1, 2)]
+    for z, n in itertools.product(range(NZ), range(NX)):
+        xx = half_x[n]
+        rows = pl.ds(pl.multiple_of(lax.rem(xx, 2) * CH, CH), CH)
+        side = jnp.where(lax.div(xx, 2) == x_ref[1], 0, 1)
+        for h in range(HALVES):
+            cols = pl.ds(z * TOK + h * CH, CH)
+            top = h * CROWS
+            second = rows_ref[z, n, top + CH : top + CROWS, :].astype(jnp.float32)[0:1, :]
+            block = rows_ref[z, n, top : top + CH, :].astype(jnp.float32)
+            xt_ref[side, 0, rows, cols] = (block * (1.0 - second)).astype(jnp.bfloat16)
+            xt_ref[side, 1, rows, cols] = (block * second).astype(jnp.bfloat16)
+    copies[1].wait()
+    grads = gm_ref[...].reshape(NY * TOK, HID)
     for e in range(2):
-        out_ref[:, e * HID : (e + 1) * HID] = jnp.dot(
-            xt_ref[e], grads, preferred_element_type=jnp.float32
+        acc_ref[e] = jnp.dot(xt_ref[0, e], grads, preferred_element_type=jnp.float32)
+        rest_ref[e] = xt_ref[1, e]
+
+
+def weight_kernel(acc_ref, rest_ref, other_ref, out_ref):
+    grads = other_ref[...].reshape(NY * TOK, HID)
+    for e in range(2):
+        out_ref[:, e * HID : (e + 1) * HID] = acc_ref[e] + jnp.dot(
+            rest_ref[e], grads, preferred_element_type=jnp.float32
         )
 
 
@@ -238,7 +264,7 @@
         mix_kernel,
         out_shape=(
             jax.ShapeDtypeStruct((NZ, ROWS, CH), bf),
-            jax.ShapeDtypeStruct((CROWS, TOK), bf),
+            jax.ShapeDtypeStruct((HALVES * CROWS, CH), bf),
         ),
         in_specs=hbm(7) + vm(1),
         out_specs=tuple(vm(2)),
@@ -257,55 +283,88 @@
     x_pos = jnp.stack([lax.rem(lax.axis_index("expert"), NX), lax.rem(lax.axis_index("dp"), 2)])
     x_pos = x_pos.astype(jnp.int32)
     x2 = to_row_block(x2)
-    x1 = spread_z(x1)
+    x1 = spread(x1, "expert", Z_GROUPS)
     x1, x2 = lax.optimization_barrier((x1, x2))
-    x1_parts = spread_x(x1)
-    x2 = spread_z(jnp.broadcast_to(x2[None], (NZ, CROWS, TOK)))
-    x1_parts, x2 = lax.optimization_barrier((x1_parts, x2))
+    rows = NZ * ROWS
+    both = jnp.concatenate([x1, x2])
+    left, right = shift_x(both, 1), shift_x(both, -1)
+    x2_far = shift_x(x2, 2)
+    left, right, x2_far = lax.optimization_barrier((left, right, x2_far))
+    far = (shift_x(left[: rows // 2], 1), shift_x(right[rows // 2 : rows], -1))
+    x2 = jnp.stack([x2, left[rows:], right[rows:], x2_far])
+    x2_all = lax.all_gather(x2, "expert", axis=0, axis_index_groups=Z_GROUPS)
+    w_all = w_all.reshape(NZ, NX, CH, 2 * HID)
+    acc, square = pl.pallas_call(
+        near_kernel,
+        out_shape=(
+            jax.ShapeDtypeStruct((TOK, 2 * HID), f32),
+            jax.ShapeDtypeStruct((TOK, CH), f32),
+        ),
+        in_specs=sm(1) + vm(3) + hbm(1),
+        out_specs=tuple(vm(2)),
+        scratch_shapes=[
+            pltpu.VMEM((TOK, 3 * NZ * CH), bf),
+            pltpu.VMEM((3, NZ, CH, 2 * HID), bf),
+            pltpu.SemaphoreType.DMA((3,)),
+        ],
+        compiler_params=params,
+        cost_estimate=pl.CostEstimate(flops=800_000_000, bytes_accessed=6_000_000, transcendentals=0),
+    )(x_pos, x1, left, right, w_all)
     activation, gm = pl.pallas_call(
         forward_kernel,
         out_shape=(
             jax.ShapeDtypeStruct((TOK, HID), bf),
             jax.ShapeDtypeStruct((NY, TOK, HID), bf),
         ),
-        in_specs=sm(1) + vm(5) + hbm(5),
+        in_specs=sm(1) + vm(4) + hbm(5),
         out_specs=tuple(vm(2)),
         scratch_shapes=[
-            pltpu.VMEM((TOK, D), bf),
+            pltpu.VMEM((TOK, NZ * CH), bf),
             pltpu.VMEM((TOK, HID), bf),
             pltpu.VMEM((1, TOK), f32),
             pltpu.VMEM((1, 384), jnp.int32),
             pltpu.VMEM((1, 2), jnp.int32),
-            pltpu.VMEM((D, 2 * HID), bf),
+            pltpu.VMEM((NZ, CH, 2 * HID), bf),
             pltpu.SemaphoreType.DMA((5,)),
         ],
         compiler_params=params,
     )(
         x_pos,
-        *x1_parts,
+        *far,
+        acc,
+        square,
         grad_out,
         route_prob.reshape(1, TOK),
         slot_token,
         expert_count,
         w_all,
     )
-    x2, gm = lax.optimization_barrier((x2, gm))
-    mine = spread(gm, "dp", Y_GROUPS)
-    x2_parts = spread_x(x2)
-    mine, x2_parts = lax.optimization_barrier((mine, x2_parts))
-    gm_parts = (mine, other_core(mine))
+    mine = spread(gm, "dp", Y_GROUPS).reshape(NY, TOK, HID)
+    other = other_core(mine)
+    acc, rest = pl.pallas_call(
+        weight_mine_kernel,
+        out_shape=(
+            jax.ShapeDtypeStruct((2, 2 * CH, HID), f32),
+            jax.ShapeDtypeStruct((2, 2 * CH, NY * TOK), bf),
+        ),
+        in_specs=sm(1) + hbm(2),
+        out_specs=tuple(vm(2)),
+        scratch_shapes=[
+            pltpu.VMEM((2, 2, 2 * CH, NY * TOK), bf),
+            pltpu.VMEM((NZ, NX, HALVES * CROWS, CH), bf),
+            pltpu.VMEM((NY, TOK, HID), bf),
+            pltpu.SemaphoreType.DMA((2,)),
+        ],
+        compiler_params=params,
+        cost_estimate=pl.CostEstimate(flops=500_000_000, bytes_accessed=6_000_000, transcendentals=0),
+    )(x_pos, x2_all, mine)
     grad_w = pl.pallas_call(
         weight_kernel,
         out_shape=jax.ShapeDtypeStruct((TOK, 2 * HID), f32),
-        in_specs=sm(1) + vm(5) + hbm(2),
+        in_specs=vm(3),
         out_specs=vm(1)[0],
-        scratch_shapes=[
-            pltpu.VMEM((2, 2 * CH, D), bf),
-            pltpu.VMEM((2, NY, TOK, HID), bf),
-            pltpu.SemaphoreType.DMA((2,)),
-        ],
         compiler_params=params,
-    )(x_pos, *x2_parts, *gm_parts)
+    )(acc, rest, other)
     return activation, grad_w.reshape(TOK, 2, HID)
 
 

time: 151 us -> 137 us (0.907)
  blocking collectives: 0 us -> 30.4 us
  waiting for transfers between devices: 58.1 us -> 31.2 us
  starting transfers between devices: 57.5 us -> 40.1 us
    all_to_all x0 -> x1, blocking collectives: none -> 30.4 us  [spread(): lax.all_to_all(copies.reshape(n * r, c), axis, 0, 0, axis_index_groups=gr...]
    ppermute x8 -> x5, waiting for transfers between devices: 36.7 us -> 12 us  [shift_x(): return lax.ppermute(value, AXES, pairs)]
    all_to_all x3 -> x1, starting transfers between devices: 18.2 us -> 6.63 us  [spread(): lax.all_to_all(copies.reshape(n * r, c), axis, 0, 0, axis_index_groups=gr...]
    ppermute x8 -> x5, starting transfers between devices: 25.2 us -> 16.5 us  [shift_x(): return lax.ppermute(value, AXES, pairs)]
    pallas_call x0 -> x2, Pallas kernels: none -> 5.29 us  [the longest x1 2.81 us: on_device(): pl.pallas_call(weight_mine_kernel, out_shape=(jax.ShapeDtypeStruct((2, 2...]
    pallas_call x1, Pallas kernels: 6.03 us -> 2.3 us  [on_device(): pl.pallas_call(forward_kernel, out_shape=(jax.ShapeDtypeStruct((TOK, HID)...]
    ppermute x1, starting transfers between devices: 6.06 us -> 8.8 us  [other_core(): return lax.ppermute(value, AXES, pairs)]
    ppermute x1, waiting for transfers between devices: 2.26 us -> 0.01 us  [other_core(): return lax.ppermute(value, AXES, pairs)]
  transfers between devices with their start and end apart: 15 -> 11, of which waited for: 9 -> 5; matrix products, arithmetic and copies ran while one was open for 1% -> 1% of each run, Pallas kernels for 2% -> 8%
where the time goes in v4:
time: 137 us; the launch traced here: 136 us
  starting transfers between devices  40.1 us (29%)
  waiting for transfers between devices  31.2 us (23%)
  blocking collectives  30.4 us (22%)
  between operations  14.3 us (10%)
  Pallas kernels  12.4 us (9%)
  local copies, waits for them, and re-layouts  7.38 us (5%)
    all_to_all x1, blocking collectives, spread(): lax.all_to_all(copies.reshape(n * r, c), axis, 0, 0, axis_index_groups=gr...  30.4 us
    ppermute x5, starting transfers between devices, shift_x(): return lax.ppermute(value, AXES, pairs)  16.5 us
    ppermute x5, waiting for transfers between devices, shift_x(): return lax.ppermute(value, AXES, pairs)  12 us
    all_to_all x1, waiting for transfers between devices, spread(): lax.all_to_all(copies.reshape(n * r, c), axis, 0, 0, axis_index_groups=gr...  10.5 us
    ppermute x1, starting transfers between devices, other_core(): return lax.ppermute(value, AXES, pairs)  8.8 us
    all_to_all x1, starting transfers between devices, spread(): lax.all_to_all(copies.reshape(n * r, c), axis, 0, 0, axis_index_groups=gr...  6.63 us
    unnamed x18, local copies, waits for them, and re-layouts  6.2 us
    ppermute x1, starting transfers between devices, on_device(): halo = lax.ppermute(halo, 'dp', [(s, s + 1) for s in range(2 * NY - 1)])  4.59 us
  transfers between devices with their start and end apart: 11, of which 5 were waited for; matrix products, arithmetic and copies ran while one was open for 1% of the time, Pallas kernels for 8%

profile of v4, /device:TPU:1, one launch (start us, length us, event | category | flops | bytes accessed | tf_op | source)
XLA Modules:
  0.0 136.5 jit_solution(17036013705037112746)
XLA Ops:
  7.2 0.0 all-gather.4.cloned.1.call-start
  7.2 1.3 shard_map.113
  8.6 1.7 %copy.12 = bf16[32,8,2,256]{3,1,2,0:T(8,128)(2,1)} copy(bf16[32,8,2,256]{3,2,1,0:T(2,128)(2,1)} %bitcast.23) | data formatting | bytes 524288
  10.3 0.0 all-gather.4.cloned.1.call-update
  10.3 4.6 %collective-permute-start = (bf16[3,16,128]{2,1,0:T(8,128)(2,1)}, bf16[3,16,128]{2,1,0:T(8,128)(2,1)S(1)}, u32[]{:S(2)}, u32[]{:S(2)}) collective-permute-start(bf16[3,16,128]{2,1,0:T(8,128)(2,1)} %shard_map.113), channel_id=1, source_target_pairs={{0,32},{32,64},{64,96},{96,128},{128,160},{160,192},{192,224},{224... | collective-permute-start | bytes 36872 | tf_op jit(solution)/shard_map/ppermute | solution.py:262
  14.9 4.4 %collective-permute-done.halo_ref = bf16[3,16,128]{2,1,0:T(8,128)(2,1)S(1)} collective-permute-done((bf16[3,16,128]{2,1,0:T(8,128)(2,1)}, bf16[3,16,128]{2,1,0:T(8,128)(2,1)S(1)}, u32[]{:S(2)}, u32[]{:S(2)}) %collective-permute-start) | collective-permute-done | bytes 12320 | tf_op jit(solution)/shard_map/ppermute | solution.py:262
  19.3 0.0 copy-start.7
  19.3 0.6 copy-done.7
  19.9 2.7 %shard_map.114 = (bf16[8,272,128]{2,1,0:T(8,128)(2,1)}, bf16[288,128]{1,0:T(8,128)(2,1)}) custom-call(bf16[256,128]{1,0:T(8,128)(2,1)} %q_hbm.1, bf16[256,128]{1,0:T(8,128)(2,1)} %k_hbm.1, bf16[256,128]{1,0:T(8,128)(2,1)} %v_hbm.1, f32[3,3,128]{2,1,0:T(4,128)} %taps_hbm.1, bf16[1,128]{1,0:T(2,128)(2,1)} %bitcast.25, s32[1,384]{1,0:T(1,128)} %slot_hbm.3, ...), custom_call_target="tpu_custom_call" | custom-call | tf_op jit(solution)/shard_map/pallas_call | solution.py:263
  22.7 6.6 %all-to-all-start = ((bf16[8,272,128]{2,1,0:T(8,128)(2,1)}), bf16[8,272,128]{2,1,0:T(8,128)(2,1)S(1)}, u32[]{:S(2)}, u32[]{:S(2)}) async-start(bf16[8,272,128]{2,1,0:T(8,128)(2,1)} %get-tuple-element.18), calls=%async_computation | async-start | bytes 1114112 | tf_op jit(solution)/shard_map/all_to_all | solution.py:50
  29.3 0.0 all-gather.6.cloned.1.call-start
  29.3 3.5 %collective-permute-start.1 = (bf16[288,128]{1,0:T(8,128)(2,1)}, bf16[288,128]{1,0:T(8,128)(2,1)S(1)}, u32[]{:S(2)}, u32[]{:S(2)}) collective-permute-start(bf16[288,128]{1,0:T(8,128)(2,1)} %get-tuple-element.19), channel_id=1, source_target_pairs={{0,0},{1,1},{2,32},{3,33},{4,64},{5,65},{6,96},{7,97},{8,128},{9,1... | collective-permute-start | bytes 221192 | tf_op jit(solution)/shard_map/ppermute | solution.py:45
  32.8 4.2 %collective-permute-done.1 = bf16[288,128]{1,0:T(8,128)(2,1)S(1)} collective-permute-done((bf16[288,128]{1,0:T(8,128)(2,1)}, bf16[288,128]{1,0:T(8,128)(2,1)S(1)}, u32[]{:S(2)}, u32[]{:S(2)}) %collective-permute-start.1) | collective-permute-done | bytes 73760 | tf_op jit(solution)/shard_map/ppermute | solution.py:45
  37.0 10.5 %all-to-all-done = bf16[8,272,128]{2,1,0:T(8,128)(2,1)S(1)} async-done(((bf16[8,272,128]{2,1,0:T(8,128)(2,1)}), bf16[8,272,128]{2,1,0:T(8,128)(2,1)S(1)}, u32[]{:S(2)}, u32[]{:S(2)}) %all-to-all-start) | async-done | bytes 557088 | tf_op jit(solution)/shard_map/all_to_all | solution.py:50
  47.6 3.1 %collective-permute-start.2 = (bf16[2464,128]{1,0:T(8,128)(2,1)S(1)}, bf16[2464,128]{1,0:T(8,128)(2,1)S(1)}, u32[]{:S(2)}, u32[]{:S(2)}) collective-permute-start(bf16[2464,128]{1,0:T(8,128)(2,1)S(1)} %constant_dynamic-update-slice_fusion), channel_id=1, source_target_pairs={{0,1},{1,2},{2,3},{3,0},{4,5},{5,6},{6,7},{7,4},{8,9},{9,10},{10,1... | collective-permute-start | bytes 1892360 | tf_op jit(solution)/shard_map/ppermute | solution.py:31
  50.7 3.4 %collective-permute-start.3 = (bf16[2464,128]{1,0:T(8,128)(2,1)S(1)}, bf16[2464,128]{1,0:T(8,128)(2,1)S(1)}, u32[]{:S(2)}, u32[]{:S(2)}) collective-permute-start(bf16[2464,128]{1,0:T(8,128)(2,1)S(1)} %constant_dynamic-update-slice_fusion), channel_id=1, source_target_pairs={{0,3},{1,0},{2,1},{3,2},{4,7},{5,4},{6,5},{7,6},{8,11},{9,8},{10,9... | collective-permute-start | bytes 1892360 | tf_op jit(solution)/shard_map/ppermute | solution.py:31
  54.1 3.4 %collective-permute-start.4 = (bf16[288,128]{1,0:T(8,128)(2,1)S(1)}, bf16[288,128]{1,0:T(8,128)(2,1)S(1)}, u32[]{:S(2)}, u32[]{:S(2)}) collective-permute-start(bf16[288,128]{1,0:T(8,128)(2,1)S(1)} %collective-permute-done.1), channel_id=1, source_target_pairs={{0,2},{1,3},{2,0},{3,1},{4,6},{5,7},{6,4},{7,5},{8,10},{9,11},{10,... | collective-permute-start | bytes 221192 | tf_op jit(solution)/shard_map/ppermute | solution.py:31
  57.5 11.2 %collective-permute-done.4 = bf16[288,128]{1,0:T(8,128)(2,1)S(1)} collective-permute-done((bf16[288,128]{1,0:T(8,128)(2,1)S(1)}, bf16[288,128]{1,0:T(8,128)(2,1)S(1)}, u32[]{:S(2)}, u32[]{:S(2)}) %collective-permute-start.4) | collective-permute-done | bytes 73760 | tf_op jit(solution)/shard_map/ppermute | solution.py:31
  68.7 0.0 collective-permute-done.2.left_ref
  68.7 0.0 collective-permute-done.3.right_ref
  68.8 0.8 pad_maximum_fusion
  69.5 0.0 all-gather.6.cloned.1.call-update
  69.6 4.1 %collective-permute-start.5 = (bf16[1088,128]{1,0:T(8,128)(2,1)S(1)}, bf16[1088,128]{1,0:T(8,128)(2,1)S(1)}, u32[]{:S(2)}, u32[]{:S(2)}) collective-permute-start(bf16[1088,128]{1,0:T(8,128)(2,1)S(1)} %slice.12), channel_id=1, source_target_pairs={{0,1},{1,2},{2,3},{3,0},{4,5},{5,6},{6,7},{7,4},{8,9},{9,10},{10,1... | collective-permute-start | bytes 835592 | tf_op jit(solution)/shard_map/ppermute | solution.py:31
  73.7 2.5 %collective-permute-start.6 = (bf16[1088,128]{1,0:T(8,128)(2,1)S(1)}, bf16[1088,128]{1,0:T(8,128)(2,1)S(1)}, u32[]{:S(2)}, u32[]{:S(2)}) collective-permute-start(bf16[1088,128]{1,0:T(8,128)(2,1)S(1)} %slice.13), channel_id=1, source_target_pairs={{0,3},{1,0},{2,1},{3,2},{4,7},{5,4},{6,5},{7,6},{8,11},{9,8},{10,9... | collective-permute-start | bytes 835592 | tf_op jit(solution)/shard_map/ppermute | solution.py:31
  76.2 0.1 pad_add_fusion.x_ref
  76.2 0.0 all-gather.4.cloned.1.call-done
  76.2 0.0 copy-start
  76.2 2.2 %copy-done = bf16[4096,512]{1,0:T(8,128)(2,1)S(1)} copy-done((bf16[4096,512]{1,0:T(8,128)(2,1)S(1)}, bf16[4096,512]{1,0:T(8,128)(2,1)}, u32[]{:S(2)}) %copy-start) | copy-done | bytes 4194328
  78.4 0.0 copy-start.1
  78.4 0.0 copy-start.6
  78.5 2.5 %shard_map.115 = (f32[256,512]{1,0:T(8,128)S(1)}, f32[256,128]{1,0:T(8,128)S(1)}) custom-call(s32[2]{0:T(128)S(1)} %pad_add_fusion.x_ref, bf16[2176,128]{1,0:T(8,128)(2,1)S(1)} %bitcast.18, bf16[2464,128]{1,0:T(8,128)(2,1)S(1)} %collective-permute-done.2.left_ref, bf16[2464,128]{1,0:T(8,128)(2,1)S(1)} %collective-permute-done.3.right_ref, ...), custom_call_target="tpu_custom_call" | custom-call | flops 800000000 | bytes 6000000 | tf_op jit(solution)/shard_map/pallas_call | solution.py:297
  80.9 0.0 collective-permute-done.5.low_ref
  81.0 0.8 collective-permute-done.6.high_ref
  81.7 0.0 copy-done.1
  81.7 0.0 copy-done.3
  81.7 0.0 copy-done.4
  81.7 0.0 copy-done.5
  81.7 0.0 copy-done.6
  81.7 2.3 %shard_map.116 = (bf16[256,256]{1,0:T(8,128)(2,1)}, bf16[8,256,256]{2,1,0:T(8,128)(2,1)S(1)}) custom-call(s32[2]{0:T(128)S(1)} %pad_add_fusion.x_ref, bf16[1088,128]{1,0:T(8,128)(2,1)S(1)} %collective-permute-done.5.low_ref, bf16[1088,128]{1,0:T(8,128)(2,1)S(1)} %collective-permute-done.6.high_ref, f32[256,512]{1,0:T(8,128)S(1)} %get-tuple-element.25.acc_ref, ...), custom_call_target="tpu_custom_call" | custom-call | tf_op jit(solution)/shard_map/pallas_call | solution.py:313
  84.1 30.4 %all_to_all.15.mine_hbm = bf16[8,256,256]{2,1,0:T(8,128)(2,1)S(1)} all-to-all(bf16[8,256,256]{2,1,0:T(8,128)(2,1)S(1)} %get-tuple-element.29), channel_id=1, replica_groups={{0,64,128,192,256,320,384,448},{32,96,160,224,288,352,416,480},{1,65,12..., dimensions={0} | all-to-all | bytes 2097152 | tf_op jit(solution)/shard_map/all_to_all | solution.py:50
  114.5 8.8 %collective-permute-start.7 = (bf16[8,256,256]{2,1,0:T(8,128)(2,1)S(1)}, bf16[8,256,256]{2,1,0:T(8,128)(2,1)S(1)}, u32[]{:S(2)}, u32[]{:S(2)}) collective-permute-start(bf16[8,256,256]{2,1,0:T(8,128)(2,1)S(1)} %all_to_all.15.mine_hbm), channel_id=1, source_target_pairs={{0,32},{1,33},{2,34},{3,35},{4,36},{5,37},{6,38},{7,39},{8,40},{9,... | collective-permute-start | bytes 3145736 | tf_op jit(solution)/shard_map/ppermute | solution.py:36
  123.3 0.0 all-gather.6.cloned.1.call-done
  123.3 0.0 copy-start.2
  123.3 1.7 %copy-done.2 = bf16[32,288,128]{2,1,0:T(8,128)(2,1)S(1)} copy-done((bf16[32,288,128]{2,1,0:T(8,128)(2,1)S(1)}, bf16[32,288,128]{2,1,0:T(8,128)(2,1)}, u32[]{:S(2)}) %copy-start.2) | copy-done | bytes 2359320
  125.0 2.8 %shard_map.117 = (f32[2,256,256]{2,1,0:T(8,128)S(1)}, bf16[2,256,2048]{2,1,0:T(8,128)(2,1)S(1)}) custom-call(s32[2]{0:T(128)S(1)} %pad_add_fusion.x_ref, bf16[8,4,288,128]{3,2,1,0:T(8,128)(2,1)S(1)} %bitcast.19, bf16[8,256,256]{2,1,0:T(8,128)(2,1)S(1)} %all_to_all.15.mine_hbm), custom_call_target="tpu_custom_call" | custom-call | flops 500000000 | bytes 6000000 | tf_op jit(solution)/shard_map/pallas_call | solution.py:344
  127.8 0.0 collective-permute-done.7.other_ref
  127.8 0.7 shard_map.118
  128.5 1.1 reshape.33
  (8 shorter events, 0.1 us)
Async XLA Ops:
  7.2 69.1 %all-gather.4.cloned.1.call-start = ((), (), s32[]{:S(2)}) async-start(), calls=%async_computation.2 | async-start | bytes 4456448 | tf_op jit(solution)/shard_map/all_gather | solution.py:261
  10.3 9.0 %collective-permute-start = (bf16[3,16,128]{2,1,0:T(8,128)(2,1)}, bf16[3,16,128]{2,1,0:T(8,128)(2,1)S(1)}, u32[]{:S(2)}, u32[]{:S(2)}) collective-permute-start(bf16[3,16,128]{2,1,0:T(8,128)(2,1)} %shard_map.113), channel_id=1, source_target_pairs={{0,32},{32,64},{64,96},{96,128},{128,160},{160,192},{192,224},{224... | collective-permute-start | bytes 36872 | tf_op jit(solution)/shard_map/ppermute | solution.py:262
  19.3 0.6 copy-start.7
  22.7 24.8 %all-to-all-start = ((bf16[8,272,128]{2,1,0:T(8,128)(2,1)}), bf16[8,272,128]{2,1,0:T(8,128)(2,1)S(1)}, u32[]{:S(2)}, u32[]{:S(2)}) async-start(bf16[8,272,128]{2,1,0:T(8,128)(2,1)} %get-tuple-element.18), calls=%async_computation | async-start | bytes 1114112 | tf_op jit(solution)/shard_map/all_to_all | solution.py:50
  29.3 94.0 %all-gather.6.cloned.1.call-start = ((), (), s32[]{:S(2)}) async-start(), calls=%async_computation.3 | async-start | bytes 2654208 | tf_op jit(solution)/shard_map/all_gather | solution.py:295
  29.3 7.7 %collective-permute-start.1 = (bf16[288,128]{1,0:T(8,128)(2,1)}, bf16[288,128]{1,0:T(8,128)(2,1)S(1)}, u32[]{:S(2)}, u32[]{:S(2)}) collective-permute-start(bf16[288,128]{1,0:T(8,128)(2,1)} %get-tuple-element.19), channel_id=1, source_target_pairs={{0,0},{1,1},{2,32},{3,33},{4,64},{5,65},{6,96},{7,97},{8,128},{9,1... | collective-permute-start | bytes 221192 | tf_op jit(solution)/shard_map/ppermute | solution.py:45
  47.6 21.2 %collective-permute-start.2 = (bf16[2464,128]{1,0:T(8,128)(2,1)S(1)}, bf16[2464,128]{1,0:T(8,128)(2,1)S(1)}, u32[]{:S(2)}, u32[]{:S(2)}) collective-permute-start(bf16[2464,128]{1,0:T(8,128)(2,1)S(1)} %constant_dynamic-update-slice_fusion), channel_id=1, source_target_pairs={{0,1},{1,2},{2,3},{3,0},{4,5},{5,6},{6,7},{7,4},{8,9},{9,10},{10,1... | collective-permute-start | bytes 1892360 | tf_op jit(solution)/shard_map/ppermute | solution.py:31
  50.7 18.1 %collective-permute-start.3 = (bf16[2464,128]{1,0:T(8,128)(2,1)S(1)}, bf16[2464,128]{1,0:T(8,128)(2,1)S(1)}, u32[]{:S(2)}, u32[]{:S(2)}) collective-permute-start(bf16[2464,128]{1,0:T(8,128)(2,1)S(1)} %constant_dynamic-update-slice_fusion), channel_id=1, source_target_pairs={{0,3},{1,0},{2,1},{3,2},{4,7},{5,4},{6,5},{7,6},{8,11},{9,8},{10,9... | collective-permute-start | bytes 1892360 | tf_op jit(solution)/shard_map/ppermute | solution.py:31
  54.1 14.7 %collective-permute-start.4 = (bf16[288,128]{1,0:T(8,128)(2,1)S(1)}, bf16[288,128]{1,0:T(8,128)(2,1)S(1)}, u32[]{:S(2)}, u32[]{:S(2)}) collective-permute-start(bf16[288,128]{1,0:T(8,128)(2,1)S(1)} %collective-permute-done.1), channel_id=1, source_target_pairs={{0,2},{1,3},{2,0},{3,1},{4,6},{5,7},{6,4},{7,5},{8,10},{9,11},{10,... | collective-permute-start | bytes 221192 | tf_op jit(solution)/shard_map/ppermute | solution.py:31
  69.6 11.3 %collective-permute-start.5 = (bf16[1088,128]{1,0:T(8,128)(2,1)S(1)}, bf16[1088,128]{1,0:T(8,128)(2,1)S(1)}, u32[]{:S(2)}, u32[]{:S(2)}) collective-permute-start(bf16[1088,128]{1,0:T(8,128)(2,1)S(1)} %slice.12), channel_id=1, source_target_pairs={{0,1},{1,2},{2,3},{3,0},{4,5},{5,6},{6,7},{7,4},{8,9},{9,10},{10,1... | collective-permute-start | bytes 835592 | tf_op jit(solution)/shard_map/ppermute | solution.py:31
  73.7 8.0 %collective-permute-start.6 = (bf16[1088,128]{1,0:T(8,128)(2,1)S(1)}, bf16[1088,128]{1,0:T(8,128)(2,1)S(1)}, u32[]{:S(2)}, u32[]{:S(2)}) collective-permute-start(bf16[1088,128]{1,0:T(8,128)(2,1)S(1)} %slice.13), channel_id=1, source_target_pairs={{0,3},{1,0},{2,1},{3,2},{4,7},{5,4},{6,5},{7,6},{8,11},{9,8},{10,9... | collective-permute-start | bytes 835592 | tf_op jit(solution)/shard_map/ppermute | solution.py:31
  76.2 2.2 %copy-start = (bf16[4096,512]{1,0:T(8,128)(2,1)S(1)}, bf16[4096,512]{1,0:T(8,128)(2,1)}, u32[]{:S(2)}) copy-start(bf16[4096,512]{1,0:T(8,128)(2,1)} %all-gather.4.cloned.1.call-done) | copy-start | bytes 12582916
  78.4 3.3 %copy-start.1 = (bf16[4096,512]{1,0:T(8,128)(2,1)S(1)}, bf16[4096,512]{1,0:T(8,128)(2,1)}, u32[]{:S(2)}) copy-start(bf16[4096,512]{1,0:T(8,128)(2,1)} %all-gather.4.cloned.1.call-done) | copy-start | bytes 12582916
  78.4 3.3 %copy-start.3 = (bf16[256,256]{1,0:T(8,128)(2,1)S(1)}, bf16[256,256]{1,0:T(8,128)(2,1)}, u32[]{:S(2)}) copy-start(bf16[256,256]{1,0:T(8,128)(2,1)} %g_hbm.1) | copy-start | bytes 393220
  78.4 3.3 %copy-start.4 = (s32[1,384]{1,0:T(1,128)S(1)}, s32[1,384]{1,0:T(1,128)}, u32[]{:S(2)}) copy-start(s32[1,384]{1,0:T(1,128)} %slot_hbm.3) | copy-start | bytes 4612
  78.4 3.3 %copy-start.5 = (s32[1,2]{1,0:T(1,128)S(1)}, s32[1,2]{1,0:T(1,128)}, u32[]{:S(2)}) copy-start(s32[1,2]{1,0:T(1,128)} %count_hbm.3) | copy-start | bytes 28
  78.4 3.3 %copy-start.6 = (f32[256]{0:T(256)S(1)}, f32[256]{0:T(256)}, u32[]{:S(2)}) copy-start(f32[256]{0:T(256)} %param.17) | copy-start | bytes 3076
  114.5 13.3 %collective-permute-start.7 = (bf16[8,256,256]{2,1,0:T(8,128)(2,1)S(1)}, bf16[8,256,256]{2,1,0:T(8,128)(2,1)S(1)}, u32[]{:S(2)}, u32[]{:S(2)}) collective-permute-start(bf16[8,256,256]{2,1,0:T(8,128)(2,1)S(1)} %all_to_all.15.mine_hbm), channel_id=1, source_target_pairs={{0,32},{1,33},{2,34},{3,35},{4,36},{5,37},{6,38},{7,39},{8,40},{9,... | collective-permute-start | bytes 3145736 | tf_op jit(solution)/shard_map/ppermute | solution.py:36
  123.3 1.7 %copy-start.2 = (bf16[32,288,128]{2,1,0:T(8,128)(2,1)S(1)}, bf16[32,288,128]{2,1,0:T(8,128)(2,1)}, u32[]{:S(2)}) copy-start(bf16[32,288,128]{2,1,0:T(8,128)(2,1)} %all-gather.6.cloned.1.call-done) | copy-start | bytes 7077892
Sparse Core Ops, SparseCore 0:
  10.4 55.8 all-gather.3
  69.7 44.6 all-gather.5

commit v5 on v4

--- a/solution.py
+++ b/solution.py
@@ -192,9 +192,7 @@
         gm_ref[n] = grad
 
 
-def weight_mine_kernel(x_ref, x_hbm, mine_hbm, acc_ref, rest_ref, xt_ref, rows_ref, gm_ref, sems):
-    copies = load_all([(x_hbm, rows_ref), (mine_hbm, gm_ref)], sems)
-    copies[0].wait()
+def weight_mine_kernel(x_ref, rows_ref, gm_ref, acc_ref, xt_ref):
     half_x = [lax.rem(x_ref[0] + off, NX) for off in (0, NX - 1, 1, 2)]
     for z, n in itertools.product(range(NZ), range(NX)):
         xx = half_x[n]
@@ -203,22 +201,21 @@
         for h in range(HALVES):
             cols = pl.ds(z * TOK + h * CH, CH)
             top = h * CROWS
-            second = rows_ref[z, n, top + CH : top + CROWS, :].astype(jnp.float32)[0:1, :]
-            block = rows_ref[z, n, top : top + CH, :].astype(jnp.float32)
-            xt_ref[side, 0, rows, cols] = (block * (1.0 - second)).astype(jnp.bfloat16)
-            xt_ref[side, 1, rows, cols] = (block * second).astype(jnp.bfloat16)
-    copies[1].wait()
+            second = jnp.broadcast_to(rows_ref[z, n, top + CH : top + CROWS, :][0:1, :], (CH, CH))
+            block = rows_ref[z, n, top : top + CH, :]
+            masked = block * second
+            xt_ref[side, 0, rows, cols] = block - masked
+            xt_ref[side, 1, rows, cols] = masked
     grads = gm_ref[...].reshape(NY * TOK, HID)
     for e in range(2):
         acc_ref[e] = jnp.dot(xt_ref[0, e], grads, preferred_element_type=jnp.float32)
-        rest_ref[e] = xt_ref[1, e]
 
 
 def weight_kernel(acc_ref, rest_ref, other_ref, out_ref):
     grads = other_ref[...].reshape(NY * TOK, HID)
     for e in range(2):
-        out_ref[:, e * HID : (e + 1) * HID] = acc_ref[e] + jnp.dot(
-            rest_ref[e], grads, preferred_element_type=jnp.float32
+        out_ref[:, e, :] = acc_ref[e] + jnp.dot(
+            rest_ref[1, e], grads, preferred_element_type=jnp.float32
         )
 
 
@@ -345,27 +342,21 @@
         weight_mine_kernel,
         out_shape=(
             jax.ShapeDtypeStruct((2, 2 * CH, HID), f32),
-            jax.ShapeDtypeStruct((2, 2 * CH, NY * TOK), bf),
+            jax.ShapeDtypeStruct((2, 2, 2 * CH, NY * TOK), bf),
         ),
-        in_specs=sm(1) + hbm(2),
+        in_specs=sm(1) + vm(2),
         out_specs=tuple(vm(2)),
-        scratch_shapes=[
-            pltpu.VMEM((2, 2, 2 * CH, NY * TOK), bf),
-            pltpu.VMEM((NZ, NX, HALVES * CROWS, CH), bf),
-            pltpu.VMEM((NY, TOK, HID), bf),
-            pltpu.SemaphoreType.DMA((2,)),
-        ],
         compiler_params=params,
         cost_estimate=pl.CostEstimate(flops=500_000_000, bytes_accessed=6_000_000, transcendentals=0),
     )(x_pos, x2_all, mine)
     grad_w = pl.pallas_call(
         weight_kernel,
-        out_shape=jax.ShapeDtypeStruct((TOK, 2 * HID), f32),
+        out_shape=jax.ShapeDtypeStruct((TOK, 2, HID), f32),
         in_specs=vm(3),
         out_specs=vm(1)[0],
         compiler_params=params,
     )(acc, rest, other)
-    return activation, grad_w.reshape(TOK, 2, HID)
+    return activation, grad_w
 
 
 def solution(mesh):

time: 137 us -> 136 us (level)
  transfers between devices with their start and end apart: 11 -> 11, of which waited for: 5 -> 5; matrix products, arithmetic and copies ran while one was open for 1% -> 1% of each run, Pallas kernels for 8% -> 7%
where the time goes in v5:
time: 136 us
  starting transfers between devices  40.2 us (30%)
  waiting for transfers between devices  31.2 us (23%)
  blocking collectives  30.4 us (22%)
  between operations  14.3 us (11%)
  Pallas kernels  12.4 us (9%)
  local copies, waits for them, and re-layouts  6.27 us (5%)
    all_to_all x1, blocking collectives, spread(): lax.all_to_all(copies.reshape(n * r, c), axis, 0, 0, axis_index_groups=gr...  30.4 us
    ppermute x5, starting transfers between devices, shift_x(): return lax.ppermute(value, AXES, pairs)  16.6 us
    ppermute x5, waiting for transfers between devices, shift_x(): return lax.ppermute(value, AXES, pairs)  12 us
    all_to_all x1, waiting for transfers between devices, spread(): lax.all_to_all(copies.reshape(n * r, c), axis, 0, 0, axis_index_groups=gr...  10.5 us
    ppermute x1, starting transfers between devices, other_core(): return lax.ppermute(value, AXES, pairs)  8.8 us
    all_to_all x1, starting transfers between devices, spread(): lax.all_to_all(copies.reshape(n * r, c), axis, 0, 0, axis_index_groups=gr...  6.63 us
    unnamed x18, local copies, waits for them, and re-layouts  6.21 us
    ppermute x1, starting transfers between devices, on_device(): halo = lax.ppermute(halo, 'dp', [(s, s + 1) for s in range(2 * NY - 1)])  4.59 us
  transfers between devices with their start and end apart: 11, of which 5 were waited for; matrix products, arithmetic and copies ran while one was open for 1% of the time, Pallas kernels for 7%

profile of v5, /device:TPU:1, one launch (start us, length us, event | category | flops | bytes accessed | tf_op | source)
XLA Modules:
  0.0 135.5 jit_solution(4346664466579264553)
XLA Ops:
  7.2 0.0 all-gather.4.cloned.1.call-start
  7.2 1.3 shard_map.113
  8.6 1.7 %copy.12 = bf16[32,8,2,256]{3,1,2,0:T(8,128)(2,1)} copy(bf16[32,8,2,256]{3,2,1,0:T(2,128)(2,1)} %bitcast.23) | data formatting | bytes 524288
  10.3 0.0 all-gather.4.cloned.1.call-update
  10.3 4.6 %collective-permute-start = (bf16[3,16,128]{2,1,0:T(8,128)(2,1)}, bf16[3,16,128]{2,1,0:T(8,128)(2,1)S(1)}, u32[]{:S(2)}, u32[]{:S(2)}) collective-permute-start(bf16[3,16,128]{2,1,0:T(8,128)(2,1)} %shard_map.113), channel_id=1, source_target_pairs={{0,32},{32,64},{64,96},{96,128},{128,160},{160,192},{192,224},{224... | collective-permute-start | bytes 36872 | tf_op jit(solution)/shard_map/ppermute | solution.py:259
  14.9 4.4 %collective-permute-done.halo_ref = bf16[3,16,128]{2,1,0:T(8,128)(2,1)S(1)} collective-permute-done((bf16[3,16,128]{2,1,0:T(8,128)(2,1)}, bf16[3,16,128]{2,1,0:T(8,128)(2,1)S(1)}, u32[]{:S(2)}, u32[]{:S(2)}) %collective-permute-start) | collective-permute-done | bytes 12320 | tf_op jit(solution)/shard_map/ppermute | solution.py:259
  19.3 0.0 copy-start.7
  19.3 0.6 copy-done.7
  19.9 2.7 %shard_map.114 = (bf16[8,272,128]{2,1,0:T(8,128)(2,1)}, bf16[288,128]{1,0:T(8,128)(2,1)}) custom-call(bf16[256,128]{1,0:T(8,128)(2,1)} %q_hbm.1, bf16[256,128]{1,0:T(8,128)(2,1)} %k_hbm.1, bf16[256,128]{1,0:T(8,128)(2,1)} %v_hbm.1, f32[3,3,128]{2,1,0:T(4,128)} %taps_hbm.1, bf16[1,128]{1,0:T(2,128)(2,1)} %bitcast.25, s32[1,384]{1,0:T(1,128)} %slot_hbm.3, ...), custom_call_target="tpu_custom_call" | custom-call | tf_op jit(solution)/shard_map/pallas_call | solution.py:260
  22.7 6.6 %all-to-all-start = ((bf16[8,272,128]{2,1,0:T(8,128)(2,1)}), bf16[8,272,128]{2,1,0:T(8,128)(2,1)S(1)}, u32[]{:S(2)}, u32[]{:S(2)}) async-start(bf16[8,272,128]{2,1,0:T(8,128)(2,1)} %get-tuple-element.18), calls=%async_computation | async-start | bytes 1114112 | tf_op jit(solution)/shard_map/all_to_all | solution.py:50
  29.3 0.0 all-gather.6.cloned.1.call-start
  29.3 3.5 %collective-permute-start.1 = (bf16[288,128]{1,0:T(8,128)(2,1)}, bf16[288,128]{1,0:T(8,128)(2,1)S(1)}, u32[]{:S(2)}, u32[]{:S(2)}) collective-permute-start(bf16[288,128]{1,0:T(8,128)(2,1)} %get-tuple-element.19), channel_id=1, source_target_pairs={{0,0},{1,1},{2,32},{3,33},{4,64},{5,65},{6,96},{7,97},{8,128},{9,1... | collective-permute-start | bytes 221192 | tf_op jit(solution)/shard_map/ppermute | solution.py:45
  32.8 4.2 %collective-permute-done.1 = bf16[288,128]{1,0:T(8,128)(2,1)S(1)} collective-permute-done((bf16[288,128]{1,0:T(8,128)(2,1)}, bf16[288,128]{1,0:T(8,128)(2,1)S(1)}, u32[]{:S(2)}, u32[]{:S(2)}) %collective-permute-start.1) | collective-permute-done | bytes 73760 | tf_op jit(solution)/shard_map/ppermute | solution.py:45
  37.0 10.5 %all-to-all-done = bf16[8,272,128]{2,1,0:T(8,128)(2,1)S(1)} async-done(((bf16[8,272,128]{2,1,0:T(8,128)(2,1)}), bf16[8,272,128]{2,1,0:T(8,128)(2,1)S(1)}, u32[]{:S(2)}, u32[]{:S(2)}) %all-to-all-start) | async-done | bytes 557088 | tf_op jit(solution)/shard_map/all_to_all | solution.py:50
  47.6 0.0 copy-start.3
  47.6 0.0 copy-start.4
  47.6 0.0 copy-start.5
  47.6 0.0 copy-start.6
  47.6 3.3 %collective-permute-start.2 = (bf16[2464,128]{1,0:T(8,128)(2,1)S(1)}, bf16[2464,128]{1,0:T(8,128)(2,1)S(1)}, u32[]{:S(2)}, u32[]{:S(2)}) collective-permute-start(bf16[2464,128]{1,0:T(8,128)(2,1)S(1)} %constant_dynamic-update-slice_fusion), channel_id=1, source_target_pairs={{0,1},{1,2},{2,3},{3,0},{4,5},{5,6},{6,7},{7,4},{8,9},{9,10},{10,1... | collective-permute-start | bytes 1892360 | tf_op jit(solution)/shard_map/ppermute | solution.py:31
  50.9 3.4 %collective-permute-start.3 = (bf16[2464,128]{1,0:T(8,128)(2,1)S(1)}, bf16[2464,128]{1,0:T(8,128)(2,1)S(1)}, u32[]{:S(2)}, u32[]{:S(2)}) collective-permute-start(bf16[2464,128]{1,0:T(8,128)(2,1)S(1)} %constant_dynamic-update-slice_fusion), channel_id=1, source_target_pairs={{0,3},{1,0},{2,1},{3,2},{4,7},{5,4},{6,5},{7,6},{8,11},{9,8},{10,9... | collective-permute-start | bytes 1892360 | tf_op jit(solution)/shard_map/ppermute | solution.py:31
  54.2 3.4 %collective-permute-start.4 = (bf16[288,128]{1,0:T(8,128)(2,1)S(1)}, bf16[288,128]{1,0:T(8,128)(2,1)S(1)}, u32[]{:S(2)}, u32[]{:S(2)}) collective-permute-start(bf16[288,128]{1,0:T(8,128)(2,1)S(1)} %collective-permute-done.1), channel_id=1, source_target_pairs={{0,2},{1,3},{2,0},{3,1},{4,6},{5,7},{6,4},{7,5},{8,10},{9,11},{10,... | collective-permute-start | bytes 221192 | tf_op jit(solution)/shard_map/ppermute | solution.py:31
  57.7 11.2 %collective-permute-done.4 = bf16[288,128]{1,0:T(8,128)(2,1)S(1)} collective-permute-done((bf16[288,128]{1,0:T(8,128)(2,1)S(1)}, bf16[288,128]{1,0:T(8,128)(2,1)S(1)}, u32[]{:S(2)}, u32[]{:S(2)}) %collective-permute-start.4) | collective-permute-done | bytes 73760 | tf_op jit(solution)/shard_map/ppermute | solution.py:31
  68.9 0.0 collective-permute-done.2.left_ref
  68.9 0.0 collective-permute-done.3.right_ref
  68.9 0.8 pad_maximum_fusion
  69.7 0.0 all-gather.6.cloned.1.call-update
  69.8 4.1 %collective-permute-start.5 = (bf16[1088,128]{1,0:T(8,128)(2,1)S(1)}, bf16[1088,128]{1,0:T(8,128)(2,1)S(1)}, u32[]{:S(2)}, u32[]{:S(2)}) collective-permute-start(bf16[1088,128]{1,0:T(8,128)(2,1)S(1)} %slice.12), channel_id=1, source_target_pairs={{0,1},{1,2},{2,3},{3,0},{4,5},{5,6},{6,7},{7,4},{8,9},{9,10},{10,1... | collective-permute-start | bytes 835592 | tf_op jit(solution)/shard_map/ppermute | solution.py:31
  73.9 2.5 %collective-permute-start.6 = (bf16[1088,128]{1,0:T(8,128)(2,1)S(1)}, bf16[1088,128]{1,0:T(8,128)(2,1)S(1)}, u32[]{:S(2)}, u32[]{:S(2)}) collective-permute-start(bf16[1088,128]{1,0:T(8,128)(2,1)S(1)} %slice.13), channel_id=1, source_target_pairs={{0,3},{1,0},{2,1},{3,2},{4,7},{5,4},{6,5},{7,6},{8,11},{9,8},{10,9... | collective-permute-start | bytes 835592 | tf_op jit(solution)/shard_map/ppermute | solution.py:31
  76.3 0.1 pad_add_fusion.x_ref
  76.4 0.0 all-gather.4.cloned.1.call-done
  76.4 2.2 %copy-done = bf16[4096,512]{1,0:T(8,128)(2,1)S(1)} copy-done((bf16[4096,512]{1,0:T(8,128)(2,1)S(1)}, bf16[4096,512]{1,0:T(8,128)(2,1)}, u32[]{:S(2)}) %copy-start) | copy-done | bytes 4194328
  78.6 2.5 %shard_map.115 = (f32[256,512]{1,0:T(8,128)S(1)}, f32[256,128]{1,0:T(8,128)S(1)}) custom-call(s32[2]{0:T(128)S(1)} %pad_add_fusion.x_ref, bf16[2176,128]{1,0:T(8,128)(2,1)S(1)} %bitcast.18, bf16[2464,128]{1,0:T(8,128)(2,1)S(1)} %collective-permute-done.2.left_ref, bf16[2464,128]{1,0:T(8,128)(2,1)S(1)} %collective-permute-done.3.right_ref, ...), custom_call_target="tpu_custom_call" | custom-call | flops 800000000 | bytes 6000000 | tf_op jit(solution)/shard_map/pallas_call | solution.py:294
  81.1 0.0 collective-permute-done.5.low_ref
  81.1 0.8 collective-permute-done.6.high_ref
  81.9 0.0 copy-done.3
  81.9 0.0 copy-done.4
  81.9 0.0 copy-done.5
  81.9 0.0 copy-done.6
  81.9 0.0 copy-done.1
  81.9 2.3 %shard_map.116 = (bf16[256,256]{1,0:T(8,128)(2,1)}, bf16[8,256,256]{2,1,0:T(8,128)(2,1)S(1)}) custom-call(s32[2]{0:T(128)S(1)} %pad_add_fusion.x_ref, bf16[1088,128]{1,0:T(8,128)(2,1)S(1)} %collective-permute-done.5.low_ref, bf16[1088,128]{1,0:T(8,128)(2,1)S(1)} %collective-permute-done.6.high_ref, f32[256,512]{1,0:T(8,128)S(1)} %get-tuple-element.25.acc_ref, ...), custom_call_target="tpu_custom_call" | custom-call | tf_op jit(solution)/shard_map/pallas_call | solution.py:310
  84.2 30.4 %all_to_all.15.gm_ref = bf16[8,256,256]{2,1,0:T(8,128)(2,1)S(1)} all-to-all(bf16[8,256,256]{2,1,0:T(8,128)(2,1)S(1)} %get-tuple-element.29), channel_id=1, replica_groups={{0,64,128,192,256,320,384,448},{32,96,160,224,288,352,416,480},{1,65,12..., dimensions={0} | all-to-all | bytes 2097152 | tf_op jit(solution)/shard_map/all_to_all | solution.py:50
  114.6 8.8 %collective-permute-start.7 = (bf16[8,256,256]{2,1,0:T(8,128)(2,1)S(1)}, bf16[8,256,256]{2,1,0:T(8,128)(2,1)S(1)}, u32[]{:S(2)}, u32[]{:S(2)}) collective-permute-start(bf16[8,256,256]{2,1,0:T(8,128)(2,1)S(1)} %all_to_all.15.gm_ref), channel_id=1, source_target_pairs={{0,32},{1,33},{2,34},{3,35},{4,36},{5,37},{6,38},{7,39},{8,40},{9,... | collective-permute-start | bytes 3145736 | tf_op jit(solution)/shard_map/ppermute | solution.py:36
  123.4 0.0 all-gather.6.cloned.1.call-done
  123.5 0.0 copy-start.2
  123.5 1.7 %copy-done.2 = bf16[32,288,128]{2,1,0:T(8,128)(2,1)S(1)} copy-done((bf16[32,288,128]{2,1,0:T(8,128)(2,1)S(1)}, bf16[32,288,128]{2,1,0:T(8,128)(2,1)}, u32[]{:S(2)}) %copy-start.2) | copy-done | bytes 2359320
  125.1 1.9 %shard_map.117 = (f32[2,256,256]{2,1,0:T(8,128)S(1)}, bf16[2,2,256,2048]{3,2,1,0:T(8,128)(2,1)S(1)}) custom-call(s32[2]{0:T(128)S(1)} %pad_add_fusion.x_ref, bf16[8,4,288,128]{3,2,1,0:T(8,128)(2,1)S(1)} %bitcast.19, bf16[8,256,256]{2,1,0:T(8,128)(2,1)S(1)} %all_to_all.15.gm_ref), custom_call_target="tpu_custom_call" | custom-call | flops 500000000 | bytes 6000000 | tf_op jit(solution)/shard_map/pallas_call | solution.py:341
  127.0 0.0 collective-permute-done.7.other_ref
  127.0 1.6 %shard_map.118 = f32[256,2,256]{2,1,0:T(2,128)} custom-call(f32[2,256,256]{2,1,0:T(8,128)S(1)} %get-tuple-element.30.acc_ref, bf16[2,2,256,2048]{3,2,1,0:T(8,128)(2,1)S(1)} %get-tuple-element.31.rest_ref, bf16[8,256,256]{2,1,0:T(8,128)(2,1)S(1)} %collective-permute-done.7.other_ref), custom_call_target="tpu_custom_call" | custom-call | tf_op jit(solution)/shard_map/pallas_call | solution.py:352
  (7 shorter events, 0.1 us)
Async XLA Ops:
  7.2 69.3 %all-gather.4.cloned.1.call-start = ((), (), s32[]{:S(2)}) async-start(), calls=%async_computation.2 | async-start | bytes 4456448 | tf_op jit(solution)/shard_map/all_gather | solution.py:258
  10.3 9.0 %collective-permute-start = (bf16[3,16,128]{2,1,0:T(8,128)(2,1)}, bf16[3,16,128]{2,1,0:T(8,128)(2,1)S(1)}, u32[]{:S(2)}, u32[]{:S(2)}) collective-permute-start(bf16[3,16,128]{2,1,0:T(8,128)(2,1)} %shard_map.113), channel_id=1, source_target_pairs={{0,32},{32,64},{64,96},{96,128},{128,160},{160,192},{192,224},{224... | collective-permute-start | bytes 36872 | tf_op jit(solution)/shard_map/ppermute | solution.py:259
  19.3 0.6 copy-start.7
  22.7 24.8 %all-to-all-start = ((bf16[8,272,128]{2,1,0:T(8,128)(2,1)}), bf16[8,272,128]{2,1,0:T(8,128)(2,1)S(1)}, u32[]{:S(2)}, u32[]{:S(2)}) async-start(bf16[8,272,128]{2,1,0:T(8,128)(2,1)} %get-tuple-element.18), calls=%async_computation | async-start | bytes 1114112 | tf_op jit(solution)/shard_map/all_to_all | solution.py:50
  29.3 94.2 %all-gather.6.cloned.1.call-start = ((), (), s32[]{:S(2)}) async-start(), calls=%async_computation.3 | async-start | bytes 2654208 | tf_op jit(solution)/shard_map/all_gather | solution.py:292
  29.3 7.7 %collective-permute-start.1 = (bf16[288,128]{1,0:T(8,128)(2,1)}, bf16[288,128]{1,0:T(8,128)(2,1)S(1)}, u32[]{:S(2)}, u32[]{:S(2)}) collective-permute-start(bf16[288,128]{1,0:T(8,128)(2,1)} %get-tuple-element.19), channel_id=1, source_target_pairs={{0,0},{1,1},{2,32},{3,33},{4,64},{5,65},{6,96},{7,97},{8,128},{9,1... | collective-permute-start | bytes 221192 | tf_op jit(solution)/shard_map/ppermute | solution.py:45
  47.6 34.3 %copy-start.3 = (bf16[256,256]{1,0:T(8,128)(2,1)S(1)}, bf16[256,256]{1,0:T(8,128)(2,1)}, u32[]{:S(2)}) copy-start(bf16[256,256]{1,0:T(8,128)(2,1)} %g_hbm.1) | copy-start | bytes 393220
  47.6 34.3 %copy-start.4 = (s32[1,384]{1,0:T(1,128)S(1)}, s32[1,384]{1,0:T(1,128)}, u32[]{:S(2)}) copy-start(s32[1,384]{1,0:T(1,128)} %slot_hbm.3) | copy-start | bytes 4612
  47.6 34.3 %copy-start.5 = (s32[1,2]{1,0:T(1,128)S(1)}, s32[1,2]{1,0:T(1,128)}, u32[]{:S(2)}) copy-start(s32[1,2]{1,0:T(1,128)} %count_hbm.3) | copy-start | bytes 28
  47.6 34.3 %copy-start.6 = (f32[256]{0:T(256)S(1)}, f32[256]{0:T(256)}, u32[]{:S(2)}) copy-start(f32[256]{0:T(256)} %param.17) | copy-start | bytes 3076
  47.6 21.3 %collective-permute-start.2 = (bf16[2464,128]{1,0:T(8,128)(2,1)S(1)}, bf16[2464,128]{1,0:T(8,128)(2,1)S(1)}, u32[]{:S(2)}, u32[]{:S(2)}) collective-permute-start(bf16[2464,128]{1,0:T(8,128)(2,1)S(1)} %constant_dynamic-update-slice_fusion), channel_id=1, source_target_pairs={{0,1},{1,2},{2,3},{3,0},{4,5},{5,6},{6,7},{7,4},{8,9},{9,10},{10,1... | collective-permute-start | bytes 1892360 | tf_op jit(solution)/shard_map/ppermute | solution.py:31
  50.9 18.1 %collective-permute-start.3 = (bf16[2464,128]{1,0:T(8,128)(2,1)S(1)}, bf16[2464,128]{1,0:T(8,128)(2,1)S(1)}, u32[]{:S(2)}, u32[]{:S(2)}) collective-permute-start(bf16[2464,128]{1,0:T(8,128)(2,1)S(1)} %constant_dynamic-update-slice_fusion), channel_id=1, source_target_pairs={{0,3},{1,0},{2,1},{3,2},{4,7},{5,4},{6,5},{7,6},{8,11},{9,8},{10,9... | collective-permute-start | bytes 1892360 | tf_op jit(solution)/shard_map/ppermute | solution.py:31
  54.2 14.7 %collective-permute-start.4 = (bf16[288,128]{1,0:T(8,128)(2,1)S(1)}, bf16[288,128]{1,0:T(8,128)(2,1)S(1)}, u32[]{:S(2)}, u32[]{:S(2)}) collective-permute-start(bf16[288,128]{1,0:T(8,128)(2,1)S(1)} %collective-permute-done.1), channel_id=1, source_target_pairs={{0,2},{1,3},{2,0},{3,1},{4,6},{5,7},{6,4},{7,5},{8,10},{9,11},{10,... | collective-permute-start | bytes 221192 | tf_op jit(solution)/shard_map/ppermute | solution.py:31
  69.8 11.3 %collective-permute-start.5 = (bf16[1088,128]{1,0:T(8,128)(2,1)S(1)}, bf16[1088,128]{1,0:T(8,128)(2,1)S(1)}, u32[]{:S(2)}, u32[]{:S(2)}) collective-permute-start(bf16[1088,128]{1,0:T(8,128)(2,1)S(1)} %slice.12), channel_id=1, source_target_pairs={{0,1},{1,2},{2,3},{3,0},{4,5},{5,6},{6,7},{7,4},{8,9},{9,10},{10,1... | collective-permute-start | bytes 835592 | tf_op jit(solution)/shard_map/ppermute | solution.py:31
  73.9 8.0 %collective-permute-start.6 = (bf16[1088,128]{1,0:T(8,128)(2,1)S(1)}, bf16[1088,128]{1,0:T(8,128)(2,1)S(1)}, u32[]{:S(2)}, u32[]{:S(2)}) collective-permute-start(bf16[1088,128]{1,0:T(8,128)(2,1)S(1)} %slice.13), channel_id=1, source_target_pairs={{0,3},{1,0},{2,1},{3,2},{4,7},{5,4},{6,5},{7,6},{8,11},{9,8},{10,9... | collective-permute-start | bytes 835592 | tf_op jit(solution)/shard_map/ppermute | solution.py:31
  76.4 2.2 %copy-start = (bf16[4096,512]{1,0:T(8,128)(2,1)S(1)}, bf16[4096,512]{1,0:T(8,128)(2,1)}, u32[]{:S(2)}) copy-start(bf16[4096,512]{1,0:T(8,128)(2,1)} %all-gather.4.cloned.1.call-done) | copy-start | bytes 12582916
  78.6 3.3 %copy-start.1 = (bf16[4096,512]{1,0:T(8,128)(2,1)S(1)}, bf16[4096,512]{1,0:T(8,128)(2,1)}, u32[]{:S(2)}) copy-start(bf16[4096,512]{1,0:T(8,128)(2,1)} %all-gather.4.cloned.1.call-done) | copy-start | bytes 12582916
  114.6 12.4 %collective-permute-start.7 = (bf16[8,256,256]{2,1,0:T(8,128)(2,1)S(1)}, bf16[8,256,256]{2,1,0:T(8,128)(2,1)S(1)}, u32[]{:S(2)}, u32[]{:S(2)}) collective-permute-start(bf16[8,256,256]{2,1,0:T(8,128)(2,1)S(1)} %all_to_all.15.gm_ref), channel_id=1, source_target_pairs={{0,32},{1,33},{2,34},{3,35},{4,36},{5,37},{6,38},{7,39},{8,40},{9,... | collective-permute-start | bytes 3145736 | tf_op jit(solution)/shard_map/ppermute | solution.py:36
  123.5 1.7 %copy-start.2 = (bf16[32,288,128]{2,1,0:T(8,128)(2,1)S(1)}, bf16[32,288,128]{2,1,0:T(8,128)(2,1)}, u32[]{:S(2)}) copy-start(bf16[32,288,128]{2,1,0:T(8,128)(2,1)} %all-gather.6.cloned.1.call-done) | copy-start | bytes 7077892
Sparse Core Ops, SparseCore 0:
  10.4 55.8 all-gather.3
  69.8 44.6 all-gather.5

commit v6 on v5

--- a/solution.py
+++ b/solution.py
@@ -83,8 +83,8 @@
 
 
 def mix_kernel(
-    q_hbm, k_hbm, v_hbm, taps_hbm, gain_hbm, slot_hbm, count_hbm, halo_ref, x1_ref, x2_ref,
-    q_ref, k_ref, v_ref, taps_ref, gain_ref, slot_ref, count_ref, sems,
+    q_hbm, k_hbm, v_hbm, taps_hbm, slot_hbm, count_hbm, gain_ref, halo_ref, x1_ref, x2_ref,
+    q_ref, k_ref, v_ref, taps_ref, slot_ref, count_ref, sems,
 ):
     for copy in load_all(
         [
@@ -92,7 +92,6 @@
             (k_hbm, k_ref),
             (v_hbm, v_ref),
             (taps_hbm, taps_ref),
-            (gain_hbm, gain_ref),
             (slot_hbm, slot_ref),
             (count_hbm, count_ref),
         ],
@@ -263,20 +262,19 @@
             jax.ShapeDtypeStruct((NZ, ROWS, CH), bf),
             jax.ShapeDtypeStruct((HALVES * CROWS, CH), bf),
         ),
-        in_specs=hbm(7) + vm(1),
+        in_specs=hbm(6) + vm(2),
         out_specs=tuple(vm(2)),
         scratch_shapes=[
             pltpu.VMEM((TOK, CH), bf),
             pltpu.VMEM((TOK, CH), bf),
             pltpu.VMEM((TOK, CH), bf),
             pltpu.VMEM((3, 3, CH), f32),
-            pltpu.VMEM((1, CH), bf),
             pltpu.VMEM((1, 384), jnp.int32),
             pltpu.VMEM((1, 2), jnp.int32),
-            pltpu.SemaphoreType.DMA((7,)),
+            pltpu.SemaphoreType.DMA((6,)),
         ],
         compiler_params=full,
-    )(stream_q, stream_k, stream_v, conv_taps, norm_gain.reshape(1, CH), slot_token, expert_count, halo)
+    )(stream_q, stream_k, stream_v, conv_taps, slot_token, expert_count, norm_gain.reshape(1, CH), halo)
     x_pos = jnp.stack([lax.rem(lax.axis_index("expert"), NX), lax.rem(lax.axis_index("dp"), 2)])
     x_pos = x_pos.astype(jnp.int32)
     x2 = to_row_block(x2)

time: 136 us -> 136 us (level)
  no operation moved by 1% of the time
where the time goes in v6:
time: 136 us
  starting transfers between devices  40.2 us (30%)
  waiting for transfers between devices  31.2 us (23%)
  blocking collectives  30.4 us (22%)
  between operations  14.3 us (11%)
  Pallas kernels  12.4 us (9%)
  local copies, waits for them, and re-layouts  6.27 us (5%)
    all_to_all x1, blocking collectives, spread(): lax.all_to_all(copies.reshape(n * r, c), axis, 0, 0, axis_index_groups=gr...  30.4 us
    ppermute x5, starting transfers between devices, shift_x(): return lax.ppermute(value, AXES, pairs)  16.6 us
    ppermute x5, waiting for transfers between devices, shift_x(): return lax.ppermute(value, AXES, pairs)  12 us
    all_to_all x1, waiting for transfers between devices, spread(): lax.all_to_all(copies.reshape(n * r, c), axis, 0, 0, axis_index_groups=gr...  10.5 us
    ppermute x1, starting transfers between devices, other_core(): return lax.ppermute(value, AXES, pairs)  8.81 us
    all_to_all x1, starting transfers between devices, spread(): lax.all_to_all(copies.reshape(n * r, c), axis, 0, 0, axis_index_groups=gr...  6.63 us
    unnamed x18, local copies, waits for them, and re-layouts  6.21 us
    ppermute x1, starting transfers between devices, on_device(): halo = lax.ppermute(halo, 'dp', [(s, s + 1) for s in range(2 * NY - 1)])  4.59 us
  transfers between devices with their start and end apart: 11, of which 5 were waited for; matrix products, arithmetic and copies ran while one was open for 1% of the time, Pallas kernels for 7%

profile of v6, /device:TPU:1, one launch (start us, length us, event | category | flops | bytes accessed | tf_op | source)
XLA Modules:
  0.0 135.5 jit_solution(7458970595935256675)
XLA Ops:
  7.2 0.0 all-gather.4.cloned.1.call-start
  7.2 1.3 shard_map.113
  8.6 1.7 %copy.12 = bf16[32,8,2,256]{3,1,2,0:T(8,128)(2,1)} copy(bf16[32,8,2,256]{3,2,1,0:T(2,128)(2,1)} %bitcast.23) | data formatting | bytes 524288
  10.3 0.0 all-gather.4.cloned.1.call-update
  10.3 4.6 %collective-permute-start = (bf16[3,16,128]{2,1,0:T(8,128)(2,1)}, bf16[3,16,128]{2,1,0:T(8,128)(2,1)S(1)}, u32[]{:S(2)}, u32[]{:S(2)}) collective-permute-start(bf16[3,16,128]{2,1,0:T(8,128)(2,1)} %shard_map.113), channel_id=1, source_target_pairs={{0,32},{32,64},{64,96},{96,128},{128,160},{160,192},{192,224},{224... | collective-permute-start | bytes 36872 | tf_op jit(solution)/shard_map/ppermute | solution.py:258
  14.9 4.4 %collective-permute-done.halo_ref = bf16[3,16,128]{2,1,0:T(8,128)(2,1)S(1)} collective-permute-done((bf16[3,16,128]{2,1,0:T(8,128)(2,1)}, bf16[3,16,128]{2,1,0:T(8,128)(2,1)S(1)}, u32[]{:S(2)}, u32[]{:S(2)}) %collective-permute-start) | collective-permute-done | bytes 12320 | tf_op jit(solution)/shard_map/ppermute | solution.py:258
  19.3 0.0 copy-start.7
  19.3 0.6 copy-done.7
  19.9 2.7 %shard_map.114 = (bf16[8,272,128]{2,1,0:T(8,128)(2,1)}, bf16[288,128]{1,0:T(8,128)(2,1)}) custom-call(bf16[256,128]{1,0:T(8,128)(2,1)} %q_hbm.1, bf16[256,128]{1,0:T(8,128)(2,1)} %k_hbm.1, bf16[256,128]{1,0:T(8,128)(2,1)} %v_hbm.1, f32[3,3,128]{2,1,0:T(4,128)} %taps_hbm.1, s32[1,384]{1,0:T(1,128)} %slot_hbm.3, s32[1,2]{1,0:T(1,128)} %count_hbm.3, ...), custom_call_target="tpu_custom_call" | custom-call | tf_op jit(solution)/shard_map/pallas_call | solution.py:259
  22.7 6.6 %all-to-all-start = ((bf16[8,272,128]{2,1,0:T(8,128)(2,1)}), bf16[8,272,128]{2,1,0:T(8,128)(2,1)S(1)}, u32[]{:S(2)}, u32[]{:S(2)}) async-start(bf16[8,272,128]{2,1,0:T(8,128)(2,1)} %get-tuple-element.18), calls=%async_computation | async-start | bytes 1114112 | tf_op jit(solution)/shard_map/all_to_all | solution.py:50
  29.3 0.0 all-gather.6.cloned.1.call-start
  29.3 3.5 %collective-permute-start.1 = (bf16[288,128]{1,0:T(8,128)(2,1)}, bf16[288,128]{1,0:T(8,128)(2,1)S(1)}, u32[]{:S(2)}, u32[]{:S(2)}) collective-permute-start(bf16[288,128]{1,0:T(8,128)(2,1)} %get-tuple-element.19), channel_id=1, source_target_pairs={{0,0},{1,1},{2,32},{3,33},{4,64},{5,65},{6,96},{7,97},{8,128},{9,1... | collective-permute-start | bytes 221192 | tf_op jit(solution)/shard_map/ppermute | solution.py:45
  32.8 4.2 %collective-permute-done.1 = bf16[288,128]{1,0:T(8,128)(2,1)S(1)} collective-permute-done((bf16[288,128]{1,0:T(8,128)(2,1)}, bf16[288,128]{1,0:T(8,128)(2,1)S(1)}, u32[]{:S(2)}, u32[]{:S(2)}) %collective-permute-start.1) | collective-permute-done | bytes 73760 | tf_op jit(solution)/shard_map/ppermute | solution.py:45
  37.0 10.5 %all-to-all-done = bf16[8,272,128]{2,1,0:T(8,128)(2,1)S(1)} async-done(((bf16[8,272,128]{2,1,0:T(8,128)(2,1)}), bf16[8,272,128]{2,1,0:T(8,128)(2,1)S(1)}, u32[]{:S(2)}, u32[]{:S(2)}) %all-to-all-start) | async-done | bytes 557088 | tf_op jit(solution)/shard_map/all_to_all | solution.py:50
  47.6 0.0 copy-start.3
  47.6 0.0 copy-start.4
  47.6 0.0 copy-start.5
  47.6 0.0 copy-start.6
  47.6 3.3 %collective-permute-start.2 = (bf16[2464,128]{1,0:T(8,128)(2,1)S(1)}, bf16[2464,128]{1,0:T(8,128)(2,1)S(1)}, u32[]{:S(2)}, u32[]{:S(2)}) collective-permute-start(bf16[2464,128]{1,0:T(8,128)(2,1)S(1)} %constant_dynamic-update-slice_fusion), channel_id=1, source_target_pairs={{0,1},{1,2},{2,3},{3,0},{4,5},{5,6},{6,7},{7,4},{8,9},{9,10},{10,1... | collective-permute-start | bytes 1892360 | tf_op jit(solution)/shard_map/ppermute | solution.py:31
  50.9 3.4 %collective-permute-start.3 = (bf16[2464,128]{1,0:T(8,128)(2,1)S(1)}, bf16[2464,128]{1,0:T(8,128)(2,1)S(1)}, u32[]{:S(2)}, u32[]{:S(2)}) collective-permute-start(bf16[2464,128]{1,0:T(8,128)(2,1)S(1)} %constant_dynamic-update-slice_fusion), channel_id=1, source_target_pairs={{0,3},{1,0},{2,1},{3,2},{4,7},{5,4},{6,5},{7,6},{8,11},{9,8},{10,9... | collective-permute-start | bytes 1892360 | tf_op jit(solution)/shard_map/ppermute | solution.py:31
  54.2 3.4 %collective-permute-start.4 = (bf16[288,128]{1,0:T(8,128)(2,1)S(1)}, bf16[288,128]{1,0:T(8,128)(2,1)S(1)}, u32[]{:S(2)}, u32[]{:S(2)}) collective-permute-start(bf16[288,128]{1,0:T(8,128)(2,1)S(1)} %collective-permute-done.1), channel_id=1, source_target_pairs={{0,2},{1,3},{2,0},{3,1},{4,6},{5,7},{6,4},{7,5},{8,10},{9,11},{10,... | collective-permute-start | bytes 221192 | tf_op jit(solution)/shard_map/ppermute | solution.py:31
  57.7 11.2 %collective-permute-done.4 = bf16[288,128]{1,0:T(8,128)(2,1)S(1)} collective-permute-done((bf16[288,128]{1,0:T(8,128)(2,1)S(1)}, bf16[288,128]{1,0:T(8,128)(2,1)S(1)}, u32[]{:S(2)}, u32[]{:S(2)}) %collective-permute-start.4) | collective-permute-done | bytes 73760 | tf_op jit(solution)/shard_map/ppermute | solution.py:31
  68.9 0.0 collective-permute-done.2.left_ref
  68.9 0.0 collective-permute-done.3.right_ref
  68.9 0.8 pad_maximum_fusion
  69.7 0.0 all-gather.6.cloned.1.call-update
  69.8 4.1 %collective-permute-start.5 = (bf16[1088,128]{1,0:T(8,128)(2,1)S(1)}, bf16[1088,128]{1,0:T(8,128)(2,1)S(1)}, u32[]{:S(2)}, u32[]{:S(2)}) collective-permute-start(bf16[1088,128]{1,0:T(8,128)(2,1)S(1)} %slice.12), channel_id=1, source_target_pairs={{0,1},{1,2},{2,3},{3,0},{4,5},{5,6},{6,7},{7,4},{8,9},{9,10},{10,1... | collective-permute-start | bytes 835592 | tf_op jit(solution)/shard_map/ppermute | solution.py:31
  73.9 2.5 %collective-permute-start.6 = (bf16[1088,128]{1,0:T(8,128)(2,1)S(1)}, bf16[1088,128]{1,0:T(8,128)(2,1)S(1)}, u32[]{:S(2)}, u32[]{:S(2)}) collective-permute-start(bf16[1088,128]{1,0:T(8,128)(2,1)S(1)} %slice.13), channel_id=1, source_target_pairs={{0,3},{1,0},{2,1},{3,2},{4,7},{5,4},{6,5},{7,6},{8,11},{9,8},{10,9... | collective-permute-start | bytes 835592 | tf_op jit(solution)/shard_map/ppermute | solution.py:31
  76.3 0.1 pad_add_fusion.x_ref
  76.4 0.0 all-gather.4.cloned.1.call-done
  76.4 2.2 %copy-done = bf16[4096,512]{1,0:T(8,128)(2,1)S(1)} copy-done((bf16[4096,512]{1,0:T(8,128)(2,1)S(1)}, bf16[4096,512]{1,0:T(8,128)(2,1)}, u32[]{:S(2)}) %copy-start) | copy-done | bytes 4194328
  78.6 2.5 %shard_map.115 = (f32[256,512]{1,0:T(8,128)S(1)}, f32[256,128]{1,0:T(8,128)S(1)}) custom-call(s32[2]{0:T(128)S(1)} %pad_add_fusion.x_ref, bf16[2176,128]{1,0:T(8,128)(2,1)S(1)} %bitcast.18, bf16[2464,128]{1,0:T(8,128)(2,1)S(1)} %collective-permute-done.2.left_ref, bf16[2464,128]{1,0:T(8,128)(2,1)S(1)} %collective-permute-done.3.right_ref, ...), custom_call_target="tpu_custom_call" | custom-call | flops 800000000 | bytes 6000000 | tf_op jit(solution)/shard_map/pallas_call | solution.py:292
  81.1 0.0 collective-permute-done.5.low_ref
  81.1 0.8 collective-permute-done.6.high_ref
  81.9 0.0 copy-done.3
  81.9 0.0 copy-done.4
  81.9 0.0 copy-done.5
  81.9 0.0 copy-done.6
  81.9 0.0 copy-done.1
  81.9 2.3 %shard_map.116 = (bf16[256,256]{1,0:T(8,128)(2,1)}, bf16[8,256,256]{2,1,0:T(8,128)(2,1)S(1)}) custom-call(s32[2]{0:T(128)S(1)} %pad_add_fusion.x_ref, bf16[1088,128]{1,0:T(8,128)(2,1)S(1)} %collective-permute-done.5.low_ref, bf16[1088,128]{1,0:T(8,128)(2,1)S(1)} %collective-permute-done.6.high_ref, f32[256,512]{1,0:T(8,128)S(1)} %get-tuple-element.25.acc_ref, ...), custom_call_target="tpu_custom_call" | custom-call | tf_op jit(solution)/shard_map/pallas_call | solution.py:308
  84.2 30.4 %all_to_all.15.gm_ref = bf16[8,256,256]{2,1,0:T(8,128)(2,1)S(1)} all-to-all(bf16[8,256,256]{2,1,0:T(8,128)(2,1)S(1)} %get-tuple-element.29), channel_id=1, replica_groups={{0,64,128,192,256,320,384,448},{32,96,160,224,288,352,416,480},{1,65,12..., dimensions={0} | all-to-all | bytes 2097152 | tf_op jit(solution)/shard_map/all_to_all | solution.py:50
  114.6 8.8 %collective-permute-start.7 = (bf16[8,256,256]{2,1,0:T(8,128)(2,1)S(1)}, bf16[8,256,256]{2,1,0:T(8,128)(2,1)S(1)}, u32[]{:S(2)}, u32[]{:S(2)}) collective-permute-start(bf16[8,256,256]{2,1,0:T(8,128)(2,1)S(1)} %all_to_all.15.gm_ref), channel_id=1, source_target_pairs={{0,32},{1,33},{2,34},{3,35},{4,36},{5,37},{6,38},{7,39},{8,40},{9,... | collective-permute-start | bytes 3145736 | tf_op jit(solution)/shard_map/ppermute | solution.py:36
  123.5 0.0 all-gather.6.cloned.1.call-done
  123.5 0.0 copy-start.2
  123.5 1.7 %copy-done.2 = bf16[32,288,128]{2,1,0:T(8,128)(2,1)S(1)} copy-done((bf16[32,288,128]{2,1,0:T(8,128)(2,1)S(1)}, bf16[32,288,128]{2,1,0:T(8,128)(2,1)}, u32[]{:S(2)}) %copy-start.2) | copy-done | bytes 2359320
  125.1 1.9 %shard_map.117 = (f32[2,256,256]{2,1,0:T(8,128)S(1)}, bf16[2,2,256,2048]{3,2,1,0:T(8,128)(2,1)S(1)}) custom-call(s32[2]{0:T(128)S(1)} %pad_add_fusion.x_ref, bf16[8,4,288,128]{3,2,1,0:T(8,128)(2,1)S(1)} %bitcast.19, bf16[8,256,256]{2,1,0:T(8,128)(2,1)S(1)} %all_to_all.15.gm_ref), custom_call_target="tpu_custom_call" | custom-call | flops 500000000 | bytes 6000000 | tf_op jit(solution)/shard_map/pallas_call | solution.py:339
  127.0 0.0 collective-permute-done.7.other_ref
  127.1 1.6 %shard_map.118 = f32[256,2,256]{2,1,0:T(2,128)} custom-call(f32[2,256,256]{2,1,0:T(8,128)S(1)} %get-tuple-element.30.acc_ref, bf16[2,2,256,2048]{3,2,1,0:T(8,128)(2,1)S(1)} %get-tuple-element.31.rest_ref, bf16[8,256,256]{2,1,0:T(8,128)(2,1)S(1)} %collective-permute-done.7.other_ref), custom_call_target="tpu_custom_call" | custom-call | tf_op jit(solution)/shard_map/pallas_call | solution.py:350
  (7 shorter events, 0.1 us)
Async XLA Ops:
  7.2 69.3 %all-gather.4.cloned.1.call-start = ((), (), s32[]{:S(2)}) async-start(), calls=%async_computation.2 | async-start | bytes 4456448 | tf_op jit(solution)/shard_map/all_gather | solution.py:257
  10.3 9.0 %collective-permute-start = (bf16[3,16,128]{2,1,0:T(8,128)(2,1)}, bf16[3,16,128]{2,1,0:T(8,128)(2,1)S(1)}, u32[]{:S(2)}, u32[]{:S(2)}) collective-permute-start(bf16[3,16,128]{2,1,0:T(8,128)(2,1)} %shard_map.113), channel_id=1, source_target_pairs={{0,32},{32,64},{64,96},{96,128},{128,160},{160,192},{192,224},{224... | collective-permute-start | bytes 36872 | tf_op jit(solution)/shard_map/ppermute | solution.py:258
  19.3 0.6 copy-start.7
  22.7 24.8 %all-to-all-start = ((bf16[8,272,128]{2,1,0:T(8,128)(2,1)}), bf16[8,272,128]{2,1,0:T(8,128)(2,1)S(1)}, u32[]{:S(2)}, u32[]{:S(2)}) async-start(bf16[8,272,128]{2,1,0:T(8,128)(2,1)} %get-tuple-element.18), calls=%async_computation | async-start | bytes 1114112 | tf_op jit(solution)/shard_map/all_to_all | solution.py:50
  29.3 94.2 %all-gather.6.cloned.1.call-start = ((), (), s32[]{:S(2)}) async-start(), calls=%async_computation.3 | async-start | bytes 2654208 | tf_op jit(solution)/shard_map/all_gather | solution.py:290
  29.3 7.7 %collective-permute-start.1 = (bf16[288,128]{1,0:T(8,128)(2,1)}, bf16[288,128]{1,0:T(8,128)(2,1)S(1)}, u32[]{:S(2)}, u32[]{:S(2)}) collective-permute-start(bf16[288,128]{1,0:T(8,128)(2,1)} %get-tuple-element.19), channel_id=1, source_target_pairs={{0,0},{1,1},{2,32},{3,33},{4,64},{5,65},{6,96},{7,97},{8,128},{9,1... | collective-permute-start | bytes 221192 | tf_op jit(solution)/shard_map/ppermute | solution.py:45
  47.6 34.3 %copy-start.3 = (bf16[256,256]{1,0:T(8,128)(2,1)S(1)}, bf16[256,256]{1,0:T(8,128)(2,1)}, u32[]{:S(2)}) copy-start(bf16[256,256]{1,0:T(8,128)(2,1)} %g_hbm.1) | copy-start | bytes 393220
  47.6 34.3 %copy-start.4 = (s32[1,384]{1,0:T(1,128)S(1)}, s32[1,384]{1,0:T(1,128)}, u32[]{:S(2)}) copy-start(s32[1,384]{1,0:T(1,128)} %slot_hbm.3) | copy-start | bytes 4612
  47.6 34.3 %copy-start.5 = (s32[1,2]{1,0:T(1,128)S(1)}, s32[1,2]{1,0:T(1,128)}, u32[]{:S(2)}) copy-start(s32[1,2]{1,0:T(1,128)} %count_hbm.3) | copy-start | bytes 28
  47.6 34.3 %copy-start.6 = (f32[256]{0:T(256)S(1)}, f32[256]{0:T(256)}, u32[]{:S(2)}) copy-start(f32[256]{0:T(256)} %param.17) | copy-start | bytes 3076
  47.6 21.3 %collective-permute-start.2 = (bf16[2464,128]{1,0:T(8,128)(2,1)S(1)}, bf16[2464,128]{1,0:T(8,128)(2,1)S(1)}, u32[]{:S(2)}, u32[]{:S(2)}) collective-permute-start(bf16[2464,128]{1,0:T(8,128)(2,1)S(1)} %constant_dynamic-update-slice_fusion), channel_id=1, source_target_pairs={{0,1},{1,2},{2,3},{3,0},{4,5},{5,6},{6,7},{7,4},{8,9},{9,10},{10,1... | collective-permute-start | bytes 1892360 | tf_op jit(solution)/shard_map/ppermute | solution.py:31
  50.9 18.1 %collective-permute-start.3 = (bf16[2464,128]{1,0:T(8,128)(2,1)S(1)}, bf16[2464,128]{1,0:T(8,128)(2,1)S(1)}, u32[]{:S(2)}, u32[]{:S(2)}) collective-permute-start(bf16[2464,128]{1,0:T(8,128)(2,1)S(1)} %constant_dynamic-update-slice_fusion), channel_id=1, source_target_pairs={{0,3},{1,0},{2,1},{3,2},{4,7},{5,4},{6,5},{7,6},{8,11},{9,8},{10,9... | collective-permute-start | bytes 1892360 | tf_op jit(solution)/shard_map/ppermute | solution.py:31
  54.2 14.7 %collective-permute-start.4 = (bf16[288,128]{1,0:T(8,128)(2,1)S(1)}, bf16[288,128]{1,0:T(8,128)(2,1)S(1)}, u32[]{:S(2)}, u32[]{:S(2)}) collective-permute-start(bf16[288,128]{1,0:T(8,128)(2,1)S(1)} %collective-permute-done.1), channel_id=1, source_target_pairs={{0,2},{1,3},{2,0},{3,1},{4,6},{5,7},{6,4},{7,5},{8,10},{9,11},{10,... | collective-permute-start | bytes 221192 | tf_op jit(solution)/shard_map/ppermute | solution.py:31
  69.8 11.3 %collective-permute-start.5 = (bf16[1088,128]{1,0:T(8,128)(2,1)S(1)}, bf16[1088,128]{1,0:T(8,128)(2,1)S(1)}, u32[]{:S(2)}, u32[]{:S(2)}) collective-permute-start(bf16[1088,128]{1,0:T(8,128)(2,1)S(1)} %slice.12), channel_id=1, source_target_pairs={{0,1},{1,2},{2,3},{3,0},{4,5},{5,6},{6,7},{7,4},{8,9},{9,10},{10,1... | collective-permute-start | bytes 835592 | tf_op jit(solution)/shard_map/ppermute | solution.py:31
  73.9 8.0 %collective-permute-start.6 = (bf16[1088,128]{1,0:T(8,128)(2,1)S(1)}, bf16[1088,128]{1,0:T(8,128)(2,1)S(1)}, u32[]{:S(2)}, u32[]{:S(2)}) collective-permute-start(bf16[1088,128]{1,0:T(8,128)(2,1)S(1)} %slice.13), channel_id=1, source_target_pairs={{0,3},{1,0},{2,1},{3,2},{4,7},{5,4},{6,5},{7,6},{8,11},{9,8},{10,9... | collective-permute-start | bytes 835592 | tf_op jit(solution)/shard_map/ppermute | solution.py:31
  76.4 2.2 %copy-start = (bf16[4096,512]{1,0:T(8,128)(2,1)S(1)}, bf16[4096,512]{1,0:T(8,128)(2,1)}, u32[]{:S(2)}) copy-start(bf16[4096,512]{1,0:T(8,128)(2,1)} %all-gather.4.cloned.1.call-done) | copy-start | bytes 12582916
  78.6 3.3 %copy-start.1 = (bf16[4096,512]{1,0:T(8,128)(2,1)S(1)}, bf16[4096,512]{1,0:T(8,128)(2,1)}, u32[]{:S(2)}) copy-start(bf16[4096,512]{1,0:T(8,128)(2,1)} %all-gather.4.cloned.1.call-done) | copy-start | bytes 12582916
  114.6 12.4 %collective-permute-start.7 = (bf16[8,256,256]{2,1,0:T(8,128)(2,1)S(1)}, bf16[8,256,256]{2,1,0:T(8,128)(2,1)S(1)}, u32[]{:S(2)}, u32[]{:S(2)}) collective-permute-start(bf16[8,256,256]{2,1,0:T(8,128)(2,1)S(1)} %all_to_all.15.gm_ref), channel_id=1, source_target_pairs={{0,32},{1,33},{2,34},{3,35},{4,36},{5,37},{6,38},{7,39},{8,40},{9,... | collective-permute-start | bytes 3145736 | tf_op jit(solution)/shard_map/ppermute | solution.py:36
  123.5 1.7 %copy-start.2 = (bf16[32,288,128]{2,1,0:T(8,128)(2,1)S(1)}, bf16[32,288,128]{2,1,0:T(8,128)(2,1)}, u32[]{:S(2)}) copy-start(bf16[32,288,128]{2,1,0:T(8,128)(2,1)} %all-gather.6.cloned.1.call-done) | copy-start | bytes 7077892
Sparse Core Ops, SparseCore 0:
  10.4 55.8 all-gather.3
  69.8 44.6 all-gather.5

commit v7 on v6

--- a/solution.py
+++ b/solution.py
@@ -82,9 +82,16 @@
     return r == c
 
 
+def route_kernel(slot_ref, count_ref, out_ref):
+    second = jnp.sum(
+        jnp.where(diagonal(), in_second(slot_ref, count_ref), 0.0), axis=0, keepdims=True
+    )
+    out_ref[...] = jnp.broadcast_to(second, (16, TOK)).astype(jnp.bfloat16)
+
+
 def mix_kernel(
-    q_hbm, k_hbm, v_hbm, taps_hbm, slot_hbm, count_hbm, gain_ref, halo_ref, x1_ref, x2_ref,
-    q_ref, k_ref, v_ref, taps_ref, slot_ref, count_ref, sems,
+    q_hbm, k_hbm, v_hbm, taps_hbm, second_hbm, gain_ref, halo_ref, x1_ref, x2_ref,
+    q_ref, k_ref, v_ref, taps_ref, second_ref, sems,
 ):
     for copy in load_all(
         [
@@ -92,8 +99,7 @@
             (k_hbm, k_ref),
             (v_hbm, v_ref),
             (taps_hbm, taps_ref),
-            (slot_hbm, slot_ref),
-            (count_hbm, count_ref),
+            (second_hbm, second_ref),
         ],
         sems,
     ):
@@ -118,10 +124,7 @@
         x1_ref[n, TOK:ROWS, :] = tail
     scaled = mixed.astype(jnp.float32) * gain
     turned = scaled.T.astype(jnp.bfloat16)
-    second = jnp.sum(
-        jnp.where(diagonal(), in_second(slot_ref, count_ref), 0.0), axis=0, keepdims=True
-    )
-    second = jnp.broadcast_to(second, (16, TOK)).astype(jnp.bfloat16)
+    second = second_ref[...]
     for h in range(HALVES):
         tokens = slice(h * CH, (h + 1) * CH)
         x2_ref[h * CROWS : h * CROWS + CH, :] = turned[:, tokens]
@@ -255,6 +258,13 @@
     )(stream_q, stream_k, stream_v)
     halo, w_proj = lax.optimization_barrier((halo, w_proj))
     w_all = lax.all_gather(w_proj.reshape(TOK, 2 * HID), "dp", axis=0, tiled=True)
+    second = pl.pallas_call(
+        route_kernel,
+        out_shape=jax.ShapeDtypeStruct((16, TOK), bf),
+        in_specs=vm(2),
+        out_specs=vm(1)[0],
+        compiler_params=full,
+    )(slot_token, expert_count)
     halo = lax.ppermute(halo, "dp", [(s, s + 1) for s in range(2 * NY - 1)])
     x1, x2 = pl.pallas_call(
         mix_kernel,
@@ -262,19 +272,18 @@
             jax.ShapeDtypeStruct((NZ, ROWS, CH), bf),
             jax.ShapeDtypeStruct((HALVES * CROWS, CH), bf),
         ),
-        in_specs=hbm(6) + vm(2),
+        in_specs=hbm(5) + vm(2),
         out_specs=tuple(vm(2)),
         scratch_shapes=[
             pltpu.VMEM((TOK, CH), bf),
             pltpu.VMEM((TOK, CH), bf),
             pltpu.VMEM((TOK, CH), bf),
             pltpu.VMEM((3, 3, CH), f32),
-            pltpu.VMEM((1, 384), jnp.int32),
-            pltpu.VMEM((1, 2), jnp.int32),
-            pltpu.SemaphoreType.DMA((6,)),
+            pltpu.VMEM((16, TOK), bf),
+            pltpu.SemaphoreType.DMA((5,)),
         ],
         compiler_params=full,
-    )(stream_q, stream_k, stream_v, conv_taps, slot_token, expert_count, norm_gain.reshape(1, CH), halo)
+    )(stream_q, stream_k, stream_v, conv_taps, second, norm_gain.reshape(1, CH), halo)
     x_pos = jnp.stack([lax.rem(lax.axis_index("expert"), NX), lax.rem(lax.axis_index("dp"), 2)])
     x_pos = x_pos.astype(jnp.int32)
     x2 = to_row_block(x2)

time: 136 us -> 137 us (level)
  waiting for transfers between devices: 31.2 us -> 29.7 us
  Pallas kernels: 12.4 us -> 13.8 us
    ppermute x1, waiting for transfers between devices: 4.43 us -> 2.94 us  [on_device(): halo = lax.ppermute(halo, 'dp', [(s, s + 1) for s in range(2 * NY - 1)])]
    pallas_call x0 -> x1, Pallas kernels: none -> 1.5 us  [on_device(): pl.pallas_call(route_kernel, out_shape=jax.ShapeDtypeStruct((16, TOK), bf...]
  transfers between devices with their start and end apart: 11 -> 11, of which waited for: 5 -> 5; matrix products, arithmetic and copies ran while one was open for 1% -> 1% of each run, Pallas kernels for 7% -> 8%
where the time goes in v7:
time: 137 us
  starting transfers between devices  40.4 us (29%)
  blocking collectives  31.4 us (23%)
  waiting for transfers between devices  29.7 us (22%)
  between operations  14.3 us (10%)
  Pallas kernels  13.8 us (10%)
  local copies, waits for them, and re-layouts  6.27 us (5%)
    all_to_all x1, blocking collectives, spread(): lax.all_to_all(copies.reshape(n * r, c), axis, 0, 0, axis_index_groups=gr...  31.4 us
    ppermute x5, starting transfers between devices, shift_x(): return lax.ppermute(value, AXES, pairs)  16.6 us
    ppermute x5, waiting for transfers between devices, shift_x(): return lax.ppermute(value, AXES, pairs)  12 us
    all_to_all x1, waiting for transfers between devices, spread(): lax.all_to_all(copies.reshape(n * r, c), axis, 0, 0, axis_index_groups=gr...  10.5 us
    ppermute x1, starting transfers between devices, other_core(): return lax.ppermute(value, AXES, pairs)  8.52 us
    all_to_all x1, starting transfers between devices, spread(): lax.all_to_all(copies.reshape(n * r, c), axis, 0, 0, axis_index_groups=gr...  7.12 us
    unnamed x18, local copies, waits for them, and re-layouts  6.21 us
    ppermute x1, starting transfers between devices, on_device(): halo = lax.ppermute(halo, 'dp', [(s, s + 1) for s in range(2 * NY - 1)])  4.59 us
  transfers between devices with their start and end apart: 11, of which 5 were waited for; matrix products, arithmetic and copies ran while one was open for 1% of the time, Pallas kernels for 8%

profile of v7, /device:TPU:1, one launch (start us, length us, event | category | flops | bytes accessed | tf_op | source)
XLA Modules:
  0.0 136.6 jit_solution(17025517416761488481)
XLA Ops:
  7.2 0.0 all-gather.4.cloned.1.call-start
  7.2 1.3 shard_map.114
  8.6 1.7 %copy.12 = bf16[32,8,2,256]{3,1,2,0:T(8,128)(2,1)} copy(bf16[32,8,2,256]{3,2,1,0:T(2,128)(2,1)} %bitcast.23) | data formatting | bytes 524288
  10.3 0.0 all-gather.4.cloned.1.call-update
  10.3 4.6 %collective-permute-start = (bf16[3,16,128]{2,1,0:T(8,128)(2,1)}, bf16[3,16,128]{2,1,0:T(8,128)(2,1)S(1)}, u32[]{:S(2)}, u32[]{:S(2)}) collective-permute-start(bf16[3,16,128]{2,1,0:T(8,128)(2,1)} %shard_map.114), channel_id=1, source_target_pairs={{0,32},{32,64},{64,96},{96,128},{128,160},{160,192},{192,224},{224... | collective-permute-start | bytes 36872 | tf_op jit(solution)/shard_map/ppermute | solution.py:268
  14.9 1.5 %shard_map.113.second_hbm = bf16[16,256]{1,0:T(8,128)(2,1)} custom-call(s32[1,384]{1,0:T(1,128)} %slot_hbm.1, s32[1,2]{1,0:T(1,128)} %count_hbm.1), custom_call_target="tpu_custom_call" | custom-call | tf_op jit(solution)/shard_map/pallas_call | solution.py:261
  16.4 2.9 %collective-permute-done.halo_ref = bf16[3,16,128]{2,1,0:T(8,128)(2,1)S(1)} collective-permute-done((bf16[3,16,128]{2,1,0:T(8,128)(2,1)}, bf16[3,16,128]{2,1,0:T(8,128)(2,1)S(1)}, u32[]{:S(2)}, u32[]{:S(2)}) %collective-permute-start) | collective-permute-done | bytes 12320 | tf_op jit(solution)/shard_map/ppermute | solution.py:268
  19.3 0.0 copy-start.7
  19.3 0.6 copy-done.7
  19.9 2.7 %shard_map.115 = (bf16[8,272,128]{2,1,0:T(8,128)(2,1)}, bf16[288,128]{1,0:T(8,128)(2,1)}) custom-call(bf16[256,128]{1,0:T(8,128)(2,1)} %q_hbm.1, bf16[256,128]{1,0:T(8,128)(2,1)} %k_hbm.1, bf16[256,128]{1,0:T(8,128)(2,1)} %v_hbm.1, f32[3,3,128]{2,1,0:T(4,128)} %taps_hbm.1, bf16[16,256]{1,0:T(8,128)(2,1)} %shard_map.113.second_hbm, bf16[1,128]{1,0:T(2,128)(2,1)} %bitcast.25, ...), custom_call_target="tpu_custom_call" | custom-call | tf_op jit(solution)/shard_map/pallas_call | solution.py:269
  22.6 7.1 %all-to-all-start = ((bf16[8,272,128]{2,1,0:T(8,128)(2,1)}), bf16[8,272,128]{2,1,0:T(8,128)(2,1)S(1)}, u32[]{:S(2)}, u32[]{:S(2)}) async-start(bf16[8,272,128]{2,1,0:T(8,128)(2,1)} %get-tuple-element.18), calls=%async_computation | async-start | bytes 1114112 | tf_op jit(solution)/shard_map/all_to_all | solution.py:50
  29.7 0.0 all-gather.6.cloned.1.call-start
  29.8 3.5 %collective-permute-start.1 = (bf16[288,128]{1,0:T(8,128)(2,1)}, bf16[288,128]{1,0:T(8,128)(2,1)S(1)}, u32[]{:S(2)}, u32[]{:S(2)}) collective-permute-start(bf16[288,128]{1,0:T(8,128)(2,1)} %get-tuple-element.19), channel_id=1, source_target_pairs={{0,0},{1,1},{2,32},{3,33},{4,64},{5,65},{6,96},{7,97},{8,128},{9,1... | collective-permute-start | bytes 221192 | tf_op jit(solution)/shard_map/ppermute | solution.py:45
  33.2 4.2 %collective-permute-done.1 = bf16[288,128]{1,0:T(8,128)(2,1)S(1)} collective-permute-done((bf16[288,128]{1,0:T(8,128)(2,1)}, bf16[288,128]{1,0:T(8,128)(2,1)S(1)}, u32[]{:S(2)}, u32[]{:S(2)}) %collective-permute-start.1) | collective-permute-done | bytes 73760 | tf_op jit(solution)/shard_map/ppermute | solution.py:45
  37.4 10.5 %all-to-all-done = bf16[8,272,128]{2,1,0:T(8,128)(2,1)S(1)} async-done(((bf16[8,272,128]{2,1,0:T(8,128)(2,1)}), bf16[8,272,128]{2,1,0:T(8,128)(2,1)S(1)}, u32[]{:S(2)}, u32[]{:S(2)}) %all-to-all-start) | async-done | bytes 557088 | tf_op jit(solution)/shard_map/all_to_all | solution.py:50
  48.0 0.0 copy-start.3
  48.0 0.0 copy-start.4
  48.0 0.0 copy-start.5
  48.0 0.0 copy-start.6
  48.0 3.3 %collective-permute-start.2 = (bf16[2464,128]{1,0:T(8,128)(2,1)S(1)}, bf16[2464,128]{1,0:T(8,128)(2,1)S(1)}, u32[]{:S(2)}, u32[]{:S(2)}) collective-permute-start(bf16[2464,128]{1,0:T(8,128)(2,1)S(1)} %constant_dynamic-update-slice_fusion), channel_id=1, source_target_pairs={{0,1},{1,2},{2,3},{3,0},{4,5},{5,6},{6,7},{7,4},{8,9},{9,10},{10,1... | collective-permute-start | bytes 1892360 | tf_op jit(solution)/shard_map/ppermute | solution.py:31
  51.3 3.4 %collective-permute-start.3 = (bf16[2464,128]{1,0:T(8,128)(2,1)S(1)}, bf16[2464,128]{1,0:T(8,128)(2,1)S(1)}, u32[]{:S(2)}, u32[]{:S(2)}) collective-permute-start(bf16[2464,128]{1,0:T(8,128)(2,1)S(1)} %constant_dynamic-update-slice_fusion), channel_id=1, source_target_pairs={{0,3},{1,0},{2,1},{3,2},{4,7},{5,4},{6,5},{7,6},{8,11},{9,8},{10,9... | collective-permute-start | bytes 1892360 | tf_op jit(solution)/shard_map/ppermute | solution.py:31
  54.7 3.4 %collective-permute-start.4 = (bf16[288,128]{1,0:T(8,128)(2,1)S(1)}, bf16[288,128]{1,0:T(8,128)(2,1)S(1)}, u32[]{:S(2)}, u32[]{:S(2)}) collective-permute-start(bf16[288,128]{1,0:T(8,128)(2,1)S(1)} %collective-permute-done.1), channel_id=1, source_target_pairs={{0,2},{1,3},{2,0},{3,1},{4,6},{5,7},{6,4},{7,5},{8,10},{9,11},{10,... | collective-permute-start | bytes 221192 | tf_op jit(solution)/shard_map/ppermute | solution.py:31
  58.1 11.2 %collective-permute-done.4 = bf16[288,128]{1,0:T(8,128)(2,1)S(1)} collective-permute-done((bf16[288,128]{1,0:T(8,128)(2,1)S(1)}, bf16[288,128]{1,0:T(8,128)(2,1)S(1)}, u32[]{:S(2)}, u32[]{:S(2)}) %collective-permute-start.4) | collective-permute-done | bytes 73760 | tf_op jit(solution)/shard_map/ppermute | solution.py:31
  69.3 0.0 collective-permute-done.2.left_ref
  69.3 0.0 collective-permute-done.3.right_ref
  69.4 0.8 pad_maximum_fusion
  70.1 0.0 all-gather.6.cloned.1.call-update
  70.2 4.1 %collective-permute-start.5 = (bf16[1088,128]{1,0:T(8,128)(2,1)S(1)}, bf16[1088,128]{1,0:T(8,128)(2,1)S(1)}, u32[]{:S(2)}, u32[]{:S(2)}) collective-permute-start(bf16[1088,128]{1,0:T(8,128)(2,1)S(1)} %slice.12), channel_id=1, source_target_pairs={{0,1},{1,2},{2,3},{3,0},{4,5},{5,6},{6,7},{7,4},{8,9},{9,10},{10,1... | collective-permute-start | bytes 835592 | tf_op jit(solution)/shard_map/ppermute | solution.py:31
  74.3 2.5 %collective-permute-start.6 = (bf16[1088,128]{1,0:T(8,128)(2,1)S(1)}, bf16[1088,128]{1,0:T(8,128)(2,1)S(1)}, u32[]{:S(2)}, u32[]{:S(2)}) collective-permute-start(bf16[1088,128]{1,0:T(8,128)(2,1)S(1)} %slice.13), channel_id=1, source_target_pairs={{0,3},{1,0},{2,1},{3,2},{4,7},{5,4},{6,5},{7,6},{8,11},{9,8},{10,9... | collective-permute-start | bytes 835592 | tf_op jit(solution)/shard_map/ppermute | solution.py:31
  76.8 0.1 pad_add_fusion.x_ref
  76.8 2.2 %copy-done = bf16[4096,512]{1,0:T(8,128)(2,1)S(1)} copy-done((bf16[4096,512]{1,0:T(8,128)(2,1)S(1)}, bf16[4096,512]{1,0:T(8,128)(2,1)}, u32[]{:S(2)}) %copy-start) | copy-done | bytes 4194328
  79.0 2.5 %shard_map.116 = (f32[256,512]{1,0:T(8,128)S(1)}, f32[256,128]{1,0:T(8,128)S(1)}) custom-call(s32[2]{0:T(128)S(1)} %pad_add_fusion.x_ref, bf16[2176,128]{1,0:T(8,128)(2,1)S(1)} %bitcast.18, bf16[2464,128]{1,0:T(8,128)(2,1)S(1)} %collective-permute-done.2.left_ref, bf16[2464,128]{1,0:T(8,128)(2,1)S(1)} %collective-permute-done.3.right_ref, ...), custom_call_target="tpu_custom_call" | custom-call | flops 800000000 | bytes 6000000 | tf_op jit(solution)/shard_map/pallas_call | solution.py:301
  81.5 0.0 collective-permute-done.5.low_ref
  81.5 0.8 collective-permute-done.6.high_ref
  82.3 0.0 copy-done.3
  82.3 0.0 copy-done.4
  82.3 0.0 copy-done.5
  82.3 0.0 copy-done.6
  82.3 0.0 copy-done.1
  82.3 2.3 %shard_map.117 = (bf16[256,256]{1,0:T(8,128)(2,1)}, bf16[8,256,256]{2,1,0:T(8,128)(2,1)S(1)}) custom-call(s32[2]{0:T(128)S(1)} %pad_add_fusion.x_ref, bf16[1088,128]{1,0:T(8,128)(2,1)S(1)} %collective-permute-done.5.low_ref, bf16[1088,128]{1,0:T(8,128)(2,1)S(1)} %collective-permute-done.6.high_ref, f32[256,512]{1,0:T(8,128)S(1)} %get-tuple-element.25.acc_ref, ...), custom_call_target="tpu_custom_call" | custom-call | tf_op jit(solution)/shard_map/pallas_call | solution.py:317
  84.6 31.4 %all_to_all.15.gm_ref = bf16[8,256,256]{2,1,0:T(8,128)(2,1)S(1)} all-to-all(bf16[8,256,256]{2,1,0:T(8,128)(2,1)S(1)} %get-tuple-element.29), channel_id=1, replica_groups={{0,64,128,192,256,320,384,448},{32,96,160,224,288,352,416,480},{1,65,12..., dimensions={0} | all-to-all | bytes 2097152 | tf_op jit(solution)/shard_map/all_to_all | solution.py:50
  116.0 8.5 %collective-permute-start.7 = (bf16[8,256,256]{2,1,0:T(8,128)(2,1)S(1)}, bf16[8,256,256]{2,1,0:T(8,128)(2,1)S(1)}, u32[]{:S(2)}, u32[]{:S(2)}) collective-permute-start(bf16[8,256,256]{2,1,0:T(8,128)(2,1)S(1)} %all_to_all.15.gm_ref), channel_id=1, source_target_pairs={{0,32},{1,33},{2,34},{3,35},{4,36},{5,37},{6,38},{7,39},{8,40},{9,... | collective-permute-start | bytes 3145736 | tf_op jit(solution)/shard_map/ppermute | solution.py:36
  124.6 0.0 all-gather.6.cloned.1.call-done
  124.6 0.0 copy-start.2
  124.6 1.7 %copy-done.2 = bf16[32,288,128]{2,1,0:T(8,128)(2,1)S(1)} copy-done((bf16[32,288,128]{2,1,0:T(8,128)(2,1)S(1)}, bf16[32,288,128]{2,1,0:T(8,128)(2,1)}, u32[]{:S(2)}) %copy-start.2) | copy-done | bytes 2359320
  126.3 1.9 %shard_map.118 = (f32[2,256,256]{2,1,0:T(8,128)S(1)}, bf16[2,2,256,2048]{3,2,1,0:T(8,128)(2,1)S(1)}) custom-call(s32[2]{0:T(128)S(1)} %pad_add_fusion.x_ref, bf16[8,4,288,128]{3,2,1,0:T(8,128)(2,1)S(1)} %bitcast.19, bf16[8,256,256]{2,1,0:T(8,128)(2,1)S(1)} %all_to_all.15.gm_ref), custom_call_target="tpu_custom_call" | custom-call | flops 500000000 | bytes 6000000 | tf_op jit(solution)/shard_map/pallas_call | solution.py:348
  128.2 0.0 collective-permute-done.7.other_ref
  128.2 1.6 %shard_map.119 = f32[256,2,256]{2,1,0:T(2,128)} custom-call(f32[2,256,256]{2,1,0:T(8,128)S(1)} %get-tuple-element.30.acc_ref, bf16[2,2,256,2048]{3,2,1,0:T(8,128)(2,1)S(1)} %get-tuple-element.31.rest_ref, bf16[8,256,256]{2,1,0:T(8,128)(2,1)S(1)} %collective-permute-done.7.other_ref), custom_call_target="tpu_custom_call" | custom-call | tf_op jit(solution)/shard_map/pallas_call | solution.py:359
  (8 shorter events, 0.1 us)
Async XLA Ops:
  7.2 69.7 %all-gather.4.cloned.1.call-start = ((), (), s32[]{:S(2)}) async-start(), calls=%async_computation.2 | async-start | bytes 4456448 | tf_op jit(solution)/shard_map/all_gather | solution.py:260
  10.3 9.0 %collective-permute-start = (bf16[3,16,128]{2,1,0:T(8,128)(2,1)}, bf16[3,16,128]{2,1,0:T(8,128)(2,1)S(1)}, u32[]{:S(2)}, u32[]{:S(2)}) collective-permute-start(bf16[3,16,128]{2,1,0:T(8,128)(2,1)} %shard_map.114), channel_id=1, source_target_pairs={{0,32},{32,64},{64,96},{96,128},{128,160},{160,192},{192,224},{224... | collective-permute-start | bytes 36872 | tf_op jit(solution)/shard_map/ppermute | solution.py:268
  19.3 0.6 copy-start.7
  22.6 25.3 %all-to-all-start = ((bf16[8,272,128]{2,1,0:T(8,128)(2,1)}), bf16[8,272,128]{2,1,0:T(8,128)(2,1)S(1)}, u32[]{:S(2)}, u32[]{:S(2)}) async-start(bf16[8,272,128]{2,1,0:T(8,128)(2,1)} %get-tuple-element.18), calls=%async_computation | async-start | bytes 1114112 | tf_op jit(solution)/shard_map/all_to_all | solution.py:50
  29.7 94.9 %all-gather.6.cloned.1.call-start = ((), (), s32[]{:S(2)}) async-start(), calls=%async_computation.3 | async-start | bytes 2654208 | tf_op jit(solution)/shard_map/all_gather | solution.py:299
  29.8 7.7 %collective-permute-start.1 = (bf16[288,128]{1,0:T(8,128)(2,1)}, bf16[288,128]{1,0:T(8,128)(2,1)S(1)}, u32[]{:S(2)}, u32[]{:S(2)}) collective-permute-start(bf16[288,128]{1,0:T(8,128)(2,1)} %get-tuple-element.19), channel_id=1, source_target_pairs={{0,0},{1,1},{2,32},{3,33},{4,64},{5,65},{6,96},{7,97},{8,128},{9,1... | collective-permute-start | bytes 221192 | tf_op jit(solution)/shard_map/ppermute | solution.py:45
  48.0 34.3 %copy-start.3 = (bf16[256,256]{1,0:T(8,128)(2,1)S(1)}, bf16[256,256]{1,0:T(8,128)(2,1)}, u32[]{:S(2)}) copy-start(bf16[256,256]{1,0:T(8,128)(2,1)} %g_hbm.1) | copy-start | bytes 393220
  48.0 34.3 %copy-start.4 = (s32[1,384]{1,0:T(1,128)S(1)}, s32[1,384]{1,0:T(1,128)}, u32[]{:S(2)}) copy-start(s32[1,384]{1,0:T(1,128)} %slot_hbm.1) | copy-start | bytes 4612
  48.0 34.3 %copy-start.5 = (s32[1,2]{1,0:T(1,128)S(1)}, s32[1,2]{1,0:T(1,128)}, u32[]{:S(2)}) copy-start(s32[1,2]{1,0:T(1,128)} %count_hbm.1) | copy-start | bytes 28
  48.0 34.3 %copy-start.6 = (f32[256]{0:T(256)S(1)}, f32[256]{0:T(256)}, u32[]{:S(2)}) copy-start(f32[256]{0:T(256)} %param.17) | copy-start | bytes 3076
  48.0 21.3 %collective-permute-start.2 = (bf16[2464,128]{1,0:T(8,128)(2,1)S(1)}, bf16[2464,128]{1,0:T(8,128)(2,1)S(1)}, u32[]{:S(2)}, u32[]{:S(2)}) collective-permute-start(bf16[2464,128]{1,0:T(8,128)(2,1)S(1)} %constant_dynamic-update-slice_fusion), channel_id=1, source_target_pairs={{0,1},{1,2},{2,3},{3,0},{4,5},{5,6},{6,7},{7,4},{8,9},{9,10},{10,1... | collective-permute-start | bytes 1892360 | tf_op jit(solution)/shard_map/ppermute | solution.py:31
  51.3 18.1 %collective-permute-start.3 = (bf16[2464,128]{1,0:T(8,128)(2,1)S(1)}, bf16[2464,128]{1,0:T(8,128)(2,1)S(1)}, u32[]{:S(2)}, u32[]{:S(2)}) collective-permute-start(bf16[2464,128]{1,0:T(8,128)(2,1)S(1)} %constant_dynamic-update-slice_fusion), channel_id=1, source_target_pairs={{0,3},{1,0},{2,1},{3,2},{4,7},{5,4},{6,5},{7,6},{8,11},{9,8},{10,9... | collective-permute-start | bytes 1892360 | tf_op jit(solution)/shard_map/ppermute | solution.py:31
  54.7 14.7 %collective-permute-start.4 = (bf16[288,128]{1,0:T(8,128)(2,1)S(1)}, bf16[288,128]{1,0:T(8,128)(2,1)S(1)}, u32[]{:S(2)}, u32[]{:S(2)}) collective-permute-start(bf16[288,128]{1,0:T(8,128)(2,1)S(1)} %collective-permute-done.1), channel_id=1, source_target_pairs={{0,2},{1,3},{2,0},{3,1},{4,6},{5,7},{6,4},{7,5},{8,10},{9,11},{10,... | collective-permute-start | bytes 221192 | tf_op jit(solution)/shard_map/ppermute | solution.py:31
  70.2 11.3 %collective-permute-start.5 = (bf16[1088,128]{1,0:T(8,128)(2,1)S(1)}, bf16[1088,128]{1,0:T(8,128)(2,1)S(1)}, u32[]{:S(2)}, u32[]{:S(2)}) collective-permute-start(bf16[1088,128]{1,0:T(8,128)(2,1)S(1)} %slice.12), channel_id=1, source_target_pairs={{0,1},{1,2},{2,3},{3,0},{4,5},{5,6},{6,7},{7,4},{8,9},{9,10},{10,1... | collective-permute-start | bytes 835592 | tf_op jit(solution)/shard_map/ppermute | solution.py:31
  74.3 8.0 %collective-permute-start.6 = (bf16[1088,128]{1,0:T(8,128)(2,1)S(1)}, bf16[1088,128]{1,0:T(8,128)(2,1)S(1)}, u32[]{:S(2)}, u32[]{:S(2)}) collective-permute-start(bf16[1088,128]{1,0:T(8,128)(2,1)S(1)} %slice.13), channel_id=1, source_target_pairs={{0,3},{1,0},{2,1},{3,2},{4,7},{5,4},{6,5},{7,6},{8,11},{9,8},{10,9... | collective-permute-start | bytes 835592 | tf_op jit(solution)/shard_map/ppermute | solution.py:31
  76.8 2.2 %copy-start = (bf16[4096,512]{1,0:T(8,128)(2,1)S(1)}, bf16[4096,512]{1,0:T(8,128)(2,1)}, u32[]{:S(2)}) copy-start(bf16[4096,512]{1,0:T(8,128)(2,1)} %all-gather.4.cloned.1.call-done) | copy-start | bytes 12582916
  79.0 3.3 %copy-start.1 = (bf16[4096,512]{1,0:T(8,128)(2,1)S(1)}, bf16[4096,512]{1,0:T(8,128)(2,1)}, u32[]{:S(2)}) copy-start(bf16[4096,512]{1,0:T(8,128)(2,1)} %all-gather.4.cloned.1.call-done) | copy-start | bytes 12582916
  116.0 12.1 %collective-permute-start.7 = (bf16[8,256,256]{2,1,0:T(8,128)(2,1)S(1)}, bf16[8,256,256]{2,1,0:T(8,128)(2,1)S(1)}, u32[]{:S(2)}, u32[]{:S(2)}) collective-permute-start(bf16[8,256,256]{2,1,0:T(8,128)(2,1)S(1)} %all_to_all.15.gm_ref), channel_id=1, source_target_pairs={{0,32},{1,33},{2,34},{3,35},{4,36},{5,37},{6,38},{7,39},{8,40},{9,... | collective-permute-start | bytes 3145736 | tf_op jit(solution)/shard_map/ppermute | solution.py:36
  124.6 1.7 %copy-start.2 = (bf16[32,288,128]{2,1,0:T(8,128)(2,1)S(1)}, bf16[32,288,128]{2,1,0:T(8,128)(2,1)}, u32[]{:S(2)}) copy-start(bf16[32,288,128]{2,1,0:T(8,128)(2,1)} %all-gather.6.cloned.1.call-done) | copy-start | bytes 7077892
Sparse Core Ops, SparseCore 0:
  10.4 55.8 all-gather.3
  70.3 45.0 all-gather.5
